TPU v7x, 32 devices: a whole 2x2x4 slice. The times are simulated.
32 devices in a mesh: dp: 8 (over y, x, core), fsdp: 4 (over z).
Axes of the slice: x: 2, y: 2, z: 4, core: 2. Of those that a mesh axis runs over, the one named last changes fastest.
Arguments:
- tokens: bfloat16 [32768, 768], P(('dp', 'fsdp')), may hold values from -6 to 6
- segment_ids: int32 [32, 1024], P(('dp', 'fsdp')), may hold values from 0 to 5, never falling along the last dimension, each value on 1 to 512 neighbouring positions
- cotangent: bfloat16 [32768, 768], P(('dp', 'fsdp')), may hold values from -6 to 6
- projector: bfloat16 [768, 2304], P(('dp', 'fsdp')), may hold values from -0.21875 to 0.21875
- combiner: bfloat16 [768, 768], P(('dp', 'fsdp')), may hold values from -0.875 to 0.875
- attend_bias: bfloat16 [768], P(('dp', 'fsdp')), may hold values from -1.796875 to 1.796875
- expander: bfloat16 [768, 3072], P(('dp', 'fsdp')), may hold values from -0.21875 to 0.21875
- expand_bias: bfloat16 [3072], P(('dp', 'fsdp')), may hold values from -1.796875 to 1.796875
- reducer: bfloat16 [3072, 768], P(('dp', 'fsdp')), may hold values from -0.109375 to 0.109375
- reduce_bias: bfloat16 [768], P(('dp', 'fsdp')), may hold values from -1.796875 to 1.796875
- first_gain: bfloat16 [768], P(('dp', 'fsdp')), may hold values from 0.5 to 1.5
- first_shift: bfloat16 [768], P(('dp', 'fsdp')), may hold values from -1.796875 to 1.796875
- second_gain: bfloat16 [768], P(('dp', 'fsdp')), may hold values from 0.5 to 1.5
- second_shift: bfloat16 [768], P(('dp', 'fsdp')), may hold values from -1.796875 to 1.796875
Outputs:
- layer_output: bfloat16 [32768, 768], P(('dp', 'fsdp'))
- grad_tokens: float32 [32768, 768], P(('dp', 'fsdp'))
- grad_projector: float32 [768, 2304], P(('dp', 'fsdp'))
- grad_combiner: float32 [768, 768], P(('dp', 'fsdp'))
- grad_attend_bias: float32 [768], P(('dp', 'fsdp'))
- grad_expander: float32 [768, 3072], P(('dp', 'fsdp'))
- grad_expand_bias: float32 [3072], P(('dp', 'fsdp'))
- grad_reducer: float32 [3072, 768], P(('dp', 'fsdp'))
- grad_reduce_bias: float32 [768], P(('dp', 'fsdp'))
- grad_first_gain: float32 [768], P(('dp', 'fsdp'))
- grad_first_shift: float32 [768], P(('dp', 'fsdp'))
- grad_second_gain: float32 [768], P(('dp', 'fsdp'))
- grad_second_shift: float32 [768], P(('dp', 'fsdp'))
Inputs may be any that keep to these rules, and one draw needn't show every extreme that they name: `segment_ids`: within each window the ids never fall; an id covers 1 to 512 consecutive positions, and some id exactly that many.
All inputs are finite; a program needn't handle non-finite values.
Results may differ from a plain program's by a relative error of at most 0.0092.
Values may be sent and summed in bfloat16 or wider, within the bound.
No kernel may reach another device: no remote copies, remote signals or barrier semaphores. Data moves between devices by JAX's collectives and lax.ppermute only.
A program may use at most 192 MiB of HBM per device.

v0:
```python
import functools
import math

import jax
import jax.numpy as jnp
import numpy as np
from jax import lax
from jax.experimental import pallas as pl
from jax.experimental.pallas import tpu as pltpu
from jax.sharding import PartitionSpec as P

D = 768
HD = 32
HEADS = 24
WIN = 1024
BLOCK = 256
EPS = 1e-05
LOG2E = math.log2(math.e)
BIG = float(2**30)
VEC = 128
f32 = jnp.float32
bf16 = jnp.bfloat16
NN = (((1,), (0,)), ((), ()))
NT = (((1,), (1,)), ((), ()))
ANY = pl.BlockSpec(memory_space=pl.ANY)
SMEM = pl.BlockSpec(memory_space=pltpu.SMEM)


def room(mib):
    return pltpu.CompilerParams(vmem_limit_bytes=mib << 20)


def dot(a, b, dims=NN):
    return lax.dot_general(a, b, dims, preferred_element_type=f32)


def whole(shape):
    return pl.BlockSpec(shape, lambda *_: (0,) * len(shape), pipeline_mode=pl.Buffered(1))


def flip(value, bit, count):
    return lax.ppermute(value, "dp", [(i, i ^ bit) for i in range(count)])


def shift(value, step, count):
    return lax.ppermute(value, "fsdp", [(i, (i + step) % count) for i in range(count)])


def after(value, *others):
    return lax.optimization_barrier((value, others))[0]


def shifts(shard, nf):
    return [shard] + [shift(shard, k, nf) for k in range(1, nf)]


def line_up_kernel(nf, moves, me_ref, *refs):
    me = me_ref[0]
    parts, outs = refs[:nf], refs[nf:]
    for k in range(nf):
        for j in range(nf):
            @pl.when(lax.rem(me - k + nf, nf) == j)
            def _():
                for source, rows, out, row, col in moves:
                    value = parts[k][source : source + rows, :]
                    at = row + j * rows
                    outs[out][at : at + rows, col : col + value.shape[1]] = value


def line_up(nf, moves, shapes, parts):
    return pl.pallas_call(
        functools.partial(line_up_kernel, nf, moves),
        in_specs=[SMEM] + [whole(p.shape) for p in parts],
        out_specs=[whole(x) for x in shapes],
        out_shape=[jax.ShapeDtypeStruct(x, bf16) for x in shapes],
        grid=(1,),
        compiler_params=room(10),
        cost_estimate=pl.CostEstimate(flops=0, bytes_accessed=4 << 20, transcendentals=0),
        name="line_up",
    )(lax.axis_index("fsdp").astype(jnp.int32).reshape(1), *parts)


def add(a, b):
    return (a.astype(f32) + b.astype(f32)).astype(bf16)


def spread_plane(block, nd):
    return {m: flip(block, m, nd) if m else block for m in range(0, nd, 2)}


def spread_cores(blocks, nd):
    both = {**blocks, **{m ^ 1: flip(v, 1, nd) for m, v in blocks.items()}}
    return [both[m] for m in range(nd)]


def sum_cores(send, keep, nd):
    got = flip(send, 1, nd)
    return [add(keep[m], got[m]) for m in range(nd // 2)]


def meet_plane(totals, nd):
    return [flip(v, 2 * m, nd) if m else v for m, v in enumerate(totals)]


def scatter_z(block, rows, nf):
    me = lax.axis_index("fsdp")

    def piece(z):
        got, at = [], 0
        for r in rows:
            got.append(lax.dynamic_slice_in_dim(block, at + z * r, r, 0))
            at += nf * r
        return got[0] if len(got) == 1 else jnp.concatenate(got, axis=0)

    total = piece(me).astype(f32)
    for k in range(1, nf):
        total = total + shift(piece(lax.rem(me + k, nf)), k, nf).astype(f32)
    return total


def half_columns(q):
    o = np.arange(D // 2)
    source = (o // q) * (2 * q) + o % q
    picks = np.arange(D)[None, :, None] == (source[None, None, :] + q * np.arange(2)[:, None, None])
    return jnp.asarray(picks, bf16)


def pack_kernel(proj_ref, exp_ref, red_ref, comb_ref, pick_ref, *refs):
    vec_refs, (w_ref, f1_ref, f2_ref) = refs[:-3], refs[-3:]
    r, q = proj_ref.shape[0], red_ref.shape[0] // 2
    w_ref[:, : 3 * D] = proj_ref[...]
    row = [ref[...].astype(f32).reshape(1, -1) for ref in vec_refs]
    rows = row[:6] + [row[6][:, j * r : (j + 1) * r] for j in range(4)]
    rows.append(jnp.zeros((VEC - 10, r), f32))
    w_ref[:, 3 * D :] = jnp.concatenate(rows, axis=0).T.astype(bf16)
    for h, ref in enumerate((f1_ref, f2_ref)):
        for c in range(4):
            at, col = (c // 2) * r, (c % 2) * (D // 2)
            ref[at : at + r, col : col + D // 2] = dot(
                exp_ref[:, c * D : (c + 1) * D], pick_ref[h]
            ).astype(bf16)
        ref[2 * r : 2 * r + q, :] = red_ref[h * q : (h + 1) * q, :]
    f1_ref[2 * r + q :, :] = comb_ref[...]


def pack(projector, expander, reducer, combiner, picks, vectors):
    r, q = projector.shape[0], reducer.shape[0] // 2
    shapes = [(r, 3 * D + VEC), (3 * r + q, D), (2 * r + q, D)]
    arrays = (projector, expander, reducer, combiner, picks, *vectors)
    return pl.pallas_call(
        pack_kernel,
        grid=(1,),
        in_specs=[whole(a.shape) for a in arrays],
        out_specs=[whole(x) for x in shapes],
        out_shape=[jax.ShapeDtypeStruct(x, bf16) for x in shapes],
        compiler_params=room(58),
        cost_estimate=pl.CostEstimate(flops=0, bytes_accessed=3 << 20, transcendentals=0),
        name="pack",
    )(*arrays)


def pieces_kernel(nf, moves, me_ref, *refs):
    terms, outs = refs[:-nf], refs[-nf:]
    me = me_ref[0]
    for row, rows, at in moves:
        for j in range(nf):
            here = slice(row + j * rows, row + (j + 1) * rows)
            value = sum(t[here, :].astype(f32) for t in terms).astype(bf16)
            for k in range(nf):
                @pl.when(lax.rem(me + k, nf) == j)
                def _():
                    outs[k][at : at + rows, :] = value


def pieces(nf, moves, terms):
    rows = sum(m[1] for m in moves)
    return pl.pallas_call(
        functools.partial(pieces_kernel, nf, moves),
        in_specs=[SMEM] + [whole(x.shape) for x in terms],
        out_specs=[whole((rows, D))] * nf,
        out_shape=[jax.ShapeDtypeStruct((rows, D), bf16)] * nf,
        grid=(1,),
        compiler_params=room(12),
        cost_estimate=pl.CostEstimate(flops=0, bytes_accessed=6 << 20, transcendentals=0),
        name="pieces",
    )(lax.axis_index("fsdp").astype(jnp.int32).reshape(1), *terms)


def finish_kernel(r, q, nf, pick_ref, *refs):
    halves, (ge_ref, gr_ref, gc_ref) = (refs[:nf], refs[nf : 2 * nf]), refs[2 * nf :]
    for c in range(4):
        total = jnp.zeros((r, D), f32)
        for h in range(2):
            at, col = (c // 2) * r, (c % 2) * (D // 2)
            for p in halves[h]:
                total += dot(p[at : at + r, col : col + D // 2], pick_ref[h], NT)
        ge_ref[:, c * D : (c + 1) * D] = total
    for h in range(2):
        gr_ref[h * q : (h + 1) * q, :] = sum(p[2 * r : 2 * r + q, :].astype(f32) for p in halves[h])
    gc_ref[...] = sum(p[2 * r + q :, :].astype(f32) for p in halves[1])


def finish(r, q, picks, first, second):
    shapes = [(r, 4 * D), (2 * q, D), (r, D)]
    arrays = (picks, *first, *second)
    return pl.pallas_call(
        functools.partial(finish_kernel, r, q, len(first)),
        grid=(1,),
        in_specs=[whole(x.shape) for x in arrays],
        out_specs=[whole(x) for x in shapes],
        out_shape=[jax.ShapeDtypeStruct(x, f32) for x in shapes],
        compiler_params=room(12),
        cost_estimate=pl.CostEstimate(flops=0, bytes_accessed=3 << 20, transcendentals=0),
        name="finish",
    )(*arrays)


def load_blocks(me, refs, target, sems, base, row=0, rows=None, col=0):
    rows = rows or refs[0].shape[0]
    width = refs[0].shape[1]
    copies = []
    for m, ref in enumerate(refs):
        at = pl.multiple_of((me ^ m) * rows, 16)
        copy = pltpu.make_async_copy(
            ref.at[pl.ds(row, rows), :], target.at[pl.ds(at, rows), pl.ds(col, width)], sems.at[base + m]
        )
        copy.start()
        copies.append(copy)
    return copies


def norm_parts(v):
    c = v - jnp.mean(v, axis=-1, keepdims=True)
    rstd = lax.rsqrt(jnp.mean(c * c, axis=-1, keepdims=True) + EPS)
    return c * rstd, rstd


def norm_back(grad, gain, h, rstd):
    e = grad * gain
    return (e - jnp.mean(e, -1, keepdims=True) - h * jnp.mean(e * h, -1, keepdims=True)) * rstd


def prepare_kernel(x_ref, cot_ref, ht_ref, ct_ref):
    @pl.loop(0, WIN // BLOCK)
    def _(t):
        rows = pl.ds(pl.multiple_of(t * BLOCK, BLOCK), BLOCK)
        h, _ = norm_parts(x_ref[rows, :].astype(f32))
        ht_ref[:, rows] = h.T
        ct_ref[:, rows] = cot_ref[rows, :].T


def prepare(tokens, cotangent):
    return pl.pallas_call(
        prepare_kernel,
        grid=(1,),
        in_specs=[whole((WIN, D))] * 2,
        out_specs=[whole((D, WIN))] * 2,
        out_shape=[jax.ShapeDtypeStruct((D, WIN), f32), jax.ShapeDtypeStruct((D, WIN), bf16)],
        compiler_params=room(20),
        cost_estimate=pl.CostEstimate(flops=5_000_000_000, bytes_accessed=8 << 20, transcendentals=0),
        name="prepare",
    )(tokens, cotangent)


def project_kernel(nd, me_ref, ht_ref, turn_ref, *rest):
    w = rest[:nd]
    pt_ref, nt_ref, vec_ref, bias_ref, full, sems = rest[nd:]
    for copy in load_blocks(me_ref[0], w, full, sems, 0):
        copy.wait()
    columns = full[:, 3 * D :].astype(f32)
    vec = columns.T
    vec_ref[...] = vec[:16]
    low = vec[:16].astype(bf16)
    for i in range(4):
        c, row = i % 2, 6 + 2 * (i // 2)
        parts = [dot(low[:, c * (D // 2) : (c + 1) * (D // 2)], turn_ref[k], NT) for k in range(2)]
        bias_ref[:, i * D : (i + 1) * D] = parts[0][row : row + 1] + parts[1][row + 1 : row + 2]
    nt_ref[...] = (ht_ref[...] * columns[:, 0:1] + columns[:, 1:2]).astype(bf16)

    for c in range(0, 3 * D, BLOCK):
        cols = slice(c, c + BLOCK)
        pt_ref[cols, :] = dot(full[:, cols].T, nt_ref[...]).astype(bf16)


def project(me, normed_t, turns, w):
    nd = len(w)
    return pl.pallas_call(
        functools.partial(project_kernel, nd),
        in_specs=[SMEM, whole((D, WIN)), whole(turns.shape)] + [ANY] * nd,
        out_specs=[whole((3 * D, WIN)), whole((D, WIN)), whole((16, D)), whole((1, 4 * D))],
        out_shape=[
            jax.ShapeDtypeStruct((3 * D, WIN), bf16),
            jax.ShapeDtypeStruct((D, WIN), bf16),
            jax.ShapeDtypeStruct((16, D), f32),
            jax.ShapeDtypeStruct((1, 4 * D), f32),
        ],
        scratch_shapes=[pltpu.VMEM((D, w[0].shape[1]), bf16), pltpu.SemaphoreType.DMA((nd,))],
        grid=(1,),
        compiler_params=room(26),
        cost_estimate=pl.CostEstimate(flops=2 * WIN * D * 3 * D, bytes_accessed=12 << 20, transcendentals=0),
        name="project",
    )(me, normed_t, turns, *w)


GH = 8
SH = 8
GR = GH * HD


def causal_penalty():
    ik = lax.broadcasted_iota(jnp.int32, (BLOCK, BLOCK), 0)
    iq = lax.broadcasted_iota(jnp.int32, (BLOCK, BLOCK), 1)
    return jnp.where(iq >= ik, 0.0, -BIG)


def split_scaled(q):
    scaled = q.astype(f32) * (HD**-0.5 * LOG2E)
    high = scaled.astype(bf16)
    return high, (scaled - high.astype(f32)).astype(bf16)


def episode_rows(seg):
    hot = lax.broadcasted_iota(jnp.int32, (8, WIN), 0) == seg
    return hot.astype(f32), jnp.where(hot, 0.0, -BIG)


def attend_kernel(q_ref, k_ref, v_ref, seg_ref, out_ref, lse_ref, qa, ka, va, cm):
    @pl.when(pl.program_id(0) == 0)
    def _():
        cm[...] = causal_penalty()

    hot, pen = episode_rows(seg_ref[...])
    pad = jnp.zeros((56, WIN), f32)
    tail_q = jnp.concatenate([hot, pad], axis=0).astype(bf16)
    tail_k = jnp.concatenate([pen, pad], axis=0).astype(bf16)
    ones = jnp.ones((16, WIN), bf16)
    for h in range(GH):
        rows = slice(h * HD, (h + 1) * HD)
        high, low = split_scaled(q_ref[rows, :])
        k = k_ref[rows, :]
        qa[h] = jnp.concatenate([high, low, tail_q], axis=0)
        ka[h] = jnp.concatenate([k, k, tail_k], axis=0).T
        va[h] = jnp.concatenate([v_ref[rows, :], ones], axis=0)
    c = cm[...]
    for qb in range(WIN // BLOCK):
        k0, k1 = max(0, qb - 2) * BLOCK, (qb + 1) * BLOCK
        qs = slice(qb * BLOCK, k1)
        for hb in range(0, GH, SH):
            heads = range(hb, hb + SH)
            s = [dot(ka[h, k0:k1, :], qa[h, :, qs]) for h in heads]
            w = k1 - k0 - BLOCK
            s = [jnp.concatenate([x[:w], x[w:] + c], axis=0) if w else x + c for x in s]
            top = [jnp.max(x, axis=0, keepdims=True) for x in s]
            p = [jnp.exp2(x - y) for x, y in zip(s, top)]
            o = [dot(va[h, :, k0:k1], y.astype(bf16)) for h, y in zip(heads, p)]
            for i, h in enumerate(heads):
                total = o[i][HD : HD + 1]
                out_ref[h * HD : (h + 1) * HD, qs] = (o[i][:HD] * (1.0 / total)).astype(bf16)
                lse_ref[h, :, qs] = top[i] + jnp.log2(total)


GROUPS = HEADS // GH


def head_rows(index):
    return pl.BlockSpec((GR, WIN), lambda i: (index, 0))


def head_sums(index):
    return pl.BlockSpec((GH, 1, WIN), lambda i: (index, 0, 0))


def attend(group, project_t, seg):
    return pl.pallas_call(
        attend_kernel,
        grid=(1,),
        in_specs=[head_rows(group + j * GROUPS) for j in range(3)] + [whole((1, WIN))],
        out_specs=[head_rows(0), head_sums(0)],
        out_shape=[
            jax.ShapeDtypeStruct((GR, WIN), bf16),
            jax.ShapeDtypeStruct((GH, 1, WIN), f32),
        ],
        scratch_shapes=[
            pltpu.VMEM((GH, 128, WIN), bf16),
            pltpu.VMEM((GH, WIN, 128), bf16),
            pltpu.VMEM((GH, HD + 16, WIN), bf16),
            pltpu.VMEM((BLOCK, BLOCK), f32),
        ],
        compiler_params=room(24),
        cost_estimate=pl.CostEstimate(flops=7_000_000_000, bytes_accessed=3 << 20, transcendentals=0),
        name="attend",
    )(project_t, project_t, project_t, seg)


def attend_back_kernel(
    q_ref, k_ref, v_ref, o_ref, do_ref, lse_ref, seg_ref, dq_ref, dk_ref, dv_ref, qa, ka, va, da, aq, cm
):
    hot, pen = episode_rows(seg_ref[...])
    ids = lax.broadcasted_iota(jnp.int32, (8, WIN), 0)
    ones3 = jnp.where(ids < 3, 1.0, 0.0)
    z48 = jnp.zeros((48, WIN), f32)
    z88 = jnp.zeros((88, WIN), f32)

    def rows3(v):
        a = v.astype(bf16).astype(f32)
        b = (v - a).astype(bf16).astype(f32)
        return jnp.where(ids == 0, a, jnp.where(ids == 1, b, jnp.where(ids == 2, v - a - b, 0.0)))

    tail_k = jnp.concatenate([pen, ones3, z48], axis=0).astype(bf16)
    tail_v = jnp.concatenate([ones3, z88], axis=0).astype(bf16)
    for h in range(GH):
        rows = slice(h * HD, (h + 1) * HD)
        high, low = split_scaled(q_ref[rows, :])
        k, v, g = k_ref[rows, :], v_ref[rows, :], do_ref[rows, :]
        delta = jnp.sum(g.astype(f32) * o_ref[rows, :].astype(f32), axis=0, keepdims=True)
        tail_q = jnp.concatenate([hot, rows3(-lse_ref[h]), z48], axis=0).astype(bf16)
        tail_g = jnp.concatenate([rows3(-delta), z88], axis=0).astype(bf16)
        qa[h] = jnp.concatenate([high, low, tail_q], axis=0).T
        ka[h] = jnp.concatenate([k, k, tail_k], axis=0)
        va[h] = jnp.concatenate([v, tail_v], axis=0)
        da[h] = jnp.concatenate([g, tail_g], axis=0).T
    ik = lax.broadcasted_iota(jnp.int32, (BLOCK, BLOCK), 1)
    iq = lax.broadcasted_iota(jnp.int32, (BLOCK, BLOCK), 0)
    cm[...] = jnp.where(iq >= ik, 0.0, -BIG)
    c = cm[...]
    scale = HD**-0.5
    step = 4
    nb = WIN // BLOCK
    for kb in range(nb):
        q0, q1 = kb * BLOCK, min(nb, kb + 3) * BLOCK
        ks = slice(q0, q0 + BLOCK)
        for hb in range(0, GH, step):
            heads = range(hb, hb + step)
            rows = [slice(h * HD, (h + 1) * HD) for h in heads]
            s = [dot(qa[h, q0:q1, :], ka[h, :, ks]) for h in heads]
            dp = [dot(da[h, q0:q1, :], va[h, :, ks]) for h in heads]
            s = [
                jnp.concatenate([x[:BLOCK] + c, x[BLOCK:]], axis=0) if q1 - q0 > BLOCK else x + c
                for x in s
            ]
            p = [jnp.exp2(x) for x in s]
            ds = [(x * y).astype(bf16) for x, y in zip(p, dp)]
            pb = [x.astype(bf16) for x in p]
            dv = [dot(do_ref[x, q0:q1], y) for x, y in zip(rows, pb)]
            dk = [dot(q_ref[x, q0:q1], y) for x, y in zip(rows, ds)]
            dq = [dot(k_ref[x, ks], y, NT) for x, y in zip(rows, ds)]
            for i in range(step):
                dv_ref[rows[i], ks] = dv[i].astype(bf16)
                dk_ref[rows[i], ks] = (dk[i] * scale).astype(bf16)
                done = min(nb, kb + 2) * BLOCK if kb else 0
                if done > q0:
                    aq[rows[i], q0:done] += dq[i][:, : done - q0]
                if q1 > max(done, q0):
                    at = max(done, q0)
                    aq[rows[i], at:q1] = dq[i][:, at - q0 :]
    dq_ref[...] = (aq[...] * scale).astype(bf16)


def attend_back(group, project_t, attended_t, grad_t, lse, seg):
    return pl.pallas_call(
        attend_back_kernel,
        grid=(1,),
        in_specs=[head_rows(group + j * GROUPS) for j in range(3)]
        + [head_rows(0), head_rows(group), head_sums(0), whole((1, WIN))],
        out_specs=[head_rows(0)] * 3,
        out_shape=[jax.ShapeDtypeStruct((GR, WIN), bf16)] * 3,
        scratch_shapes=[
            pltpu.VMEM((GH, WIN, 128), bf16),
            pltpu.VMEM((GH, 128, WIN), bf16),
            pltpu.VMEM((GH, 128, WIN), bf16),
            pltpu.VMEM((GH, WIN, 128), bf16),
            pltpu.VMEM((GR, WIN), f32),
            pltpu.VMEM((BLOCK, BLOCK), f32),
        ],
        compiler_params=room(32),
        cost_estimate=pl.CostEstimate(flops=14_000_000_000, bytes_accessed=5 << 20, transcendentals=0),
        name="attend_back",
    )(project_t, project_t, project_t, attended_t, grad_t, lse, seg)


def gelu_both(u):
    a, b = math.sqrt(2 / math.pi), 0.044715
    sq = u * u
    t = jnp.tanh(u * (a + (a * b) * sq))
    half = 0.5 + 0.5 * t
    slope = half + (0.5 * u) * (1.0 - t * t) * (a + (3 * a * b) * sq)
    return u * half, slope


TB = 512


def token_loop(step):
    @pl.loop(0, WIN // TB)
    def _(t):
        step(pl.ds(pl.multiple_of(t * TB, TB), TB))


def load_weights(me, nd, blocks, exp, red, sems):
    rb, rr = D // nd, red.shape[0] // nd
    copies = load_blocks(me, blocks, exp, sems, nd, 0, rb, 0)
    copies += load_blocks(me, blocks, exp, sems, 2 * nd, rb, rb, D)
    return copies + load_blocks(me, blocks, red, sems, 3 * nd, 2 * rb, rr, 0)


def ffn_chunk(i, me, nd, cot_ref, be_ref, exp, red, n2, n2t, cott, oacc, nacc, ascr, gscr, tmp, gbe_ref, send, keep):
    rb, rr, chunk = D // nd, red.shape[0] // nd, tmp.shape[1]
    cols = pl.ds(pl.multiple_of(i * chunk, 128), chunk)
    gbe_ref[...] = jnp.zeros((1, chunk), f32)

    def step(rows):
        u = dot(n2[rows, :], exp[:, cols]) + be_ref[...]
        ga = dot(cot_ref[rows, :], red[cols, :], NT)
        act, slope = gelu_both(u)
        act = act.astype(bf16)
        gu = (ga * slope).astype(bf16)
        ascr[rows, :] = act
        gscr[rows, :] = gu
        gbe_ref[...] += jnp.sum(gu.astype(f32), axis=0, keepdims=True)
        oacc[rows, :] += dot(act, red[cols, :])
        nacc[rows, :] += dot(gu, exp[:, cols], NT)

    token_loop(step)
    tmp[...] = dot(n2t[...], gscr[...]).astype(bf16)
    emit(me, tmp, send, keep, pl.ds(pl.multiple_of(i * rb, 16), rb))
    tmp[...] = dot(cott[...], ascr[...]).astype(bf16).T
    per = chunk // rr
    for b in range(per):
        mask = me ^ (i * per + b)
        for odd, ref in ((1, send), (0, keep)):
            @pl.when((mask & 1) == odd)
            def _():
                ref[mask >> 1, 2 * rb : 2 * rb + rr, :] = tmp[b * rr : (b + 1) * rr, :]


def ffn_first_kernel(nd, me_ref, x_ref, cot_ref, cott, vec_ref, be_ref, *rest):
    att, blocks, rest = rest[:GROUPS], rest[GROUPS : GROUPS + nd], rest[GROUPS + nd :]
    mid_ref, n2_ref, part_ref, nacc_ref, send, keep, gbe_ref = rest[:7]
    comb, exp, red, mid, n2, n2t, oacc, nacc, ascr, gscr, tmp, sems = rest[7:]
    i = pl.program_id(0)
    me = me_ref[0]
    rb, rr = D // nd, red.shape[0] // nd
    outs = [
        pltpu.make_async_copy(a, b, sems.at[4 * nd + j])
        for j, (a, b) in enumerate(((mid, mid_ref), (n2, n2_ref), (oacc, part_ref), (nacc, nacc_ref)))
    ]

    @pl.when(i == 0)
    def _():
        got = load_blocks(me, blocks, comb, sems, 0, 2 * rb + rr, rb, 0)
        late = load_weights(me, nd, blocks, exp, red, sems)
        for copy in got:
            copy.wait()

        def step(rows):
            m = x_ref[rows, :].astype(f32) + vec_ref[2:3, :]
            for g in range(GROUPS):
                m += dot(att[g][:, rows].T, comb[g * GR : (g + 1) * GR, :])
            mid[rows, :] = m
            oacc[rows, :] = m + vec_ref[5:6, :]
            h, _ = norm_parts(m)
            n = (h * vec_ref[3:4, :] + vec_ref[4:5, :]).astype(bf16)
            n2[rows, :] = n
            n2t[:, rows] = n.T

        token_loop(step)
        nacc[...] = jnp.zeros_like(nacc)
        outs[0].start()
        outs[1].start()
        for copy in late:
            copy.wait()

    ffn_chunk(i, me, nd, cot_ref, be_ref, exp, red, n2, n2t, cott, oacc, nacc, ascr, gscr, tmp, gbe_ref, send, keep)

    @pl.when(i == pl.num_programs(0) - 1)
    def _():
        outs[2].start()
        outs[3].start()
        for copy in outs:
            copy.wait()


def ffn_last_kernel(nd, me_ref, cot_ref, cott, vec_ref, be_ref, *rest):
    att, blocks, rest = rest[:GROUPS], rest[GROUPS : GROUPS + nd], rest[GROUPS + nd :]
    others, rest = rest[:nd], rest[nd:]
    mid_ref, n2_ref, part_ref, naccin_ref = rest[:4]
    out_ref, gm_ref, dt_ref, send, keep, gbe_ref, gv_ref = rest[4:11]
    comb, exp, red, mid, part, nin, n2, n2t, oacc, nacc, ascr, gscr, tmp, sems = rest[11:]
    i = pl.program_id(0)
    me = me_ref[0]
    rb, rr = D // nd, red.shape[0] // nd
    ins = [
        pltpu.make_async_copy(a, b, sems.at[4 * nd + j])
        for j, (a, b) in enumerate(((n2_ref, n2), (mid_ref, mid), (part_ref, part), (naccin_ref, nin)))
    ]

    @pl.when(i == 0)
    def _():
        ins[0].start()
        got = load_weights(me, nd, blocks, exp, red, sems)
        got += load_blocks(me, others, comb, sems, 0, 2 * rb + rr, rb, 0)
        for copy in ins[1:]:
            copy.start()
        oacc[...] = jnp.zeros_like(oacc)
        nacc[...] = jnp.zeros_like(nacc)
        ins[0].wait()
        n2t[...] = n2[...].T
        for copy in got:
            copy.wait()

    ffn_chunk(i, me, nd, cot_ref, be_ref, exp, red, n2, n2t, cott, oacc, nacc, ascr, gscr, tmp, gbe_ref, send, keep)

    @pl.when(i == pl.num_programs(0) - 1)
    def _():
        for copy in ins[1:]:
            copy.wait()
        gv_ref[...] = jnp.zeros((8, D), f32)

        def step(rows):
            out_ref[rows, :] = (part[rows, :] + oacc[rows, :]).astype(bf16)
            h, rstd = norm_parts(mid[rows, :])
            g = nacc[rows, :] + nin[rows, :]
            cot = cot_ref[rows, :].astype(f32)
            gm = cot + norm_back(g, vec_ref[3:4, :], h, rstd)
            gm_ref[rows, :] = gm
            low = gm.astype(bf16)
            n2[rows, :] = low
            n2t[:, rows] = low.T
            sums = (low.astype(f32), g * h, g, cot)
            gv_ref[2:6, :] += jnp.concatenate([jnp.sum(v, axis=0, keepdims=True) for v in sums], axis=0)

        token_loop(step)
        dt_ref[...] = dot(comb[...], n2t[...]).astype(bf16)
        for g in range(GROUPS):
            tmp[g * GR : (g + 1) * GR, :] = dot(att[g][...], n2[...]).astype(bf16)
        emit(me, tmp, send, keep, slice(2 * rb + rr, 3 * rb + rr))


def ffn_call(kernel, specs, arrays, nd, rows, out_shapes, last):
    ff = 2 * D
    shape = jax.ShapeDtypeStruct
    half = (nd // 2, rows, D)
    wide = pltpu.VMEM((WIN, D), f32)
    low, turned = pltpu.VMEM((WIN, D), bf16), pltpu.VMEM((D, WIN), bf16)
    return pl.pallas_call(
        functools.partial(kernel, nd),
        grid=(ff // D,),
        in_specs=specs,
        out_specs=[whole(x.shape) if last else ANY for x in out_shapes]
        + [whole(half), whole(half), pl.BlockSpec((1, D), lambda i: (0, i))]
        + ([whole((8, D))] if last else []),
        out_shape=list(out_shapes)
        + [shape(half, bf16), shape(half, bf16), shape((1, ff), f32)]
        + ([shape((8, D), f32)] if last else []),
        scratch_shapes=[pltpu.VMEM((D, D), bf16), pltpu.VMEM((D, ff), bf16), pltpu.VMEM((ff, D), bf16)]
        + [wide] * (3 if last else 1)
        + [low, turned, wide, wide, low, low, pltpu.VMEM((D, D), bf16)]
        + [pltpu.SemaphoreType.DMA((4 * nd + 4,))],
        compiler_params=room(52 if last else 36),
        cost_estimate=pl.CostEstimate(flops=12 * WIN * D * ff, bytes_accessed=20 << 20, transcendentals=0),
        name="ffn_last" if last else "ffn_first",
    )(*arrays)


def ffn_first(me, tokens, attended, cotangent, cotangent_t, vec, bias, blocks, nd):
    shape = jax.ShapeDtypeStruct
    outs = [shape((WIN, D), f32), shape((WIN, D), bf16), shape((WIN, D), f32), shape((WIN, D), f32)]
    specs = [SMEM, whole((WIN, D)), whole((WIN, D)), whole((D, WIN)), whole((16, D))]
    specs += [pl.BlockSpec((1, D), lambda i: (0, i))]
    specs += [whole((GR, WIN))] * GROUPS + [ANY] * nd
    arrays = (me, tokens, cotangent, cotangent_t, vec, bias, *attended, *blocks)
    return ffn_call(ffn_first_kernel, specs, arrays, nd, (4 * D) // nd, outs, False)


def ffn_last(me, attended, cotangent, cotangent_t, vec, bias, blocks, others, state, nd):
    shape = jax.ShapeDtypeStruct
    outs = [shape((WIN, D), bf16), shape((WIN, D), f32), shape((D, WIN), bf16)]
    specs = [SMEM, whole((WIN, D)), whole((D, WIN)), whole((16, D)), pl.BlockSpec((1, D), lambda i: (0, i + 2))]
    specs += [whole((GR, WIN))] * GROUPS + [ANY] * (2 * nd + 4)
    arrays = (me, cotangent, cotangent_t, vec, bias, *attended, *blocks, *others, *state)
    return ffn_call(ffn_last_kernel, specs, arrays, nd, (5 * D) // nd, outs, True)


def emit(me, source, send, keep, rows=slice(None), cols=slice(None)):
    steps = send.shape[0]
    rb = source.shape[0] // (2 * steps)
    for s in range(steps):
        far = pl.multiple_of((me ^ (2 * s + 1)) * rb, 16)
        near = pl.multiple_of((me ^ (2 * s)) * rb, 16)
        send[s, rows, cols] = source[pl.ds(far, rb), :]
        keep[s, rows, cols] = source[pl.ds(near, rb), :]


def weight_grad_kernel(nd, me_ref, nt_ref, vec_ref, gv_ref, b1_ref, b2_ref, turn_ref, *rest):
    grads, rest = rest[: 3 * GROUPS], rest[3 * GROUPS :]
    send, keep, full, tmp, gvt, acc, sems = rest[nd:]
    me = me_ref[0]
    copies = load_blocks(me, rest[:nd], full, sems, 0)
    acc[...] = jnp.zeros_like(acc)
    for i, ref in enumerate(grads):
        g = ref[...].T
        gw = dot(nt_ref[...], g)
        tmp[...] = gw.astype(bf16)
        emit(me, tmp, send, keep, cols=slice(i * GR, (i + 1) * GR))
        if i == 0:
            for copy in copies:
                copy.wait()
        w = full[:, i * GR : (i + 1) * GR].astype(f32)
        total = jnp.sum(g.astype(f32), axis=0, keepdims=True)
        for j, value in enumerate((w * gw, w * total)):
            acc[j] += value[:, :128] + value[:, 128:]
    rows = [gv_ref[:6, :]]
    for ref in (b1_ref, b2_ref):
        low = ref[...].astype(bf16)
        for k in range(2):
            rows.append(
                jnp.concatenate([dot(low[:, c * D : (c + 1) * D], turn_ref[k]) for c in range(2)], axis=1)
            )
    rows += [jnp.zeros((6, D), f32), vec_ref[:2, :], jnp.zeros((VEC - 18, D), f32)]
    base = jnp.concatenate(rows, axis=0).T
    gshift = jnp.sum(acc[1], axis=1, keepdims=True)
    ggain = (jnp.sum(acc[0], axis=1, keepdims=True) - base[:, 17:18] * gshift) / base[:, 16:17]
    lane = lax.broadcasted_iota(jnp.int32, (D, VEC), 1)
    gvt[...] = jnp.where(lane == 0, ggain, jnp.where(lane == 1, gshift, base)).astype(bf16)
    emit(me, gvt, send, keep, cols=slice(3 * D, 3 * D + VEC))


def weight_grad(me, nd, normed_t, vec, gvec, sums, turns, grads, w):
    half = (nd // 2, D // nd, 3 * D + VEC)
    return pl.pallas_call(
        functools.partial(weight_grad_kernel, nd),
        grid=(1,),
        in_specs=[SMEM, whole((D, WIN)), whole((16, D)), whole((8, D))]
        + [whole((1, 2 * D))] * 2
        + [whole(turns.shape)]
        + [whole((GR, WIN))] * (3 * GROUPS)
        + [ANY] * nd,
        out_specs=[whole(half)] * 2,
        out_shape=[jax.ShapeDtypeStruct(half, bf16)] * 2,
        scratch_shapes=[
            pltpu.VMEM((D, 3 * D + VEC), bf16),
            pltpu.VMEM((D, GR), bf16),
            pltpu.VMEM((D, VEC), bf16),
            pltpu.VMEM((2, D, 128), f32),
            pltpu.SemaphoreType.DMA((nd,)),
        ],
        compiler_params=room(30),
        cost_estimate=pl.CostEstimate(flops=2 * WIN * D * 3 * D, bytes_accessed=10 << 20, transcendentals=0),
        name="weight_grad",
    )(me, normed_t, vec, gvec, *sums, turns, *grads, *w)


def project_back_kernel(nd, me_ref, x_ref, gm_ref, vec_ref, *rest):
    grads, rest = rest[: 3 * GROUPS], rest[3 * GROUPS :]
    gt_ref, full, sems = rest[nd:]
    for copy in load_blocks(me_ref[0], rest[:nd], full, sems, 0):
        copy.wait()

    @pl.loop(0, WIN // BLOCK)
    def _(t):
        rows = pl.ds(pl.multiple_of(t * BLOCK, BLOCK), BLOCK)
        total = dot(full[:, :GR], grads[0][:, rows])
        for i in range(1, 3 * GROUPS):
            total += dot(full[:, i * GR : (i + 1) * GR], grads[i][:, rows])
        h, rstd = norm_parts(x_ref[rows, :].astype(f32))
        gt_ref[rows, :] = gm_ref[rows, :] + norm_back(total.T, vec_ref[0:1, :], h, rstd)


def project_back(me, tokens, grad_middle, vec, grads, w):
    nd = len(w)
    return pl.pallas_call(
        functools.partial(project_back_kernel, nd),
        grid=(1,),
        in_specs=[SMEM, whole((WIN, D)), whole((WIN, D)), whole((16, D))]
        + [whole((GR, WIN))] * (3 * GROUPS)
        + [ANY] * nd,
        out_specs=whole((WIN, D)),
        out_shape=jax.ShapeDtypeStruct((WIN, D), f32),
        scratch_shapes=[pltpu.VMEM((D, w[0].shape[1]), bf16), pltpu.SemaphoreType.DMA((nd,))],
        compiler_params=room(58),
        cost_estimate=pl.CostEstimate(flops=2 * WIN * D * 3 * D, bytes_accessed=20 << 20, transcendentals=0),
        name="project_back",
    )(me, tokens, grad_middle, vec, *grads, *w)


def body(nd, nf, tokens, segment_ids, cotangent, projector, combiner, attend_bias, expander,
         expand_bias, reducer, reduce_bias, first_gain, first_shift, second_gain, second_shift):
    r, q = projector.shape[0], reducer.shape[0] // 2
    count = nd * nf
    me = lax.axis_index("dp").astype(jnp.int32).reshape(1)
    picks = half_columns(q)
    turns = half_columns(r)
    vectors = (first_gain, first_shift, attend_bias, second_gain, second_shift, reduce_bias, expand_bias)
    tie = lax.optimization_barrier

    shard_w, shard_1, shard_2 = pack(projector, expander, reducer, combiner, picks, vectors)
    parts_w, parts_1 = shifts(shard_w, nf), shifts(shard_1, nf)
    scaled_t, cotangent_t = prepare(after(tokens, shard_w), cotangent)
    parts_w, scaled_t, cotangent_t = tie((parts_w, scaled_t, cotangent_t))
    (zw,) = line_up(nf, [(0, r, 0, 0, 0)], [(nf * r, 3 * D + VEC)], parts_w)
    w = spread_plane(zw, nd)
    moves = [(0, r, 0, 0, 0), (r, r, 0, nf * r, 0), (2 * r, q, 0, 2 * nf * r, 0)]
    extra = [(2 * r + q, r, 0, nf * (2 * r + q), 0)]
    (z1,) = line_up(nf, moves + extra, [(nf * (3 * r + q), D)], after(parts_1, zw))
    w, z1 = tie((w, z1))
    w = spread_cores(w, nd)
    scaled_t, z1 = tie((scaled_t, z1))
    f1 = spread_plane(z1, nd)
    project_t, normed_t, vecs, bias = project(me, scaled_t, turns, w)
    parts_2 = shifts(after(shard_2, project_t), nf)
    attended, sums = [], []
    for g in range(GROUPS):
        if g == GROUPS - 1:
            f1, parts_2, project_t, _ = tie((f1, parts_2, project_t, attended))
            (z2,) = line_up(nf, moves, [(nf * (2 * r + q), D)], parts_2)
            z2, project_t = tie((z2, project_t))
            f2 = spread_plane(z2, nd)
            f1 = spread_cores(f1, nd)
        a, l = attend(g, project_t, segment_ids)
        attended.append(a)
        sums.append(l)
    *state, s1, k1, gbe1 = ffn_first(me, tokens, attended, cotangent, cotangent_t, vecs, bias, f1, nd)
    s1, k1, f2 = tie((s1, k1, f2))
    got, f2 = tie((flip(s1, 1, nd), f2))
    f2 = spread_cores(f2, nd)
    t1 = [add(k1[m], got[m]) for m in range(nd // 2)]
    t1, cotangent = tie((t1, cotangent))
    m1 = meet_plane(t1, nd)
    out, grad_middle, grad_t, s2, k2, gbe2, gvec = ffn_last(
        me, attended, cotangent, cotangent_t, vecs, bias, f2, f1, state, nd
    )

    cuts = [(0, r, 0), (nf * r, r, r), (2 * nf * r, q, 2 * r)]
    more = [(nf * (2 * r + q), r, 2 * r + q)]
    m1, s2, k2, grad_t = tie((m1, s2, k2, grad_t))
    p1 = pieces(nf, cuts, m1)
    p1, grad_t = tie((p1, grad_t))
    got = flip(s2, 1, nd)
    p1 = [shift(p, k, nf) if k else p for k, p in enumerate(p1)]
    grads = [attend_back(0, project_t, attended[0], grad_t, sums[0], segment_ids)]
    got, k2, grads, grad_t, p1 = tie((got, k2, grads, grad_t, p1))
    t2 = [add(k2[m], got[m]) for m in range(nd // 2)]
    t2, grad_t = tie((t2, grad_t))
    m2 = meet_plane(t2, nd)
    for g in range(1, GROUPS):
        grads.append(attend_back(g, project_t, attended[g], grad_t, sums[g], segment_ids))
    m2, p1, grads = tie((m2, p1, grads))
    p2 = pieces(nf, cuts + more, m2)
    p2, grads = tie((p2, grads))
    p2 = [shift(p, k, nf) if k else p for k, p in enumerate(p2)]
    grads = [grads[g][j] for j in range(3) for g in range(GROUPS)]
    send, keep = weight_grad(me, nd, normed_t, vecs, gvec, (gbe1, gbe2), turns, grads, w)
    totals = sum_cores(send, keep, nd)
    grads, totals = tie((grads, totals))
    met = meet_plane(totals, nd)
    grad_tokens = project_back(me, tokens, grad_middle, vecs, grads, w)
    grad_tokens, met, p2 = tie((grad_tokens, met, p2))
    gw = sum(v.astype(f32) for v in met).astype(bf16)
    grad_expander, grad_reducer, grad_combiner = finish(r, q, picks, p1, p2)
    last = scatter_z(gw, [r], nf)
    grad_projector, small = last[:, : 3 * D], last[:, 3 * D :]
    return (
        out,
        grad_tokens,
        grad_projector,
        grad_combiner,
        small[:, 2],
        grad_expander,
        small[:, 6:10].T.reshape(-1),
        grad_reducer,
        small[:, 5],
        small[:, 0],
        small[:, 1],
        small[:, 3],
        small[:, 4],
    )


def solution(mesh):
    rows, flat = P(("dp", "fsdp"), None), P(("dp", "fsdp"))
    return jax.shard_map(
        functools.partial(body, mesh.shape["dp"], mesh.shape["fsdp"]),
        mesh=mesh,
        in_specs=(rows, rows, rows, rows, rows, flat, rows, flat, rows, flat, flat, flat, flat, flat),
        out_specs=(rows, rows, rows, rows, flat, rows, flat, rows, flat, flat, flat, flat, flat),
        check_vma=False,
    )
```

profile of v0, /device:TPU:0, one launch (start us, length us, event | category | flops | bytes accessed | tf_op | source)
XLA Modules:
  0.0 283.4 jit_solution(17958975708409798748)
XLA Ops:
  0.7 3.1 %pack.1 = (bf16[24,2432]{1,0:T(8,128)(2,1)}, bf16[120,768]{1,0:T(8,128)(2,1)}, bf16[96,768]{1,0:T(8,128)(2,1)}) custom-call(bf16[24,2304]{1,0:T(8,128)(2,1)} %proj_ref.1, bf16[24,3072]{1,0:T(8,128)(2,1)} %exp_ref.1, bf16[96,768]{1,0:T(8,128)(2,1)} %red_ref.1, bf16[24,768]{1,0:T(8,128)(2,1)} %comb_ref.1, bf16[2,768,384]{2,1,0:T(8,128)(2,1)} %constant.32.clone.pick_ref, ...), custom_call_target="tpu_custom_call" | custom-call | bytes 3145728 | tf_op jit(solution)/shard_map/pack/pallas_call | solution.py:150
  3.7 3.1 %collective-permute-start = (bf16[24,2432]{1,0:T(8,128)(2,1)}, bf16[24,2432]{1,0:T(8,128)(2,1)S(1)}, u32[]{:S(2)}, u32[]{:S(2)}) collective-permute-start(bf16[24,2432]{1,0:T(8,128)(2,1)} %get-tuple-element.195.refs_0_), channel_id=1, source_target_pairs={{0,1},{1,2},{2,3},{3,0},{4,5},{5,6},{6,7},{7,4},{8,9},{9,10},{10,1... | collective-permute-start | bytes 350216 | tf_op jit(solution)/shard_map/ppermute | solution.py:46
  6.8 2.6 collective-permute-start.1
  9.4 1.3 collective-permute-start.2
  10.7 1.4 copy-done.29
  12.2 2.4 prepare.1
  14.6 1.7 copy-done.49
  16.2 1.1 copy-done.51
  17.5 1.6 collective-permute-start.3
  19.1 1.5 collective-permute-start.4
  21.1 2.9 %collective-permute-start.6 = (bf16[120,768]{1,0:T(8,128)(2,1)S(1)}, bf16[120,768]{1,0:T(8,128)(2,1)S(1)}, u32[]{:S(2)}, u32[]{:S(2)}) collective-permute-start(bf16[120,768]{1,0:T(8,128)(2,1)S(1)} %copy-done.17), channel_id=1, source_target_pairs={{0,1},{1,2},{2,3},{3,0},{4,5},{5,6},{6,7},{7,4},{8,9},{9,10},{10,1... | collective-permute-start | bytes 552968 | tf_op jit(solution)/shard_map/ppermute | solution.py:46
  24.0 1.6 collective-permute-start.7
  25.6 5.1 %collective-permute-done.6.refs_1_ = bf16[120,768]{1,0:T(8,128)(2,1)S(1)} collective-permute-done((bf16[120,768]{1,0:T(8,128)(2,1)S(1)}, bf16[120,768]{1,0:T(8,128)(2,1)S(1)}, u32[]{:S(2)}, u32[]{:S(2)}) %collective-permute-start.6) | collective-permute-done | bytes 184352 | tf_op jit(solution)/shard_map/ppermute | solution.py:46
  31.5 5.0 %collective-permute-done.7.refs_2_ = bf16[120,768]{1,0:T(8,128)(2,1)S(1)} collective-permute-done((bf16[120,768]{1,0:T(8,128)(2,1)S(1)}, bf16[120,768]{1,0:T(8,128)(2,1)S(1)}, u32[]{:S(2)}, u32[]{:S(2)}) %collective-permute-start.7) | collective-permute-done | bytes 184352 | tf_op jit(solution)/shard_map/ppermute | solution.py:46
  36.4 1.8 collective-permute-done.8.refs_3_
  38.3 3.1 %collective-permute-done.4.rest_4_.rest_13_ = bf16[96,2432]{1,0:T(8,128)(2,1)} collective-permute-done((bf16[96,2432]{1,0:T(8,128)(2,1)S(1)}, bf16[96,2432]{1,0:T(8,128)(2,1)}, u32[]{:S(2)}, u32[]{:S(2)}) %collective-permute-start.4) | collective-permute-done | bytes 466976 | tf_op jit(solution)/shard_map/ppermute | solution.py:42
  42.4 1.2 collective-permute-start.13
  44.0 1.5 collective-permute-start.14
  45.5 1.2 collective-permute-start.15
  46.7 1.3 copy-done.43
  48.0 1.9 copy-done.50
  49.9 7.5 %project.1 = (bf16[2304,1024]{1,0:T(8,128)(2,1)S(1)}, bf16[768,1024]{1,0:T(8,128)(2,1)S(1)}, f32[16,768]{1,0:T(8,128)S(1)}, f32[1,3072]{1,0:T(1,128)S(1)}) custom-call(s32[1]{0:T(128)} %bitcast.me_ref, f32[768,1024]{1,0:T(8,128)S(1)} %copy-done.50, bf16[2,768,384]{2,1,0:T(8,128)(2,1)S(1)} %copy-done.43, bf16[96,2432]{1,0:T(8,128)(2,1)S(1)} %line_up.3.rest_0_.rest_9_, ...), custom_call_target="tpu_custom_call" | custom-call | flops 3623878656 | bytes 12582912 | tf_op jit(solution)/shard_map/project/pallas_call | solution.py:287
  57.4 3.5 %collective-permute-start.16 = (bf16[96,768]{1,0:T(8,128)(2,1)S(1)}, bf16[96,768]{1,0:T(8,128)(2,1)S(1)}, u32[]{:S(2)}, u32[]{:S(2)}) collective-permute-start(bf16[96,768]{1,0:T(8,128)(2,1)S(1)} %copy-done.26), channel_id=1, source_target_pairs={{0,1},{1,2},{2,3},{3,0},{4,5},{5,6},{6,7},{7,4},{8,9},{9,10},{10,1... | collective-permute-start | bytes 442376 | tf_op jit(solution)/shard_map/ppermute | solution.py:46
  60.9 1.0 collective-permute-start.17
  61.9 6.1 %attend.3 = (bf16[256,1024]{1,0:T(8,128)(2,1)S(1)}, f32[8,1,1024]{2,1,0:T(1,128)S(1)}) custom-call(bf16[2304,1024]{1,0:T(8,128)(2,1)S(1)} %get-tuple-element.223.q_ref.k_ref.v_ref, bf16[2304,1024]{1,0:T(8,128)(2,1)S(1)} %get-tuple-element.223.q_ref.k_ref.v_ref, bf16[2304,1024]{1,0:T(8,128)(2,1)S(1)} %get-tuple-element.223.q_ref.k_ref.v_ref, ...), custom_call_target="tpu_custom_call" | custom-call | flops 7000000000 | bytes 3145728 | tf_op jit(solution)/shard_map/attend/pallas_call | solution.py:374
  68.0 2.9 %collective-permute-start.18 = (bf16[96,768]{1,0:T(8,128)(2,1)S(1)}, bf16[96,768]{1,0:T(8,128)(2,1)S(1)}, u32[]{:S(2)}, u32[]{:S(2)}) collective-permute-start(bf16[96,768]{1,0:T(8,128)(2,1)S(1)} %copy-done.26), channel_id=1, source_target_pairs={{0,3},{1,0},{2,1},{3,2},{4,7},{5,4},{6,5},{7,6},{8,11},{9,8},{10,9... | collective-permute-start | bytes 442376 | tf_op jit(solution)/shard_map/ppermute | solution.py:46
  70.9 6.1 %attend.4 = (bf16[256,1024]{1,0:T(8,128)(2,1)S(1)}, f32[8,1,1024]{2,1,0:T(1,128)S(1)}) custom-call(bf16[2304,1024]{1,0:T(8,128)(2,1)S(1)} %get-tuple-element.223.q_ref.k_ref.v_ref, bf16[2304,1024]{1,0:T(8,128)(2,1)S(1)} %get-tuple-element.223.q_ref.k_ref.v_ref, bf16[2304,1024]{1,0:T(8,128)(2,1)S(1)} %get-tuple-element.223.q_ref.k_ref.v_ref, ...), custom_call_target="tpu_custom_call" | custom-call | flops 7000000000 | bytes 3145728 | tf_op jit(solution)/shard_map/attend/pallas_call | solution.py:374
  77.0 1.3 collective-permute-done.14.rest_7_.rest_15_
  79.4 10.1 %line_up.5.rest_3_ = bf16[384,768]{1,0:T(8,128)(2,1)S(1)} custom-call(s32[1]{0:T(128)} %bitcast.1.me_ref, bf16[96,768]{1,0:T(8,128)(2,1)S(1)} %copy-done.26, bf16[96,768]{1,0:T(8,128)(2,1)S(1)} %collective-permute-done.16.refs_1_, bf16[96,768]{1,0:T(8,128)(2,1)S(1)} %collective-permute-done.17.refs_2_, bf16[96,768]{1,0:T(8,128)(2,1)S(1)} %collective-permute-done.18.refs_3_), custom_call_target="tpu_custom_call" | custom-call | bytes 4194304 | tf_op jit(solution)/shard_map/line_up/pallas_call | solution.py:71
  89.5 1.3 collective-permute-start.23
  90.8 6.1 %attend.5 = (bf16[256,1024]{1,0:T(8,128)(2,1)S(1)}, f32[8,1,1024]{2,1,0:T(1,128)S(1)}) custom-call(bf16[2304,1024]{1,0:T(8,128)(2,1)S(1)} %get-tuple-element.223.q_ref.k_ref.v_ref, bf16[2304,1024]{1,0:T(8,128)(2,1)S(1)} %get-tuple-element.223.q_ref.k_ref.v_ref, bf16[2304,1024]{1,0:T(8,128)(2,1)S(1)} %get-tuple-element.223.q_ref.k_ref.v_ref, ...), custom_call_target="tpu_custom_call" | custom-call | flops 7000000000 | bytes 3145728 | tf_op jit(solution)/shard_map/attend/pallas_call | solution.py:374
  97.8 1.4 collective-permute-start.25
  99.3 25.3 %ffn_first.1 = (f32[1024,768]{1,0:T(8,128)}, bf16[1024,768]{1,0:T(8,128)(2,1)S(1)}, f32[1024,768]{1,0:T(8,128)}, f32[1024,768]{1,0:T(8,128)}, bf16[4,384,768]{2,...) custom-call(s32[1]{0:T(128)} %bitcast.me_ref, bf16[1024,768]{1,0:T(8,128)(2,1)S(1)} %copy-done.2, ...), custom_call_target="tpu_custom_call" | custom-call | flops 14495514624 | bytes 20971520 | tf_op jit(solution)/shard_map/ffn_first/pallas_call | solution.py:645
  124.9 4.5 %collective-permute-done.26 = bf16[4,384,768]{2,1,0:T(8,128)(2,1)S(1)} collective-permute-done((bf16[4,384,768]{2,1,0:T(8,128)(2,1)S(1)}, bf16[4,384,768]{2,1,0:T(8,128)(2,1)S(1)}, u32[]{:S(2)}, u32[]{:S(2)}) %collective-permute-start.26) | collective-permute-done | bytes 2359328 | tf_op jit(solution)/shard_map/ppermute | solution.py:42
  130.4 1.5 fusion.7
  131.9 1.3 collective-permute-start.31
  134.2 1.3 collective-permute-start.33
  136.5 33.0 %ffn_last.1 = (bf16[1024,768]{1,0:T(8,128)(2,1)}, f32[1024,768]{1,0:T(8,128)}, bf16[768,1024]{1,0:T(8,128)(2,1)}, bf16[4,480,768]{2,1,0:T(8,128)(2,1)}, bf16[4,4...) custom-call(s32[1]{0:T(128)} %bitcast.me_ref, bf16[1024,768]{1,0:T(8,128)(2,1)} %cot_ref.4, ...), custom_call_target="tpu_custom_call" | custom-call | flops 14495514624 | bytes 20971520 | tf_op jit(solution)/shard_map/ffn_last/pallas_call | solution.py:645
  170.8 3.1 %collective-permute-start.35 = (bf16[96,768]{1,0:T(8,128)(2,1)S(1)}, bf16[96,768]{1,0:T(8,128)(2,1)S(1)}, u32[]{:S(2)}, u32[]{:S(2)}) collective-permute-start(bf16[96,768]{1,0:T(8,128)(2,1)S(1)} %get-tuple-element.274), channel_id=1, source_target_pairs={{0,1},{1,2},{2,3},{3,0},{4,5},{5,6},{6,7},{7,4},{8,9},{9,10},{10,1... | collective-permute-start | bytes 442376 | tf_op jit(solution)/shard_map/ppermute | solution.py:46
  174.4 2.6 collective-permute-start.37
  177.0 2.3 copy-done.48
  179.4 11.0 %attend_back.3 = (bf16[256,1024]{1,0:T(8,128)(2,1)S(1)}, bf16[256,1024]{1,0:T(8,128)(2,1)S(1)}, bf16[256,1024]{1,0:T(8,128)(2,1)S(1)}) custom-call(bf16[2304,1024]{1,0:T(8,128)(2,1)S(1)} %copy-done.48, bf16[2304,1024]{1,0:T(8,128)(2,1)S(1)} %copy-done.48, bf16[2304,1024]{1,0:T(8,128)(2,1)S(1)} %copy-done.48, bf16[256,1024]{1,0:T(8,128)(2,1)S(1)} %copy-done.56, ...), custom_call_target="tpu_custom_call" | custom-call | flops 14000000000 | bytes 5242880 | tf_op jit(solution)/shard_map/attend_back/pallas_call | solution.py:460
  191.3 1.2 collective-permute-start.38
  192.5 1.6 collective-permute-start.39
  194.8 11.2 %attend_back.5 = (bf16[256,1024]{1,0:T(8,128)(2,1)S(1)}, bf16[256,1024]{1,0:T(8,128)(2,1)S(1)}, bf16[256,1024]{1,0:T(8,128)(2,1)S(1)}) custom-call(bf16[2304,1024]{1,0:T(8,128)(2,1)S(1)} %copy-done.48, bf16[2304,1024]{1,0:T(8,128)(2,1)S(1)} %copy-done.48, bf16[2304,1024]{1,0:T(8,128)(2,1)S(1)} %copy-done.48, bf16[256,1024]{1,0:T(8,128)(2,1)S(1)} %copy-done.58, ...), custom_call_target="tpu_custom_call" | custom-call | flops 14000000000 | bytes 5242880 | tf_op jit(solution)/shard_map/attend_back/pallas_call | solution.py:460
  206.0 11.2 %attend_back.4 = (bf16[256,1024]{1,0:T(8,128)(2,1)S(1)}, bf16[256,1024]{1,0:T(8,128)(2,1)S(1)}, bf16[256,1024]{1,0:T(8,128)(2,1)S(1)}) custom-call(bf16[2304,1024]{1,0:T(8,128)(2,1)S(1)} %copy-done.48, bf16[2304,1024]{1,0:T(8,128)(2,1)S(1)} %copy-done.48, bf16[2304,1024]{1,0:T(8,128)(2,1)S(1)} %copy-done.48, bf16[256,1024]{1,0:T(8,128)(2,1)S(1)} %copy-done.54, ...), custom_call_target="tpu_custom_call" | custom-call | flops 14000000000 | bytes 5242880 | tf_op jit(solution)/shard_map/attend_back/pallas_call | solution.py:460
  217.3 7.8 %collective-permute-done.39.refs_2_ = bf16[480,768]{1,0:T(8,128)(2,1)S(1)} collective-permute-done((bf16[480,768]{1,0:T(8,128)(2,1)S(1)}, bf16[480,768]{1,0:T(8,128)(2,1)S(1)}, u32[]{:S(2)}, u32[]{:S(2)}) %collective-permute-start.39) | collective-permute-done | bytes 737312 | tf_op jit(solution)/shard_map/ppermute | solution.py:42
  226.1 1.3 pieces.3
  227.5 9.1 %weight_grad.1 = (bf16[4,96,2432]{2,1,0:T(8,128)(2,1)S(1)}, bf16[4,96,2432]{2,1,0:T(8,128)(2,1)S(1)}) custom-call(s32[1]{0:T(128)} %bitcast.me_ref, bf16[768,1024]{1,0:T(8,128)(2,1)S(1)} %copy-done.46, f32[16,768]{1,0:T(8,128)S(1)} %get-tuple-element.210.vec_ref, f32[8,768]{1,0:T(8,128)S(1)} %get-tuple-element.327.gv_ref, ...), custom_call_target="tpu_custom_call" | custom-call | flops 3623878656 | bytes 10485760 | tf_op jit(solution)/shard_map/weight_grad/pallas_call | solution.py:730
  237.0 3.5 %collective-permute-done.41 = bf16[4,96,2432]{2,1,0:T(8,128)(2,1)S(1)} collective-permute-done((bf16[4,96,2432]{2,1,0:T(8,128)(2,1)S(1)}, bf16[4,96,2432]{2,1,0:T(8,128)(2,1)S(1)}, u32[]{:S(2)}, u32[]{:S(2)}) %collective-permute-start.41) | collective-permute-done | bytes 1867808 | tf_op jit(solution)/shard_map/ppermute | solution.py:42
  240.5 1.4 fusion.11
  241.9 1.3 collective-permute-start.42
  243.2 1.0 collective-permute-start.43
  244.2 1.2 collective-permute-start.44
  246.0 1.6 collective-permute-start.47
  247.6 13.1 %project_back.1 = f32[1024,768]{1,0:T(8,128)} custom-call(s32[1]{0:T(128)} %bitcast.me_ref, bf16[1024,768]{1,0:T(8,128)(2,1)} %x_ref.4, f32[1024,768]{1,0:T(8,128)} %get-tuple-element.249.gm_ref, f32[16,768]{1,0:T(8,128)} %copy-done.28, bf16[256,1024]{1,0:T(8,128)(2,1)} %copy-done.5, bf16[256,1024]{1,0:T(8,128)(2,1)} %copy-done.11, ...), custom_call_target="tpu_custom_call" | custom-call | flops 3623878656 | bytes 20971520 | tf_op jit(solution)/shard_map/project_back/pallas_call | solution.py:771
  260.8 3.8 %collective-permute-done.43 = bf16[96,2432]{1,0:T(8,128)(2,1)} collective-permute-done((bf16[96,2432]{1,0:T(8,128)(2,1)}, bf16[96,2432]{1,0:T(8,128)(2,1)}, u32[]{:S(2)}, u32[]{:S(2)}) %collective-permute-start.43) | collective-permute-done | bytes 466976 | tf_op jit(solution)/shard_map/ppermute | solution.py:42
  264.6 1.4 collective-permute-done.44
  266.0 1.6 add_convert_fusion.8
  268.2 1.7 collective-permute-start.49
  270.0 2.1 collective-permute-start.50
  272.1 6.5 %finish.1 = (f32[24,3072]{1,0:T(8,128)}, f32[96,768]{1,0:T(8,128)}, f32[24,768]{1,0:T(8,128)}) custom-call(bf16[2,768,384]{2,1,0:T(8,128)(2,1)S(1)} %copy-done, bf16[96,768]{1,0:T(8,128)(2,1)S(1)} %copy-done.19, bf16[96,768]{1,0:T(8,128)(2,1)S(1)} %copy-done.21, bf16[96,768]{1,0:T(8,128)(2,1)S(1)} %copy-done.23, bf16[96,768]{1,0:T(8,128)(2,1)S(1)} %copy-done.25, ...), custom_call_target="tpu_custom_call" | custom-call | bytes 3145728 | tf_op jit(solution)/shard_map/finish/pallas_call | solution.py:206
  278.6 1.2 collective-permute-done.49
  279.8 1.0 convert_add_fusion
  (206 shorter events, 16.1 us)
Async XLA Ops:
  3.7 13.7 %collective-permute-start = (bf16[24,2432]{1,0:T(8,128)(2,1)}, bf16[24,2432]{1,0:T(8,128)(2,1)S(1)}, u32[]{:S(2)}, u32[]{:S(2)}) collective-permute-start(bf16[24,2432]{1,0:T(8,128)(2,1)} %get-tuple-element.195.refs_0_), channel_id=1, source_target_pairs={{0,1},{1,2},{2,3},{3,0},{4,5},{5,6},{6,7},{7,4},{8,9},{9,10},{10,1... | collective-permute-start | bytes 350216 | tf_op jit(solution)/shard_map/ppermute | solution.py:46
  6.8 10.6 %collective-permute-start.1 = (bf16[24,2432]{1,0:T(8,128)(2,1)}, bf16[24,2432]{1,0:T(8,128)(2,1)S(1)}, u32[]{:S(2)}, u32[]{:S(2)}) collective-permute-start(bf16[24,2432]{1,0:T(8,128)(2,1)} %get-tuple-element.195.refs_0_), channel_id=1, source_target_pairs={{0,2},{1,3},{2,0},{3,1},{4,6},{5,7},{6,4},{7,5},{8,10},{9,11},{10,... | collective-permute-start | bytes 350216 | tf_op jit(solution)/shard_map/ppermute | solution.py:46
  9.4 8.0 %collective-permute-start.2 = (bf16[24,2432]{1,0:T(8,128)(2,1)}, bf16[24,2432]{1,0:T(8,128)(2,1)S(1)}, u32[]{:S(2)}, u32[]{:S(2)}) collective-permute-start(bf16[24,2432]{1,0:T(8,128)(2,1)} %get-tuple-element.195.refs_0_), channel_id=1, source_target_pairs={{0,3},{1,0},{2,1},{3,2},{4,7},{5,4},{6,5},{7,6},{8,11},{9,8},{10,9... | collective-permute-start | bytes 350216 | tf_op jit(solution)/shard_map/ppermute | solution.py:46
  17.5 209.8 %copy-start.1 = (bf16[96,2432]{1,0:T(8,128)(2,1)}, bf16[96,2432]{1,0:T(8,128)(2,1)S(1)}, u32[]{:S(2)}) copy-start(bf16[96,2432]{1,0:T(8,128)(2,1)S(1)} %line_up.3.rest_0_.rest_9_) | copy-start | bytes 1400836
  17.5 20.8 %collective-permute-start.3 = (bf16[96,2432]{1,0:T(8,128)(2,1)S(1)}, bf16[96,2432]{1,0:T(8,128)(2,1)S(1)}, u32[]{:S(2)}, u32[]{:S(2)}) collective-permute-start(bf16[96,2432]{1,0:T(8,128)(2,1)S(1)} %line_up.3.rest_0_.rest_9_), channel_id=1, source_target_pairs={{0,8},{4,12},{8,0},{12,4},{16,24},{20,28},{24,16},{28,20},{1,9},{5... | collective-permute-start | bytes 1400840 | tf_op jit(solution)/shard_map/ppermute | solution.py:42
  19.1 22.3 %collective-permute-start.4 = (bf16[96,2432]{1,0:T(8,128)(2,1)S(1)}, bf16[96,2432]{1,0:T(8,128)(2,1)}, u32[]{:S(2)}, u32[]{:S(2)}) collective-permute-start(bf16[96,2432]{1,0:T(8,128)(2,1)S(1)} %line_up.3.rest_0_.rest_9_), channel_id=1, source_target_pairs={{0,16},{4,20},{8,24},{12,28},{16,0},{20,4},{24,8},{28,12},{1,17},{... | collective-permute-start | bytes 1400840 | tf_op jit(solution)/shard_map/ppermute | solution.py:42
  20.6 20.8 %collective-permute-start.5 = (bf16[96,2432]{1,0:T(8,128)(2,1)S(1)}, bf16[96,2432]{1,0:T(8,128)(2,1)}, u32[]{:S(2)}, u32[]{:S(2)}) collective-permute-start(bf16[96,2432]{1,0:T(8,128)(2,1)S(1)} %line_up.3.rest_0_.rest_9_), channel_id=1, source_target_pairs={{0,24},{4,28},{8,16},{12,20},{16,8},{20,12},{24,0},{28,4},{1,25},{... | collective-permute-start | bytes 1400840 | tf_op jit(solution)/shard_map/ppermute | solution.py:42
  21.1 9.6 %collective-permute-start.6 = (bf16[120,768]{1,0:T(8,128)(2,1)S(1)}, bf16[120,768]{1,0:T(8,128)(2,1)S(1)}, u32[]{:S(2)}, u32[]{:S(2)}) collective-permute-start(bf16[120,768]{1,0:T(8,128)(2,1)S(1)} %copy-done.17), channel_id=1, source_target_pairs={{0,1},{1,2},{2,3},{3,0},{4,5},{5,6},{6,7},{7,4},{8,9},{9,10},{10,1... | collective-permute-start | bytes 552968 | tf_op jit(solution)/shard_map/ppermute | solution.py:46
  24.0 12.5 %collective-permute-start.7 = (bf16[120,768]{1,0:T(8,128)(2,1)S(1)}, bf16[120,768]{1,0:T(8,128)(2,1)S(1)}, u32[]{:S(2)}, u32[]{:S(2)}) collective-permute-start(bf16[120,768]{1,0:T(8,128)(2,1)S(1)} %copy-done.17), channel_id=1, source_target_pairs={{0,2},{1,3},{2,0},{3,1},{4,6},{5,7},{6,4},{7,5},{8,10},{9,11},{10,... | collective-permute-start | bytes 552968 | tf_op jit(solution)/shard_map/ppermute | solution.py:46
  30.7 7.5 %collective-permute-start.8 = (bf16[120,768]{1,0:T(8,128)(2,1)S(1)}, bf16[120,768]{1,0:T(8,128)(2,1)S(1)}, u32[]{:S(2)}, u32[]{:S(2)}) collective-permute-start(bf16[120,768]{1,0:T(8,128)(2,1)S(1)} %copy-done.17), channel_id=1, source_target_pairs={{0,3},{1,0},{2,1},{3,2},{4,7},{5,4},{6,5},{7,6},{8,11},{9,8},{10,9... | collective-permute-start | bytes 552968 | tf_op jit(solution)/shard_map/ppermute | solution.py:46
  38.3 60.9 %copy-start.3 = (bf16[480,768]{1,0:T(8,128)(2,1)}, bf16[480,768]{1,0:T(8,128)(2,1)S(1)}, u32[]{:S(2)}) copy-start(bf16[480,768]{1,0:T(8,128)(2,1)S(1)} %line_up.4.rest_3_.rest_11_) | copy-start | bytes 2211844
  38.3 189.0 %copy-start.14 = (bf16[96,2432]{1,0:T(8,128)(2,1)}, bf16[96,2432]{1,0:T(8,128)(2,1)S(1)}, u32[]{:S(2)}) copy-start(bf16[96,2432]{1,0:T(8,128)(2,1)S(1)} %collective-permute-done.3.rest_2_.rest_11_) | copy-start | bytes 1400836
  41.4 2.6 collective-permute-start.10
  41.4 4.1 %collective-permute-start.11 = (bf16[96,2432]{1,0:T(8,128)(2,1)}, bf16[96,2432]{1,0:T(8,128)(2,1)}, u32[]{:S(2)}, u32[]{:S(2)}) collective-permute-start(bf16[96,2432]{1,0:T(8,128)(2,1)} %collective-permute-done.4.rest_4_.rest_13_), channel_id=1, source_target_pairs={{0,4},{4,0},{8,12},{12,8},{16,20},{20,16},{24,28},{28,24},{1,5},{5... | collective-permute-start | bytes 1400840 | tf_op jit(solution)/shard_map/ppermute | solution.py:42
  41.9 4.8 %collective-permute-start.12 = (bf16[96,2432]{1,0:T(8,128)(2,1)}, bf16[96,2432]{1,0:T(8,128)(2,1)}, u32[]{:S(2)}, u32[]{:S(2)}) collective-permute-start(bf16[96,2432]{1,0:T(8,128)(2,1)} %collective-permute-done.5.rest_6_.rest_15_), channel_id=1, source_target_pairs={{0,4},{4,0},{8,12},{12,8},{16,20},{20,16},{24,28},{28,24},{1,5},{5... | collective-permute-start | bytes 1400840 | tf_op jit(solution)/shard_map/ppermute | solution.py:42
  41.9 4.8 %collective-permute-start.9 = (bf16[96,2432]{1,0:T(8,128)(2,1)S(1)}, bf16[96,2432]{1,0:T(8,128)(2,1)}, u32[]{:S(2)}, u32[]{:S(2)}) collective-permute-start(bf16[96,2432]{1,0:T(8,128)(2,1)S(1)} %line_up.3.rest_0_.rest_9_), channel_id=1, source_target_pairs={{0,4},{4,0},{8,12},{12,8},{16,20},{20,16},{24,28},{28,24},{1,5},{5... | collective-permute-start | bytes 1400840 | tf_op jit(solution)/shard_map/ppermute | solution.py:42
  42.4 34.6 %collective-permute-start.13 = (bf16[480,768]{1,0:T(8,128)(2,1)S(1)}, bf16[480,768]{1,0:T(8,128)(2,1)S(1)}, u32[]{:S(2)}, u32[]{:S(2)}) collective-permute-start(bf16[480,768]{1,0:T(8,128)(2,1)S(1)} %line_up.4.rest_3_.rest_11_), channel_id=1, source_target_pairs={{0,8},{4,12},{8,0},{12,4},{16,24},{20,28},{24,16},{28,20},{1,9},{5... | collective-permute-start | bytes 2211848 | tf_op jit(solution)/shard_map/ppermute | solution.py:42
  44.0 34.3 %collective-permute-start.14 = (bf16[480,768]{1,0:T(8,128)(2,1)S(1)}, bf16[480,768]{1,0:T(8,128)(2,1)S(1)}, u32[]{:S(2)}, u32[]{:S(2)}) collective-permute-start(bf16[480,768]{1,0:T(8,128)(2,1)S(1)} %line_up.4.rest_3_.rest_11_), channel_id=1, source_target_pairs={{0,16},{4,20},{8,24},{12,28},{16,0},{20,4},{24,8},{28,12},{1,17},{... | collective-permute-start | bytes 2211848 | tf_op jit(solution)/shard_map/ppermute | solution.py:42
  45.5 32.8 %collective-permute-start.15 = (bf16[480,768]{1,0:T(8,128)(2,1)S(1)}, bf16[480,768]{1,0:T(8,128)(2,1)S(1)}, u32[]{:S(2)}, u32[]{:S(2)}) collective-permute-start(bf16[480,768]{1,0:T(8,128)(2,1)S(1)} %line_up.4.rest_3_.rest_11_), channel_id=1, source_target_pairs={{0,24},{4,28},{8,16},{12,20},{16,8},{20,12},{24,0},{28,4},{1,25},{... | collective-permute-start | bytes 2211848 | tf_op jit(solution)/shard_map/ppermute | solution.py:42
  57.4 33.4 %copy-start.47 = (bf16[2304,1024]{1,0:T(8,128)(2,1)}, bf16[2304,1024]{1,0:T(8,128)(2,1)S(1)}, u32[]{:S(2)}) copy-start(bf16[2304,1024]{1,0:T(8,128)(2,1)S(1)} %get-tuple-element.223.q_ref.k_ref.v_ref) | copy-start | bytes 14155780
  57.4 170.0 %copy-start.28 = (f32[16,768]{1,0:T(8,128)}, f32[16,768]{1,0:T(8,128)S(1)}, u32[]{:S(2)}) copy-start(f32[16,768]{1,0:T(8,128)S(1)} %get-tuple-element.210.vec_ref) | copy-start | bytes 147460
  57.4 10.6 %collective-permute-start.16 = (bf16[96,768]{1,0:T(8,128)(2,1)S(1)}, bf16[96,768]{1,0:T(8,128)(2,1)S(1)}, u32[]{:S(2)}, u32[]{:S(2)}) collective-permute-start(bf16[96,768]{1,0:T(8,128)(2,1)S(1)} %copy-done.26), channel_id=1, source_target_pairs={{0,1},{1,2},{2,3},{3,0},{4,5},{5,6},{6,7},{7,4},{8,9},{9,10},{10,1... | collective-permute-start | bytes 442376 | tf_op jit(solution)/shard_map/ppermute | solution.py:46
  60.9 16.0 %collective-permute-start.17 = (bf16[96,768]{1,0:T(8,128)(2,1)S(1)}, bf16[96,768]{1,0:T(8,128)(2,1)S(1)}, u32[]{:S(2)}, u32[]{:S(2)}) collective-permute-start(bf16[96,768]{1,0:T(8,128)(2,1)S(1)} %copy-done.26), channel_id=1, source_target_pairs={{0,2},{1,3},{2,0},{3,1},{4,6},{5,7},{6,4},{7,5},{8,10},{9,11},{10,... | collective-permute-start | bytes 442376 | tf_op jit(solution)/shard_map/ppermute | solution.py:46
  68.0 31.3 %copy-start.55 = (bf16[256,1024]{1,0:T(8,128)(2,1)}, bf16[256,1024]{1,0:T(8,128)(2,1)S(1)}, u32[]{:S(2)}) copy-start(bf16[256,1024]{1,0:T(8,128)(2,1)S(1)} %get-tuple-element.213.rest_0_.o_ref) | copy-start | bytes 1572868
  68.0 9.0 %collective-permute-start.18 = (bf16[96,768]{1,0:T(8,128)(2,1)S(1)}, bf16[96,768]{1,0:T(8,128)(2,1)S(1)}, u32[]{:S(2)}, u32[]{:S(2)}) collective-permute-start(bf16[96,768]{1,0:T(8,128)(2,1)S(1)} %copy-done.26), channel_id=1, source_target_pairs={{0,3},{1,0},{2,1},{3,2},{4,7},{5,4},{6,5},{7,6},{8,11},{9,8},{10,9... | collective-permute-start | bytes 442376 | tf_op jit(solution)/shard_map/ppermute | solution.py:46
  78.3 18.5 %collective-permute-start.19 = (bf16[480,768]{1,0:T(8,128)(2,1)S(1)}, bf16[480,768]{1,0:T(8,128)(2,1)S(1)}, u32[]{:S(2)}, u32[]{:S(2)}) collective-permute-start(bf16[480,768]{1,0:T(8,128)(2,1)S(1)} %line_up.4.rest_3_.rest_11_), channel_id=1, source_target_pairs={{0,4},{4,0},{8,12},{12,8},{16,20},{20,16},{24,28},{28,24},{1,5},{5... | collective-permute-start | bytes 2211848 | tf_op jit(solution)/shard_map/ppermute | solution.py:42
  78.4 19.4 %collective-permute-start.20 = (bf16[480,768]{1,0:T(8,128)(2,1)S(1)}, bf16[480,768]{1,0:T(8,128)(2,1)S(1)}, u32[]{:S(2)}, u32[]{:S(2)}) collective-permute-start(bf16[480,768]{1,0:T(8,128)(2,1)S(1)} %collective-permute-done.13.rest_5_.rest_13_), channel_id=1, source_target_pairs={{0,4},{4,0},{8,12},{12,8},{16,20},{20,16},{24,28},{28,24},{1,5},{5... | collective-permute-start | bytes 2211848 | tf_op jit(solution)/shard_map/ppermute | solution.py:42
  78.9 20.3 %collective-permute-start.21 = (bf16[480,768]{1,0:T(8,128)(2,1)S(1)}, bf16[480,768]{1,0:T(8,128)(2,1)S(1)}, u32[]{:S(2)}, u32[]{:S(2)}) collective-permute-start(bf16[480,768]{1,0:T(8,128)(2,1)S(1)} %collective-permute-done.14.rest_7_.rest_15_), channel_id=1, source_target_pairs={{0,4},{4,0},{8,12},{12,8},{16,20},{20,16},{24,28},{28,24},{1,5},{5... | collective-permute-start | bytes 2211848 | tf_op jit(solution)/shard_map/ppermute | solution.py:42
  79.0 20.2 %collective-permute-start.22 = (bf16[480,768]{1,0:T(8,128)(2,1)S(1)}, bf16[480,768]{1,0:T(8,128)(2,1)S(1)}, u32[]{:S(2)}, u32[]{:S(2)}) collective-permute-start(bf16[480,768]{1,0:T(8,128)(2,1)S(1)} %collective-permute-done.15.rest_9_.rest_17_), channel_id=1, source_target_pairs={{0,4},{4,0},{8,12},{12,8},{16,20},{20,16},{24,28},{28,24},{1,5},{5... | collective-permute-start | bytes 2211848 | tf_op jit(solution)/shard_map/ppermute | solution.py:42
  89.5 39.9 %copy-start.4 = (bf16[384,768]{1,0:T(8,128)(2,1)}, bf16[384,768]{1,0:T(8,128)(2,1)S(1)}, u32[]{:S(2)}) copy-start(bf16[384,768]{1,0:T(8,128)(2,1)S(1)} %line_up.5.rest_3_) | copy-start | bytes 1769476
  89.5 35.2 %collective-permute-start.23 = (bf16[384,768]{1,0:T(8,128)(2,1)S(1)}, bf16[384,768]{1,0:T(8,128)(2,1)S(1)}, u32[]{:S(2)}, u32[]{:S(2)}) collective-permute-start(bf16[384,768]{1,0:T(8,128)(2,1)S(1)} %line_up.5.rest_3_), channel_id=1, source_target_pairs={{0,8},{4,12},{8,0},{12,4},{16,24},{20,28},{24,16},{28,20},{1,9},{5... | collective-permute-start | bytes 1769480 | tf_op jit(solution)/shard_map/ppermute | solution.py:42
  96.9 27.8 %copy-start.57 = (bf16[256,1024]{1,0:T(8,128)(2,1)}, bf16[256,1024]{1,0:T(8,128)(2,1)S(1)}, u32[]{:S(2)}) copy-start(bf16[256,1024]{1,0:T(8,128)(2,1)S(1)} %get-tuple-element.224.rest_2_.o_ref) | copy-start | bytes 1572868
  96.9 27.8 %copy-start.34 = (bf16[480,768]{1,0:T(8,128)(2,1)}, bf16[480,768]{1,0:T(8,128)(2,1)S(1)}, u32[]{:S(2)}) copy-start(bf16[480,768]{1,0:T(8,128)(2,1)S(1)} %collective-permute-done.19.rest_4_.rest_12_) | copy-start | bytes 2211844
  96.9 27.8 %collective-permute-start.24 = (bf16[384,768]{1,0:T(8,128)(2,1)S(1)}, bf16[384,768]{1,0:T(8,128)(2,1)S(1)}, u32[]{:S(2)}, u32[]{:S(2)}) collective-permute-start(bf16[384,768]{1,0:T(8,128)(2,1)S(1)} %line_up.5.rest_3_), channel_id=1, source_target_pairs={{0,16},{4,20},{8,24},{12,28},{16,0},{20,4},{24,8},{28,12},{1,17},{... | collective-permute-start | bytes 1769480 | tf_op jit(solution)/shard_map/ppermute | solution.py:42
  97.8 26.9 %copy-start.35 = (bf16[480,768]{1,0:T(8,128)(2,1)}, bf16[480,768]{1,0:T(8,128)(2,1)S(1)}, u32[]{:S(2)}) copy-start(bf16[480,768]{1,0:T(8,128)(2,1)S(1)} %collective-permute-done.20.rest_6_.rest_14_) | copy-start | bytes 2211844
  97.8 27.0 %collective-permute-start.25 = (bf16[384,768]{1,0:T(8,128)(2,1)S(1)}, bf16[384,768]{1,0:T(8,128)(2,1)S(1)}, u32[]{:S(2)}, u32[]{:S(2)}) collective-permute-start(bf16[384,768]{1,0:T(8,128)(2,1)S(1)} %line_up.5.rest_3_), channel_id=1, source_target_pairs={{0,24},{4,28},{8,16},{12,20},{16,8},{20,12},{24,0},{28,4},{1,25},{... | collective-permute-start | bytes 1769480 | tf_op jit(solution)/shard_map/ppermute | solution.py:42
  124.8 4.6 %collective-permute-start.26 = (bf16[4,384,768]{2,1,0:T(8,128)(2,1)S(1)}, bf16[4,384,768]{2,1,0:T(8,128)(2,1)S(1)}, u32[]{:S(2)}, u32[]{:S(2)}) collective-permute-start(bf16[4,384,768]{2,1,0:T(8,128)(2,1)S(1)} %get-tuple-element.233), channel_id=1, source_target_pairs={{0,4},{4,0},{8,12},{12,8},{16,20},{20,16},{24,28},{28,24},{1,5},{5... | collective-permute-start | bytes 7077896 | tf_op jit(solution)/shard_map/ppermute | solution.py:42
  129.4 3.8 %collective-permute-start.27 = (bf16[384,768]{1,0:T(8,128)(2,1)S(1)}, bf16[384,768]{1,0:T(8,128)(2,1)S(1)}, u32[]{:S(2)}, u32[]{:S(2)}) collective-permute-start(bf16[384,768]{1,0:T(8,128)(2,1)S(1)} %line_up.5.rest_3_), channel_id=1, source_target_pairs={{0,4},{4,0},{8,12},{12,8},{16,20},{20,16},{24,28},{28,24},{1,5},{5... | collective-permute-start | bytes 1769480 | tf_op jit(solution)/shard_map/ppermute | solution.py:42
  129.5 4.6 %collective-permute-start.28 = (bf16[384,768]{1,0:T(8,128)(2,1)S(1)}, bf16[384,768]{1,0:T(8,128)(2,1)S(1)}, u32[]{:S(2)}, u32[]{:S(2)}) collective-permute-start(bf16[384,768]{1,0:T(8,128)(2,1)S(1)} %collective-permute-done.23.rest_5_), channel_id=1, source_target_pairs={{0,4},{4,0},{8,12},{12,8},{16,20},{20,16},{24,28},{28,24},{1,5},{5... | collective-permute-start | bytes 1769480 | tf_op jit(solution)/shard_map/ppermute | solution.py:42
  129.9 5.6 %collective-permute-start.29 = (bf16[384,768]{1,0:T(8,128)(2,1)S(1)}, bf16[384,768]{1,0:T(8,128)(2,1)S(1)}, u32[]{:S(2)}, u32[]{:S(2)}) collective-permute-start(bf16[384,768]{1,0:T(8,128)(2,1)S(1)} %collective-permute-done.24.rest_7_), channel_id=1, source_target_pairs={{0,4},{4,0},{8,12},{12,8},{16,20},{20,16},{24,28},{28,24},{1,5},{5... | collective-permute-start | bytes 1769480 | tf_op jit(solution)/shard_map/ppermute | solution.py:42
  130.1 5.4 %collective-permute-start.30 = (bf16[384,768]{1,0:T(8,128)(2,1)S(1)}, bf16[384,768]{1,0:T(8,128)(2,1)S(1)}, u32[]{:S(2)}, u32[]{:S(2)}) collective-permute-start(bf16[384,768]{1,0:T(8,128)(2,1)S(1)} %collective-permute-done.25.rest_9_), channel_id=1, source_target_pairs={{0,4},{4,0},{8,12},{12,8},{16,20},{20,16},{24,28},{28,24},{1,5},{5... | collective-permute-start | bytes 1769480 | tf_op jit(solution)/shard_map/ppermute | solution.py:42
  131.9 37.7 %collective-permute-start.31 = (bf16[384,768]{1,0:T(8,128)(2,1)}, bf16[384,768]{1,0:T(8,128)(2,1)S(1)}, u32[]{:S(2)}, u32[]{:S(2)}) collective-permute-start(bf16[384,768]{1,0:T(8,128)(2,1)} %get-tuple-element.251), channel_id=1, source_target_pairs={{0,8},{4,12},{8,0},{12,4},{16,24},{20,28},{24,16},{28,20},{1,9},{5... | collective-permute-start | bytes 1769480 | tf_op jit(solution)/shard_map/ppermute | solution.py:42
  133.2 36.4 %collective-permute-start.32 = (bf16[384,768]{1,0:T(8,128)(2,1)S(1)}, bf16[384,768]{1,0:T(8,128)(2,1)S(1)}, u32[]{:S(2)}, u32[]{:S(2)}) collective-permute-start(bf16[384,768]{1,0:T(8,128)(2,1)S(1)} %get-tuple-element.252), channel_id=1, source_target_pairs={{0,16},{4,20},{8,24},{12,28},{16,0},{20,4},{24,8},{28,12},{1,17},{... | collective-permute-start | bytes 1769480 | tf_op jit(solution)/shard_map/ppermute | solution.py:42
  134.2 35.4 %collective-permute-start.33 = (bf16[384,768]{1,0:T(8,128)(2,1)S(1)}, bf16[384,768]{1,0:T(8,128)(2,1)S(1)}, u32[]{:S(2)}, u32[]{:S(2)}) collective-permute-start(bf16[384,768]{1,0:T(8,128)(2,1)S(1)} %get-tuple-element.253), channel_id=1, source_target_pairs={{0,24},{4,28},{8,16},{12,20},{16,8},{20,12},{24,0},{28,4},{1,25},{... | collective-permute-start | bytes 1769480 | tf_op jit(solution)/shard_map/ppermute | solution.py:42
  169.6 20.9 %collective-permute-start.34 = (bf16[4,480,768]{2,1,0:T(8,128)(2,1)}, bf16[4,480,768]{2,1,0:T(8,128)(2,1)S(1)}, u32[]{:S(2)}, u32[]{:S(2)}) collective-permute-start(bf16[4,480,768]{2,1,0:T(8,128)(2,1)} %get-tuple-element.257), channel_id=1, source_target_pairs={{0,4},{4,0},{8,12},{12,8},{16,20},{20,16},{24,28},{28,24},{1,5},{5... | collective-permute-start | bytes 8847368 | tf_op jit(solution)/shard_map/ppermute | solution.py:42
  170.8 19.6 %collective-permute-start.35 = (bf16[96,768]{1,0:T(8,128)(2,1)S(1)}, bf16[96,768]{1,0:T(8,128)(2,1)S(1)}, u32[]{:S(2)}, u32[]{:S(2)}) collective-permute-start(bf16[96,768]{1,0:T(8,128)(2,1)S(1)} %get-tuple-element.274), channel_id=1, source_target_pairs={{0,1},{1,2},{2,3},{3,0},{4,5},{5,6},{6,7},{7,4},{8,9},{9,10},{10,1... | collective-permute-start | bytes 442376 | tf_op jit(solution)/shard_map/ppermute | solution.py:46
  173.9 16.5 %collective-permute-start.36 = (bf16[96,768]{1,0:T(8,128)(2,1)S(1)}, bf16[96,768]{1,0:T(8,128)(2,1)S(1)}, u32[]{:S(2)}, u32[]{:S(2)}) collective-permute-start(bf16[96,768]{1,0:T(8,128)(2,1)S(1)} %get-tuple-element.275), channel_id=1, source_target_pairs={{0,2},{1,3},{2,0},{3,1},{4,6},{5,7},{6,4},{7,5},{8,10},{9,11},{10,... | collective-permute-start | bytes 442376 | tf_op jit(solution)/shard_map/ppermute | solution.py:46
  174.4 16.1 %collective-permute-start.37 = (bf16[96,768]{1,0:T(8,128)(2,1)S(1)}, bf16[96,768]{1,0:T(8,128)(2,1)S(1)}, u32[]{:S(2)}, u32[]{:S(2)}) collective-permute-start(bf16[96,768]{1,0:T(8,128)(2,1)S(1)} %get-tuple-element.276), channel_id=1, source_target_pairs={{0,3},{1,0},{2,1},{3,2},{4,7},{5,4},{6,5},{7,6},{8,11},{9,8},{10,9... | collective-permute-start | bytes 442376 | tf_op jit(solution)/shard_map/ppermute | solution.py:46
  190.4 37.0 %copy-start.5 = (bf16[256,1024]{1,0:T(8,128)(2,1)}, bf16[256,1024]{1,0:T(8,128)(2,1)S(1)}, u32[]{:S(2)}) copy-start(bf16[256,1024]{1,0:T(8,128)(2,1)S(1)} %get-tuple-element.332.rest_0_) | copy-start | bytes 1572868
  190.4 37.0 %copy-start.6 = (bf16[256,1024]{1,0:T(8,128)(2,1)}, bf16[256,1024]{1,0:T(8,128)(2,1)S(1)}, u32[]{:S(2)}) copy-start(bf16[256,1024]{1,0:T(8,128)(2,1)S(1)} %get-tuple-element.335.rest_3_) | copy-start | bytes 1572868
  190.4 37.0 %copy-start.7 = (bf16[256,1024]{1,0:T(8,128)(2,1)}, bf16[256,1024]{1,0:T(8,128)(2,1)S(1)}, u32[]{:S(2)}) copy-start(bf16[256,1024]{1,0:T(8,128)(2,1)S(1)} %get-tuple-element.338.rest_6_) | copy-start | bytes 1572868
  191.3 26.0 %collective-permute-start.38 = (bf16[480,768]{1,0:T(8,128)(2,1)S(1)}, bf16[480,768]{1,0:T(8,128)(2,1)S(1)}, u32[]{:S(2)}, u32[]{:S(2)}) collective-permute-start(bf16[480,768]{1,0:T(8,128)(2,1)S(1)} %get-tuple-element.281), channel_id=1, source_target_pairs={{0,8},{4,12},{8,0},{12,4},{16,24},{20,28},{24,16},{28,20},{1,9},{5... | collective-permute-start | bytes 2211848 | tf_op jit(solution)/shard_map/ppermute | solution.py:42
  192.5 32.7 %collective-permute-start.39 = (bf16[480,768]{1,0:T(8,128)(2,1)S(1)}, bf16[480,768]{1,0:T(8,128)(2,1)S(1)}, u32[]{:S(2)}, u32[]{:S(2)}) collective-permute-start(bf16[480,768]{1,0:T(8,128)(2,1)S(1)} %get-tuple-element.282), channel_id=1, source_target_pairs={{0,16},{4,20},{8,24},{12,28},{16,0},{20,4},{24,8},{28,12},{1,17},{... | collective-permute-start | bytes 2211848 | tf_op jit(solution)/shard_map/ppermute | solution.py:42
  194.1 32.0 %collective-permute-start.40 = (bf16[480,768]{1,0:T(8,128)(2,1)S(1)}, bf16[480,768]{1,0:T(8,128)(2,1)S(1)}, u32[]{:S(2)}, u32[]{:S(2)}) collective-permute-start(bf16[480,768]{1,0:T(8,128)(2,1)S(1)} %get-tuple-element.283), channel_id=1, source_target_pairs={{0,24},{4,28},{8,16},{12,20},{16,8},{20,12},{24,0},{28,4},{1,25},{... | collective-permute-start | bytes 2211848 | tf_op jit(solution)/shard_map/ppermute | solution.py:42
  236.6 3.9 %collective-permute-start.41 = (bf16[4,96,2432]{2,1,0:T(8,128)(2,1)S(1)}, bf16[4,96,2432]{2,1,0:T(8,128)(2,1)S(1)}, u32[]{:S(2)}, u32[]{:S(2)}) collective-permute-start(bf16[4,96,2432]{2,1,0:T(8,128)(2,1)S(1)} %get-tuple-element.331), channel_id=1, source_target_pairs={{0,4},{4,0},{8,12},{12,8},{16,20},{20,16},{24,28},{28,24},{1,5},{5... | collective-permute-start | bytes 5603336 | tf_op jit(solution)/shard_map/ppermute | solution.py:42
  236.7 9.3 %collective-permute-start.45 = (bf16[120,768]{1,0:T(8,128)(2,1)}, bf16[120,768]{1,0:T(8,128)(2,1)S(1)}, u32[]{:S(2)}, u32[]{:S(2)}) collective-permute-start(bf16[120,768]{1,0:T(8,128)(2,1)} %get-tuple-element.346), channel_id=1, source_target_pairs={{0,1},{1,2},{2,3},{3,0},{4,5},{5,6},{6,7},{7,4},{8,9},{9,10},{10,1... | collective-permute-start | bytes 552968 | tf_op jit(solution)/shard_map/ppermute | solution.py:46
  241.9 18.9 %collective-permute-start.42 = (bf16[96,2432]{1,0:T(8,128)(2,1)}, bf16[96,2432]{1,0:T(8,128)(2,1)}, u32[]{:S(2)}, u32[]{:S(2)}) collective-permute-start(bf16[96,2432]{1,0:T(8,128)(2,1)} %get-tuple-element.342), channel_id=1, source_target_pairs={{0,8},{4,12},{8,0},{12,4},{16,24},{20,28},{24,16},{28,20},{1,9},{5... | collective-permute-start | bytes 1400840 | tf_op jit(solution)/shard_map/ppermute | solution.py:42
  243.2 21.4 %collective-permute-start.43 = (bf16[96,2432]{1,0:T(8,128)(2,1)}, bf16[96,2432]{1,0:T(8,128)(2,1)}, u32[]{:S(2)}, u32[]{:S(2)}) collective-permute-start(bf16[96,2432]{1,0:T(8,128)(2,1)} %get-tuple-element.343), channel_id=1, source_target_pairs={{0,16},{4,20},{8,24},{12,28},{16,0},{20,4},{24,8},{28,12},{1,17},{... | collective-permute-start | bytes 1400840 | tf_op jit(solution)/shard_map/ppermute | solution.py:42
  244.2 21.7 %collective-permute-start.44 = (bf16[96,2432]{1,0:T(8,128)(2,1)}, bf16[96,2432]{1,0:T(8,128)(2,1)}, u32[]{:S(2)}, u32[]{:S(2)}) collective-permute-start(bf16[96,2432]{1,0:T(8,128)(2,1)} %get-tuple-element.344), channel_id=1, source_target_pairs={{0,24},{4,28},{8,16},{12,20},{16,8},{20,12},{24,0},{28,4},{1,25},{... | collective-permute-start | bytes 1400840 | tf_op jit(solution)/shard_map/ppermute | solution.py:42
  245.4 15.3 %collective-permute-start.46 = (bf16[120,768]{1,0:T(8,128)(2,1)S(1)}, bf16[120,768]{1,0:T(8,128)(2,1)S(1)}, u32[]{:S(2)}, u32[]{:S(2)}) collective-permute-start(bf16[120,768]{1,0:T(8,128)(2,1)S(1)} %copy-done.41), channel_id=1, source_target_pairs={{0,2},{1,3},{2,0},{3,1},{4,6},{5,7},{6,4},{7,5},{8,10},{9,11},{10,... | collective-permute-start | bytes 552968 | tf_op jit(solution)/shard_map/ppermute | solution.py:46
  246.0 14.8 %collective-permute-start.47 = (bf16[120,768]{1,0:T(8,128)(2,1)S(1)}, bf16[120,768]{1,0:T(8,128)(2,1)S(1)}, u32[]{:S(2)}, u32[]{:S(2)}) collective-permute-start(bf16[120,768]{1,0:T(8,128)(2,1)S(1)} %copy-done.39), channel_id=1, source_target_pairs={{0,3},{1,0},{2,1},{3,2},{4,7},{5,4},{6,5},{7,6},{8,11},{9,8},{10,9... | collective-permute-start | bytes 552968 | tf_op jit(solution)/shard_map/ppermute | solution.py:46
  268.2 10.3 %collective-permute-start.48 = (bf16[24,2432]{1,0:T(8,128)(2,1)}, bf16[24,2432]{1,0:T(8,128)(2,1)S(1)}, u32[]{:S(2)}, u32[]{:S(2)}) collective-permute-start(bf16[24,2432]{1,0:T(8,128)(2,1)} %get-tuple-element.383), channel_id=1, source_target_pairs={{0,1},{1,2},{2,3},{3,0},{4,5},{5,6},{6,7},{7,4},{8,9},{9,10},{10,1... | collective-permute-start | bytes 350216 | tf_op jit(solution)/shard_map/ppermute | solution.py:46
  268.2 11.6 %collective-permute-start.49 = (bf16[24,2432]{1,0:T(8,128)(2,1)S(1)}, bf16[24,2432]{1,0:T(8,128)(2,1)S(1)}, u32[]{:S(2)}, u32[]{:S(2)}) collective-permute-start(bf16[24,2432]{1,0:T(8,128)(2,1)S(1)} %get-tuple-element.385), channel_id=1, source_target_pairs={{0,2},{1,3},{2,0},{3,1},{4,6},{5,7},{6,4},{7,5},{8,10},{9,11},{10,... | collective-permute-start | bytes 350216 | tf_op jit(solution)/shard_map/ppermute | solution.py:46
  270.0 9.8 %collective-permute-start.50 = (bf16[24,2432]{1,0:T(8,128)(2,1)S(1)}, bf16[24,2432]{1,0:T(8,128)(2,1)}, u32[]{:S(2)}, u32[]{:S(2)}) collective-permute-start(bf16[24,2432]{1,0:T(8,128)(2,1)S(1)} %get-tuple-element.384), channel_id=1, source_target_pairs={{0,3},{1,0},{2,1},{3,2},{4,7},{5,4},{6,5},{7,6},{8,11},{9,8},{10,9... | collective-permute-start | bytes 350216 | tf_op jit(solution)/shard_map/ppermute | solution.py:46
  (56 other events, 579.7 us)
where the time goes:
time: 284 us; the launch traced here: 283 us
  Pallas kernels  164 us (58%)
  starting transfers between devices  56.9 us (20%)
  waiting for transfers between devices  40 us (14%)
  local copies, waits for them, and re-layouts  14.6 us (5%)
  other arithmetic  6.08 us (2%)
    pallas_call x2, Pallas kernels, ffn_call(): pl.pallas_call(functools.partial(kernel, nd), grid=(ff // D,), in_specs=s...  58.3 us
    pallas_call x3, Pallas kernels, attend_back(): pl.pallas_call(attend_back_kernel, grid=(1,), in_specs=[head_rows(group +...  33.4 us
    ppermute x18, starting transfers between devices, shift(): lax.ppermute(value, 'fsdp', [(i, (i + step) % count) for i in range(count)])  32 us
    ppermute x33, waiting for transfers between devices, flip(): return lax.ppermute(value, 'dp', [(i, i ^ bit) for i in range(count)])  26.8 us
    ppermute x33, starting transfers between devices, flip(): return lax.ppermute(value, 'dp', [(i, i ^ bit) for i in range(count)])  25 us
    pallas_call x3, Pallas kernels, attend(): pl.pallas_call(attend_kernel, grid=(1,), in_specs=[head_rows(group + j *...  18.2 us
    ppermute x18, waiting for transfers between devices, shift(): lax.ppermute(value, 'fsdp', [(i, (i + step) % count) for i in range(count)])  13.2 us
    pallas_call x1, Pallas kernels, project_back(): pl.pallas_call(functools.partial(project_back_kernel, nd), grid=(1,), in_...  13.1 us
  transfers between devices with their start and end apart: 51, of which 14 were waited for; matrix products, arithmetic and copies ran while one was open for 1% of the time, Pallas kernels for 53%

commit v1 on v0

--- a/solution.py
+++ b/solution.py
@@ -584,8 +584,9 @@
     att, blocks, rest = rest[:GROUPS], rest[GROUPS : GROUPS + nd], rest[GROUPS + nd :]
     others, rest = rest[:nd], rest[nd:]
     mid_ref, n2_ref, part_ref, naccin_ref = rest[:4]
-    out_ref, gm_ref, dt_ref, send, keep, gbe_ref, gv_ref = rest[4:11]
-    comb, exp, red, mid, part, nin, n2, n2t, oacc, nacc, ascr, gscr, tmp, sems = rest[11:]
+    out_any, gm_any, dt_any, send_any, keep_any, gbe_ref, gv_ref = rest[4:11]
+    comb, exp, red, mid, part, nin, n2, n2t, oacc, nacc, ascr, gscr, tmp, sems = rest[11:25]
+    out_ref, gm_ref, dt_ref, send, keep = rest[25:]
     i = pl.program_id(0)
     me = me_ref[0]
     rb, rr = D // nd, red.shape[0] // nd
@@ -593,6 +594,17 @@
         pltpu.make_async_copy(a, b, sems.at[4 * nd + j])
         for j, (a, b) in enumerate(((n2_ref, n2), (mid_ref, mid), (part_ref, part), (naccin_ref, nin)))
     ]
+    early, last = pl.ds(0, 2 * rb + rr), pl.ds(2 * rb + rr, rb)
+    leaving = (
+        (send.at[:, early, :], send_any.at[:, early, :]),
+        (keep.at[:, early, :], keep_any.at[:, early, :]),
+        (out_ref, out_any),
+        (gm_ref, gm_any),
+        (dt_ref, dt_any),
+        (send.at[:, last, :], send_any.at[:, last, :]),
+        (keep.at[:, last, :], keep_any.at[:, last, :]),
+    )
+    outs = [pltpu.make_async_copy(a, b, sems.at[4 * nd + 4 + j]) for j, (a, b) in enumerate(leaving)]
 
     @pl.when(i == 0)
     def _():
@@ -612,6 +624,8 @@
 
     @pl.when(i == pl.num_programs(0) - 1)
     def _():
+        for copy in outs[:2]:
+            copy.start()
         for copy in ins[1:]:
             copy.wait()
         gv_ref[...] = jnp.zeros((8, D), f32)
@@ -630,10 +644,17 @@
             gv_ref[2:6, :] += jnp.concatenate([jnp.sum(v, axis=0, keepdims=True) for v in sums], axis=0)
 
         token_loop(step)
+        outs[2].start()
+        outs[3].start()
         dt_ref[...] = dot(comb[...], n2t[...]).astype(bf16)
+        outs[4].start()
         for g in range(GROUPS):
             tmp[g * GR : (g + 1) * GR, :] = dot(att[g][...], n2[...]).astype(bf16)
         emit(me, tmp, send, keep, slice(2 * rb + rr, 3 * rb + rr))
+        outs[5].start()
+        outs[6].start()
+        for copy in outs:
+            copy.wait()
 
 
 def ffn_call(kernel, specs, arrays, nd, rows, out_shapes, last):
@@ -646,8 +667,9 @@
         functools.partial(kernel, nd),
         grid=(ff // D,),
         in_specs=specs,
-        out_specs=[whole(x.shape) if last else ANY for x in out_shapes]
-        + [whole(half), whole(half), pl.BlockSpec((1, D), lambda i: (0, i))]
+        out_specs=[ANY for x in out_shapes]
+        + [ANY if last else whole(half)] * 2
+        + [pl.BlockSpec((1, D), lambda i: (0, i))]
         + ([whole((8, D))] if last else []),
         out_shape=list(out_shapes)
         + [shape(half, bf16), shape(half, bf16), shape((1, ff), f32)]
@@ -655,7 +677,8 @@
         scratch_shapes=[pltpu.VMEM((D, D), bf16), pltpu.VMEM((D, ff), bf16), pltpu.VMEM((ff, D), bf16)]
         + [wide] * (3 if last else 1)
         + [low, turned, wide, wide, low, low, pltpu.VMEM((D, D), bf16)]
-        + [pltpu.SemaphoreType.DMA((4 * nd + 4,))],
+        + [pltpu.SemaphoreType.DMA((4 * nd + 11,))]
+        + ([low, wide, turned, pltpu.VMEM(half, bf16), pltpu.VMEM(half, bf16)] if last else []),
         compiler_params=room(52 if last else 36),
         cost_estimate=pl.CostEstimate(flops=12 * WIN * D * ff, bytes_accessed=20 << 20, transcendentals=0),
         name="ffn_last" if last else "ffn_first",
@@ -833,23 +856,22 @@
     cuts = [(0, r, 0), (nf * r, r, r), (2 * nf * r, q, 2 * r)]
     more = [(nf * (2 * r + q), r, 2 * r + q)]
     m1, s2, k2, grad_t = tie((m1, s2, k2, grad_t))
+    got = flip(s2, 1, nd)
     p1 = pieces(nf, cuts, m1)
-    p1, grad_t = tie((p1, grad_t))
-    got = flip(s2, 1, nd)
-    p1 = [shift(p, k, nf) if k else p for k, p in enumerate(p1)]
-    grads = [attend_back(0, project_t, attended[0], grad_t, sums[0], segment_ids)]
-    got, k2, grads, grad_t, p1 = tie((got, k2, grads, grad_t, p1))
+    got, k2, p1, grad_t = tie((got, k2, p1, grad_t))
     t2 = [add(k2[m], got[m]) for m in range(nd // 2)]
     t2, grad_t = tie((t2, grad_t))
     m2 = meet_plane(t2, nd)
+    p1 = [shift(p, k, nf) if k else p for k, p in enumerate(p1)]
+    grads = [attend_back(0, project_t, attended[0], grad_t, sums[0], segment_ids)]
+    grads, grad_t, p1 = tie((grads, grad_t, p1))
     for g in range(1, GROUPS):
         grads.append(attend_back(g, project_t, attended[g], grad_t, sums[g], segment_ids))
-    m2, p1, grads = tie((m2, p1, grads))
-    p2 = pieces(nf, cuts + more, m2)
-    p2, grads = tie((p2, grads))
+    grads = [grads[g][j] for j in range(3) for g in range(GROUPS)]
+    m2, grads = tie((m2, grads))
+    send, keep = weight_grad(me, nd, normed_t, vecs, gvec, (gbe1, gbe2), turns, grads, w)
+    p2 = pieces(nf, cuts + more, after(m2, send))
     p2 = [shift(p, k, nf) if k else p for k, p in enumerate(p2)]
-    grads = [grads[g][j] for j in range(3) for g in range(GROUPS)]
-    send, keep = weight_grad(me, nd, normed_t, vecs, gvec, (gbe1, gbe2), turns, grads, w)
     totals = sum_cores(send, keep, nd)
     grads, totals = tie((grads, totals))
     met = meet_plane(totals, nd)

time: 284 us -> 276 us (0.972)
  waiting for transfers between devices: 40 us -> 35.5 us
  Pallas kernels: 164 us -> 160 us
    ppermute x33, waiting for transfers between devices: 26.8 us -> 21.9 us  [flip(): return lax.ppermute(value, 'dp', [(i, i ^ bit) for i in range(count)])]
    pallas_call x2, Pallas kernels: 58.3 us -> 54.9 us  [ffn_call(): pl.pallas_call(functools.partial(kernel, nd), grid=(ff // D,), in_specs=s...]
    unnamed x138 -> x130, local copies, waits for them, and re-layouts: 11.7 us -> 11.3 us
  transfers between devices with their start and end apart: 51 -> 51, of which waited for: 14 -> 13; matrix products, arithmetic and copies ran while one was open for 1% -> 1% of each run, Pallas kernels for 53% -> 54%
where the time goes in v1:
time: 276 us; the launch traced here: 275 us
  Pallas kernels  160 us (58%)
  starting transfers between devices  56.2 us (20%)
  waiting for transfers between devices  35.5 us (13%)
  local copies, waits for them, and re-layouts  14.3 us (5%)
  other arithmetic  7.2 us (3%)
    pallas_call x2, Pallas kernels, ffn_call(): pl.pallas_call(functools.partial(kernel, nd), grid=(ff // D,), in_specs=s...  54.9 us
    pallas_call x3, Pallas kernels, attend_back(): pl.pallas_call(attend_back_kernel, grid=(1,), in_specs=[head_rows(group +...  34 us
    ppermute x18, starting transfers between devices, shift(): lax.ppermute(value, 'fsdp', [(i, (i + step) % count) for i in range(count)])  31.3 us
    ppermute x33, starting transfers between devices, flip(): return lax.ppermute(value, 'dp', [(i, i ^ bit) for i in range(count)])  25 us
    ppermute x33, waiting for transfers between devices, flip(): return lax.ppermute(value, 'dp', [(i, i ^ bit) for i in range(count)])  21.9 us
    pallas_call x3, Pallas kernels, attend(): pl.pallas_call(attend_kernel, grid=(1,), in_specs=[head_rows(group + j *...  18.2 us
    ppermute x18, waiting for transfers between devices, shift(): lax.ppermute(value, 'fsdp', [(i, (i + step) % count) for i in range(count)])  13.6 us
    pallas_call x1, Pallas kernels, project_back(): pl.pallas_call(functools.partial(project_back_kernel, nd), grid=(1,), in_...  13.1 us
  transfers between devices with their start and end apart: 51, of which 13 were waited for; matrix products, arithmetic and copies ran while one was open for 1% of the time, Pallas kernels for 54%

profile of v1, /device:TPU:0, one launch (start us, length us, event | category | flops | bytes accessed | tf_op | source)
XLA Modules:
  0.0 275.0 jit_solution(6889083148391254664)
XLA Ops:
  0.7 3.1 %pack.1 = (bf16[24,2432]{1,0:T(8,128)(2,1)}, bf16[120,768]{1,0:T(8,128)(2,1)}, bf16[96,768]{1,0:T(8,128)(2,1)}) custom-call(bf16[24,2304]{1,0:T(8,128)(2,1)} %proj_ref.1, bf16[24,3072]{1,0:T(8,128)(2,1)} %exp_ref.1, bf16[96,768]{1,0:T(8,128)(2,1)} %red_ref.1, bf16[24,768]{1,0:T(8,128)(2,1)} %comb_ref.1, bf16[2,768,384]{2,1,0:T(8,128)(2,1)} %constant.32.clone.pick_ref, ...), custom_call_target="tpu_custom_call" | custom-call | bytes 3145728 | tf_op jit(solution)/shard_map/pack/pallas_call | solution.py:150
  3.7 3.1 %collective-permute-start = (bf16[24,2432]{1,0:T(8,128)(2,1)}, bf16[24,2432]{1,0:T(8,128)(2,1)S(1)}, u32[]{:S(2)}, u32[]{:S(2)}) collective-permute-start(bf16[24,2432]{1,0:T(8,128)(2,1)} %get-tuple-element.182.refs_0_), channel_id=1, source_target_pairs={{0,1},{1,2},{2,3},{3,0},{4,5},{5,6},{6,7},{7,4},{8,9},{9,10},{10,1... | collective-permute-start | bytes 350216 | tf_op jit(solution)/shard_map/ppermute | solution.py:46
  6.8 2.6 collective-permute-start.1
  9.4 1.3 collective-permute-start.2
  10.7 1.4 copy-done.27
  12.2 2.4 prepare.1
  14.6 1.7 copy-done.42
  16.2 1.1 copy-done.44
  17.5 1.6 collective-permute-start.3
  19.1 1.5 collective-permute-start.4
  21.1 2.9 %collective-permute-start.6 = (bf16[120,768]{1,0:T(8,128)(2,1)S(1)}, bf16[120,768]{1,0:T(8,128)(2,1)S(1)}, u32[]{:S(2)}, u32[]{:S(2)}) collective-permute-start(bf16[120,768]{1,0:T(8,128)(2,1)S(1)} %copy-done.15), channel_id=1, source_target_pairs={{0,1},{1,2},{2,3},{3,0},{4,5},{5,6},{6,7},{7,4},{8,9},{9,10},{10,1... | collective-permute-start | bytes 552968 | tf_op jit(solution)/shard_map/ppermute | solution.py:46
  24.0 1.6 collective-permute-start.7
  25.6 5.1 %collective-permute-done.6.refs_1_ = bf16[120,768]{1,0:T(8,128)(2,1)S(1)} collective-permute-done((bf16[120,768]{1,0:T(8,128)(2,1)S(1)}, bf16[120,768]{1,0:T(8,128)(2,1)S(1)}, u32[]{:S(2)}, u32[]{:S(2)}) %collective-permute-start.6) | collective-permute-done | bytes 184352 | tf_op jit(solution)/shard_map/ppermute | solution.py:46
  31.5 5.0 %collective-permute-done.7.refs_2_ = bf16[120,768]{1,0:T(8,128)(2,1)S(1)} collective-permute-done((bf16[120,768]{1,0:T(8,128)(2,1)S(1)}, bf16[120,768]{1,0:T(8,128)(2,1)S(1)}, u32[]{:S(2)}, u32[]{:S(2)}) %collective-permute-start.7) | collective-permute-done | bytes 184352 | tf_op jit(solution)/shard_map/ppermute | solution.py:46
  36.4 1.8 collective-permute-done.8.refs_3_
  38.3 3.1 %collective-permute-done.4.rest_4_.rest_13_ = bf16[96,2432]{1,0:T(8,128)(2,1)} collective-permute-done((bf16[96,2432]{1,0:T(8,128)(2,1)S(1)}, bf16[96,2432]{1,0:T(8,128)(2,1)}, u32[]{:S(2)}, u32[]{:S(2)}) %collective-permute-start.4) | collective-permute-done | bytes 466976 | tf_op jit(solution)/shard_map/ppermute | solution.py:42
  42.4 1.2 collective-permute-start.13
  44.0 1.5 collective-permute-start.14
  45.5 1.2 collective-permute-start.15
  46.7 1.3 copy-done.37
  48.0 1.9 copy-done.43
  49.9 7.5 %project.1 = (bf16[2304,1024]{1,0:T(8,128)(2,1)S(1)}, bf16[768,1024]{1,0:T(8,128)(2,1)S(1)}, f32[16,768]{1,0:T(8,128)S(1)}, f32[1,3072]{1,0:T(1,128)S(1)}) custom-call(s32[1]{0:T(128)} %bitcast.me_ref, f32[768,1024]{1,0:T(8,128)S(1)} %copy-done.43, bf16[2,768,384]{2,1,0:T(8,128)(2,1)S(1)} %copy-done.37, bf16[96,2432]{1,0:T(8,128)(2,1)S(1)} %line_up.3.rest_0_.rest_9_, ...), custom_call_target="tpu_custom_call" | custom-call | flops 3623878656 | bytes 12582912 | tf_op jit(solution)/shard_map/project/pallas_call | solution.py:287
  57.4 3.5 %collective-permute-start.16 = (bf16[96,768]{1,0:T(8,128)(2,1)S(1)}, bf16[96,768]{1,0:T(8,128)(2,1)S(1)}, u32[]{:S(2)}, u32[]{:S(2)}) collective-permute-start(bf16[96,768]{1,0:T(8,128)(2,1)S(1)} %copy-done.24), channel_id=1, source_target_pairs={{0,1},{1,2},{2,3},{3,0},{4,5},{5,6},{6,7},{7,4},{8,9},{9,10},{10,1... | collective-permute-start | bytes 442376 | tf_op jit(solution)/shard_map/ppermute | solution.py:46
  60.9 1.0 collective-permute-start.17
  61.9 6.1 %attend.3 = (bf16[256,1024]{1,0:T(8,128)(2,1)S(1)}, f32[8,1,1024]{2,1,0:T(1,128)S(1)}) custom-call(bf16[2304,1024]{1,0:T(8,128)(2,1)S(1)} %get-tuple-element.210.q_ref.k_ref.v_ref, bf16[2304,1024]{1,0:T(8,128)(2,1)S(1)} %get-tuple-element.210.q_ref.k_ref.v_ref, bf16[2304,1024]{1,0:T(8,128)(2,1)S(1)} %get-tuple-element.210.q_ref.k_ref.v_ref, ...), custom_call_target="tpu_custom_call" | custom-call | flops 7000000000 | bytes 3145728 | tf_op jit(solution)/shard_map/attend/pallas_call | solution.py:374
  68.0 2.9 %collective-permute-start.18 = (bf16[96,768]{1,0:T(8,128)(2,1)S(1)}, bf16[96,768]{1,0:T(8,128)(2,1)S(1)}, u32[]{:S(2)}, u32[]{:S(2)}) collective-permute-start(bf16[96,768]{1,0:T(8,128)(2,1)S(1)} %copy-done.24), channel_id=1, source_target_pairs={{0,3},{1,0},{2,1},{3,2},{4,7},{5,4},{6,5},{7,6},{8,11},{9,8},{10,9... | collective-permute-start | bytes 442376 | tf_op jit(solution)/shard_map/ppermute | solution.py:46
  70.9 6.1 %attend.4 = (bf16[256,1024]{1,0:T(8,128)(2,1)S(1)}, f32[8,1,1024]{2,1,0:T(1,128)S(1)}) custom-call(bf16[2304,1024]{1,0:T(8,128)(2,1)S(1)} %get-tuple-element.210.q_ref.k_ref.v_ref, bf16[2304,1024]{1,0:T(8,128)(2,1)S(1)} %get-tuple-element.210.q_ref.k_ref.v_ref, bf16[2304,1024]{1,0:T(8,128)(2,1)S(1)} %get-tuple-element.210.q_ref.k_ref.v_ref, ...), custom_call_target="tpu_custom_call" | custom-call | flops 7000000000 | bytes 3145728 | tf_op jit(solution)/shard_map/attend/pallas_call | solution.py:374
  77.0 1.3 collective-permute-done.14.rest_7_.rest_15_
  79.4 10.1 %line_up.5.rest_3_ = bf16[384,768]{1,0:T(8,128)(2,1)S(1)} custom-call(s32[1]{0:T(128)} %bitcast.1.me_ref, bf16[96,768]{1,0:T(8,128)(2,1)S(1)} %copy-done.24, bf16[96,768]{1,0:T(8,128)(2,1)S(1)} %collective-permute-done.16.refs_1_, bf16[96,768]{1,0:T(8,128)(2,1)S(1)} %collective-permute-done.17.refs_2_, bf16[96,768]{1,0:T(8,128)(2,1)S(1)} %collective-permute-done.18.refs_3_), custom_call_target="tpu_custom_call" | custom-call | bytes 4194304 | tf_op jit(solution)/shard_map/line_up/pallas_call | solution.py:71
  89.5 1.3 collective-permute-start.23
  90.8 6.1 %attend.5 = (bf16[256,1024]{1,0:T(8,128)(2,1)S(1)}, f32[8,1,1024]{2,1,0:T(1,128)S(1)}) custom-call(bf16[2304,1024]{1,0:T(8,128)(2,1)S(1)} %get-tuple-element.210.q_ref.k_ref.v_ref, bf16[2304,1024]{1,0:T(8,128)(2,1)S(1)} %get-tuple-element.210.q_ref.k_ref.v_ref, bf16[2304,1024]{1,0:T(8,128)(2,1)S(1)} %get-tuple-element.210.q_ref.k_ref.v_ref, ...), custom_call_target="tpu_custom_call" | custom-call | flops 7000000000 | bytes 3145728 | tf_op jit(solution)/shard_map/attend/pallas_call | solution.py:374
  96.9 0.9 collective-permute-start.24
  97.8 1.4 collective-permute-start.25
  99.3 25.4 %ffn_first.1 = (f32[1024,768]{1,0:T(8,128)}, bf16[1024,768]{1,0:T(8,128)(2,1)S(1)}, f32[1024,768]{1,0:T(8,128)}, f32[1024,768]{1,0:T(8,128)}, bf16[4,384,768]{2,...) custom-call(s32[1]{0:T(128)} %bitcast.me_ref, bf16[1024,768]{1,0:T(8,128)(2,1)S(1)} %copy-done.2, ...), custom_call_target="tpu_custom_call" | custom-call | flops 14495514624 | bytes 20971520 | tf_op jit(solution)/shard_map/ffn_first/pallas_call | solution.py:666
  125.0 4.5 %collective-permute-done.26 = bf16[4,384,768]{2,1,0:T(8,128)(2,1)S(1)} collective-permute-done((bf16[4,384,768]{2,1,0:T(8,128)(2,1)S(1)}, bf16[4,384,768]{2,1,0:T(8,128)(2,1)S(1)}, u32[]{:S(2)}, u32[]{:S(2)}) %collective-permute-start.26) | collective-permute-done | bytes 2359328 | tf_op jit(solution)/shard_map/ppermute | solution.py:42
  131.2 1.3 collective-permute-start.31
  132.5 0.9 collective-permute-start.32
  133.4 1.4 collective-permute-start.33
  134.8 0.8 copy-done.61
  135.8 29.6 %ffn_last.1 = (bf16[1024,768]{1,0:T(8,128)(2,1)}, f32[1024,768]{1,0:T(8,128)}, bf16[768,1024]{1,0:T(8,128)(2,1)}, bf16[4,480,768]{2,1,0:T(8,128)(2,1)}, bf16[4,4...) custom-call(s32[1]{0:T(128)} %bitcast.me_ref, bf16[1024,768]{1,0:T(8,128)(2,1)} %cot_ref.4, ...), custom_call_target="tpu_custom_call" | custom-call | flops 14495514624 | bytes 20971520 | tf_op jit(solution)/shard_map/ffn_last/pallas_call | solution.py:666
  166.6 4.4 %collective-permute-done.34 = bf16[4,480,768]{2,1,0:T(8,128)(2,1)S(1)} collective-permute-done((bf16[4,480,768]{2,1,0:T(8,128)(2,1)}, bf16[4,480,768]{2,1,0:T(8,128)(2,1)S(1)}, u32[]{:S(2)}, u32[]{:S(2)}) %collective-permute-start.34) | collective-permute-done | bytes 2949152 | tf_op jit(solution)/shard_map/ppermute | solution.py:42
  171.1 2.7 fusion.3
  173.7 3.1 %collective-permute-start.38 = (bf16[96,768]{1,0:T(8,128)(2,1)S(1)}, bf16[96,768]{1,0:T(8,128)(2,1)S(1)}, u32[]{:S(2)}, u32[]{:S(2)}) collective-permute-start(bf16[96,768]{1,0:T(8,128)(2,1)S(1)} %get-tuple-element.268), channel_id=1, source_target_pairs={{0,1},{1,2},{2,3},{3,0},{4,5},{5,6},{6,7},{7,4},{8,9},{9,10},{10,1... | collective-permute-start | bytes 442376 | tf_op jit(solution)/shard_map/ppermute | solution.py:46
  177.4 2.4 collective-permute-start.40
  179.7 1.2 collective-permute-start.35
  181.0 1.6 collective-permute-start.36
  182.6 11.1 %attend_back.3 = (bf16[256,1024]{1,0:T(8,128)(2,1)S(1)}, bf16[256,1024]{1,0:T(8,128)(2,1)S(1)}, bf16[256,1024]{1,0:T(8,128)(2,1)S(1)}) custom-call(bf16[2304,1024]{1,0:T(8,128)(2,1)S(1)} %bitcast.29, bf16[2304,1024]{1,0:T(8,128)(2,1)S(1)} %bitcast.29, bf16[2304,1024]{1,0:T(8,128)(2,1)S(1)} %bitcast.29, bf16[256,1024]{1,0:T(8,128)(2,1)S(1)} %copy-done.50, ...), custom_call_target="tpu_custom_call" | custom-call | flops 14000000000 | bytes 5242880 | tf_op jit(solution)/shard_map/attend_back/pallas_call | solution.py:460
  196.5 11.3 %attend_back.5 = (bf16[256,1024]{1,0:T(8,128)(2,1)S(1)}, bf16[256,1024]{1,0:T(8,128)(2,1)S(1)}, bf16[256,1024]{1,0:T(8,128)(2,1)S(1)}) custom-call(bf16[2304,1024]{1,0:T(8,128)(2,1)S(1)} %bitcast.29, bf16[2304,1024]{1,0:T(8,128)(2,1)S(1)} %bitcast.29, bf16[2304,1024]{1,0:T(8,128)(2,1)S(1)} %bitcast.29, bf16[256,1024]{1,0:T(8,128)(2,1)S(1)} %copy-done.53, ...), custom_call_target="tpu_custom_call" | custom-call | flops 14000000000 | bytes 5242880 | tf_op jit(solution)/shard_map/attend_back/pallas_call | solution.py:460
  207.9 11.5 %attend_back.4 = (bf16[256,1024]{1,0:T(8,128)(2,1)S(1)}, bf16[256,1024]{1,0:T(8,128)(2,1)S(1)}, bf16[256,1024]{1,0:T(8,128)(2,1)S(1)}) custom-call(bf16[2304,1024]{1,0:T(8,128)(2,1)S(1)} %bitcast.29, bf16[2304,1024]{1,0:T(8,128)(2,1)S(1)} %bitcast.29, bf16[2304,1024]{1,0:T(8,128)(2,1)S(1)} %bitcast.29, bf16[256,1024]{1,0:T(8,128)(2,1)S(1)} %copy-done.47, ...), custom_call_target="tpu_custom_call" | custom-call | flops 14000000000 | bytes 5242880 | tf_op jit(solution)/shard_map/attend_back/pallas_call | solution.py:460
  219.6 8.8 %weight_grad.1 = (bf16[4,96,2432]{2,1,0:T(8,128)(2,1)S(1)}, bf16[4,96,2432]{2,1,0:T(8,128)(2,1)S(1)}) custom-call(s32[1]{0:T(128)} %bitcast.me_ref, bf16[768,1024]{1,0:T(8,128)(2,1)S(1)} %copy-done.40, f32[16,768]{1,0:T(8,128)S(1)} %get-tuple-element.197.vec_ref, f32[8,768]{1,0:T(8,128)S(1)} %get-tuple-element.293.gv_ref, ...), custom_call_target="tpu_custom_call" | custom-call | flops 3623878656 | bytes 10485760 | tf_op jit(solution)/shard_map/weight_grad/pallas_call | solution.py:753
  229.2 3.2 %collective-permute-done.41 = bf16[4,96,2432]{2,1,0:T(8,128)(2,1)S(1)} collective-permute-done((bf16[4,96,2432]{2,1,0:T(8,128)(2,1)S(1)}, bf16[4,96,2432]{2,1,0:T(8,128)(2,1)S(1)}, u32[]{:S(2)}, u32[]{:S(2)}) %collective-permute-start.41) | collective-permute-done | bytes 1867808 | tf_op jit(solution)/shard_map/ppermute | solution.py:42
  232.4 1.4 fusion.11
  233.7 1.2 collective-permute-start.42
  234.9 1.6 collective-permute-start.43
  238.0 1.5 collective-permute-start.47
  239.5 13.1 %project_back.1 = f32[1024,768]{1,0:T(8,128)} custom-call(s32[1]{0:T(128)} %bitcast.me_ref, bf16[1024,768]{1,0:T(8,128)(2,1)} %x_ref.4, f32[1024,768]{1,0:T(8,128)} %get-tuple-element.236.gm_ref, f32[16,768]{1,0:T(8,128)} %copy-done.26, bf16[256,1024]{1,0:T(8,128)(2,1)} %copy-done.5, bf16[256,1024]{1,0:T(8,128)(2,1)} %copy-done.11, ...), custom_call_target="tpu_custom_call" | custom-call | flops 3623878656 | bytes 20971520 | tf_op jit(solution)/shard_map/project_back/pallas_call | solution.py:794
  252.7 4.1 %collective-permute-done.43 = bf16[96,2432]{1,0:T(8,128)(2,1)} collective-permute-done((bf16[96,2432]{1,0:T(8,128)(2,1)}, bf16[96,2432]{1,0:T(8,128)(2,1)}, u32[]{:S(2)}, u32[]{:S(2)}) %collective-permute-start.43) | collective-permute-done | bytes 466976 | tf_op jit(solution)/shard_map/ppermute | solution.py:42
  256.8 0.9 collective-permute-done.44
  257.7 1.6 add_convert_fusion.8
  260.0 2.2 collective-permute-start.49
  262.2 1.6 collective-permute-start.50
  263.9 6.5 %finish.1 = (f32[24,3072]{1,0:T(8,128)}, f32[96,768]{1,0:T(8,128)}, f32[24,768]{1,0:T(8,128)}) custom-call(bf16[2,768,384]{2,1,0:T(8,128)(2,1)S(1)} %copy-done, bf16[96,768]{1,0:T(8,128)(2,1)S(1)} %copy-done.17, bf16[96,768]{1,0:T(8,128)(2,1)S(1)} %copy-done.19, bf16[96,768]{1,0:T(8,128)(2,1)S(1)} %copy-done.21, bf16[96,768]{1,0:T(8,128)(2,1)S(1)} %copy-done.23, ...), custom_call_target="tpu_custom_call" | custom-call | bytes 3145728 | tf_op jit(solution)/shard_map/finish/pallas_call | solution.py:206
  270.3 1.2 collective-permute-done.49
  271.6 1.0 convert_add_fusion
  (199 shorter events, 15.7 us)
Async XLA Ops:
  3.7 13.7 %collective-permute-start = (bf16[24,2432]{1,0:T(8,128)(2,1)}, bf16[24,2432]{1,0:T(8,128)(2,1)S(1)}, u32[]{:S(2)}, u32[]{:S(2)}) collective-permute-start(bf16[24,2432]{1,0:T(8,128)(2,1)} %get-tuple-element.182.refs_0_), channel_id=1, source_target_pairs={{0,1},{1,2},{2,3},{3,0},{4,5},{5,6},{6,7},{7,4},{8,9},{9,10},{10,1... | collective-permute-start | bytes 350216 | tf_op jit(solution)/shard_map/ppermute | solution.py:46
  6.8 10.6 %collective-permute-start.1 = (bf16[24,2432]{1,0:T(8,128)(2,1)}, bf16[24,2432]{1,0:T(8,128)(2,1)S(1)}, u32[]{:S(2)}, u32[]{:S(2)}) collective-permute-start(bf16[24,2432]{1,0:T(8,128)(2,1)} %get-tuple-element.182.refs_0_), channel_id=1, source_target_pairs={{0,2},{1,3},{2,0},{3,1},{4,6},{5,7},{6,4},{7,5},{8,10},{9,11},{10,... | collective-permute-start | bytes 350216 | tf_op jit(solution)/shard_map/ppermute | solution.py:46
  9.4 8.0 %collective-permute-start.2 = (bf16[24,2432]{1,0:T(8,128)(2,1)}, bf16[24,2432]{1,0:T(8,128)(2,1)S(1)}, u32[]{:S(2)}, u32[]{:S(2)}) collective-permute-start(bf16[24,2432]{1,0:T(8,128)(2,1)} %get-tuple-element.182.refs_0_), channel_id=1, source_target_pairs={{0,3},{1,0},{2,1},{3,2},{4,7},{5,4},{6,5},{7,6},{8,11},{9,8},{10,9... | collective-permute-start | bytes 350216 | tf_op jit(solution)/shard_map/ppermute | solution.py:46
  17.5 202.0 %copy-start.1 = (bf16[96,2432]{1,0:T(8,128)(2,1)}, bf16[96,2432]{1,0:T(8,128)(2,1)S(1)}, u32[]{:S(2)}) copy-start(bf16[96,2432]{1,0:T(8,128)(2,1)S(1)} %line_up.3.rest_0_.rest_9_) | copy-start | bytes 1400836
  17.5 20.8 %collective-permute-start.3 = (bf16[96,2432]{1,0:T(8,128)(2,1)S(1)}, bf16[96,2432]{1,0:T(8,128)(2,1)S(1)}, u32[]{:S(2)}, u32[]{:S(2)}) collective-permute-start(bf16[96,2432]{1,0:T(8,128)(2,1)S(1)} %line_up.3.rest_0_.rest_9_), channel_id=1, source_target_pairs={{0,8},{4,12},{8,0},{12,4},{16,24},{20,28},{24,16},{28,20},{1,9},{5... | collective-permute-start | bytes 1400840 | tf_op jit(solution)/shard_map/ppermute | solution.py:42
  19.1 22.3 %collective-permute-start.4 = (bf16[96,2432]{1,0:T(8,128)(2,1)S(1)}, bf16[96,2432]{1,0:T(8,128)(2,1)}, u32[]{:S(2)}, u32[]{:S(2)}) collective-permute-start(bf16[96,2432]{1,0:T(8,128)(2,1)S(1)} %line_up.3.rest_0_.rest_9_), channel_id=1, source_target_pairs={{0,16},{4,20},{8,24},{12,28},{16,0},{20,4},{24,8},{28,12},{1,17},{... | collective-permute-start | bytes 1400840 | tf_op jit(solution)/shard_map/ppermute | solution.py:42
  20.6 20.8 %collective-permute-start.5 = (bf16[96,2432]{1,0:T(8,128)(2,1)S(1)}, bf16[96,2432]{1,0:T(8,128)(2,1)}, u32[]{:S(2)}, u32[]{:S(2)}) collective-permute-start(bf16[96,2432]{1,0:T(8,128)(2,1)S(1)} %line_up.3.rest_0_.rest_9_), channel_id=1, source_target_pairs={{0,24},{4,28},{8,16},{12,20},{16,8},{20,12},{24,0},{28,4},{1,25},{... | collective-permute-start | bytes 1400840 | tf_op jit(solution)/shard_map/ppermute | solution.py:42
  21.1 9.6 %collective-permute-start.6 = (bf16[120,768]{1,0:T(8,128)(2,1)S(1)}, bf16[120,768]{1,0:T(8,128)(2,1)S(1)}, u32[]{:S(2)}, u32[]{:S(2)}) collective-permute-start(bf16[120,768]{1,0:T(8,128)(2,1)S(1)} %copy-done.15), channel_id=1, source_target_pairs={{0,1},{1,2},{2,3},{3,0},{4,5},{5,6},{6,7},{7,4},{8,9},{9,10},{10,1... | collective-permute-start | bytes 552968 | tf_op jit(solution)/shard_map/ppermute | solution.py:46
  24.0 12.5 %collective-permute-start.7 = (bf16[120,768]{1,0:T(8,128)(2,1)S(1)}, bf16[120,768]{1,0:T(8,128)(2,1)S(1)}, u32[]{:S(2)}, u32[]{:S(2)}) collective-permute-start(bf16[120,768]{1,0:T(8,128)(2,1)S(1)} %copy-done.15), channel_id=1, source_target_pairs={{0,2},{1,3},{2,0},{3,1},{4,6},{5,7},{6,4},{7,5},{8,10},{9,11},{10,... | collective-permute-start | bytes 552968 | tf_op jit(solution)/shard_map/ppermute | solution.py:46
  30.7 7.5 %collective-permute-start.8 = (bf16[120,768]{1,0:T(8,128)(2,1)S(1)}, bf16[120,768]{1,0:T(8,128)(2,1)S(1)}, u32[]{:S(2)}, u32[]{:S(2)}) collective-permute-start(bf16[120,768]{1,0:T(8,128)(2,1)S(1)} %copy-done.15), channel_id=1, source_target_pairs={{0,3},{1,0},{2,1},{3,2},{4,7},{5,4},{6,5},{7,6},{8,11},{9,8},{10,9... | collective-permute-start | bytes 552968 | tf_op jit(solution)/shard_map/ppermute | solution.py:46
  38.3 61.0 %copy-start.3 = (bf16[480,768]{1,0:T(8,128)(2,1)}, bf16[480,768]{1,0:T(8,128)(2,1)S(1)}, u32[]{:S(2)}) copy-start(bf16[480,768]{1,0:T(8,128)(2,1)S(1)} %line_up.4.rest_3_.rest_11_) | copy-start | bytes 2211844
  38.3 181.1 %copy-start.14 = (bf16[96,2432]{1,0:T(8,128)(2,1)}, bf16[96,2432]{1,0:T(8,128)(2,1)S(1)}, u32[]{:S(2)}) copy-start(bf16[96,2432]{1,0:T(8,128)(2,1)S(1)} %collective-permute-done.3.rest_2_.rest_11_) | copy-start | bytes 1400836
  41.4 2.6 collective-permute-start.10
  41.4 4.1 %collective-permute-start.11 = (bf16[96,2432]{1,0:T(8,128)(2,1)}, bf16[96,2432]{1,0:T(8,128)(2,1)}, u32[]{:S(2)}, u32[]{:S(2)}) collective-permute-start(bf16[96,2432]{1,0:T(8,128)(2,1)} %collective-permute-done.4.rest_4_.rest_13_), channel_id=1, source_target_pairs={{0,4},{4,0},{8,12},{12,8},{16,20},{20,16},{24,28},{28,24},{1,5},{5... | collective-permute-start | bytes 1400840 | tf_op jit(solution)/shard_map/ppermute | solution.py:42
  41.9 4.8 %collective-permute-start.12 = (bf16[96,2432]{1,0:T(8,128)(2,1)}, bf16[96,2432]{1,0:T(8,128)(2,1)}, u32[]{:S(2)}, u32[]{:S(2)}) collective-permute-start(bf16[96,2432]{1,0:T(8,128)(2,1)} %collective-permute-done.5.rest_6_.rest_15_), channel_id=1, source_target_pairs={{0,4},{4,0},{8,12},{12,8},{16,20},{20,16},{24,28},{28,24},{1,5},{5... | collective-permute-start | bytes 1400840 | tf_op jit(solution)/shard_map/ppermute | solution.py:42
  41.9 4.8 %collective-permute-start.9 = (bf16[96,2432]{1,0:T(8,128)(2,1)S(1)}, bf16[96,2432]{1,0:T(8,128)(2,1)}, u32[]{:S(2)}, u32[]{:S(2)}) collective-permute-start(bf16[96,2432]{1,0:T(8,128)(2,1)S(1)} %line_up.3.rest_0_.rest_9_), channel_id=1, source_target_pairs={{0,4},{4,0},{8,12},{12,8},{16,20},{20,16},{24,28},{28,24},{1,5},{5... | collective-permute-start | bytes 1400840 | tf_op jit(solution)/shard_map/ppermute | solution.py:42
  42.4 34.6 %collective-permute-start.13 = (bf16[480,768]{1,0:T(8,128)(2,1)S(1)}, bf16[480,768]{1,0:T(8,128)(2,1)S(1)}, u32[]{:S(2)}, u32[]{:S(2)}) collective-permute-start(bf16[480,768]{1,0:T(8,128)(2,1)S(1)} %line_up.4.rest_3_.rest_11_), channel_id=1, source_target_pairs={{0,8},{4,12},{8,0},{12,4},{16,24},{20,28},{24,16},{28,20},{1,9},{5... | collective-permute-start | bytes 2211848 | tf_op jit(solution)/shard_map/ppermute | solution.py:42
  44.0 34.3 %collective-permute-start.14 = (bf16[480,768]{1,0:T(8,128)(2,1)S(1)}, bf16[480,768]{1,0:T(8,128)(2,1)S(1)}, u32[]{:S(2)}, u32[]{:S(2)}) collective-permute-start(bf16[480,768]{1,0:T(8,128)(2,1)S(1)} %line_up.4.rest_3_.rest_11_), channel_id=1, source_target_pairs={{0,16},{4,20},{8,24},{12,28},{16,0},{20,4},{24,8},{28,12},{1,17},{... | collective-permute-start | bytes 2211848 | tf_op jit(solution)/shard_map/ppermute | solution.py:42
  45.5 32.8 %collective-permute-start.15 = (bf16[480,768]{1,0:T(8,128)(2,1)S(1)}, bf16[480,768]{1,0:T(8,128)(2,1)S(1)}, u32[]{:S(2)}, u32[]{:S(2)}) collective-permute-start(bf16[480,768]{1,0:T(8,128)(2,1)S(1)} %line_up.4.rest_3_.rest_11_), channel_id=1, source_target_pairs={{0,24},{4,28},{8,16},{12,20},{16,8},{20,12},{24,0},{28,4},{1,25},{... | collective-permute-start | bytes 2211848 | tf_op jit(solution)/shard_map/ppermute | solution.py:42
  57.4 33.4 %copy-start.41 = (bf16[2304,1024]{1,0:T(8,128)(2,1)}, bf16[2304,1024]{1,0:T(8,128)(2,1)S(1)}, u32[]{:S(2)}) copy-start(bf16[2304,1024]{1,0:T(8,128)(2,1)S(1)} %get-tuple-element.210.q_ref.k_ref.v_ref) | copy-start | bytes 14155780
  57.4 162.1 %copy-start.26 = (f32[16,768]{1,0:T(8,128)}, f32[16,768]{1,0:T(8,128)S(1)}, u32[]{:S(2)}) copy-start(f32[16,768]{1,0:T(8,128)S(1)} %get-tuple-element.197.vec_ref) | copy-start | bytes 147460
  57.4 10.6 %collective-permute-start.16 = (bf16[96,768]{1,0:T(8,128)(2,1)S(1)}, bf16[96,768]{1,0:T(8,128)(2,1)S(1)}, u32[]{:S(2)}, u32[]{:S(2)}) collective-permute-start(bf16[96,768]{1,0:T(8,128)(2,1)S(1)} %copy-done.24), channel_id=1, source_target_pairs={{0,1},{1,2},{2,3},{3,0},{4,5},{5,6},{6,7},{7,4},{8,9},{9,10},{10,1... | collective-permute-start | bytes 442376 | tf_op jit(solution)/shard_map/ppermute | solution.py:46
  60.9 16.1 %collective-permute-start.17 = (bf16[96,768]{1,0:T(8,128)(2,1)S(1)}, bf16[96,768]{1,0:T(8,128)(2,1)S(1)}, u32[]{:S(2)}, u32[]{:S(2)}) collective-permute-start(bf16[96,768]{1,0:T(8,128)(2,1)S(1)} %copy-done.24), channel_id=1, source_target_pairs={{0,2},{1,3},{2,0},{3,1},{4,6},{5,7},{6,4},{7,5},{8,10},{9,11},{10,... | collective-permute-start | bytes 442376 | tf_op jit(solution)/shard_map/ppermute | solution.py:46
  68.0 31.3 %copy-start.48 = (bf16[256,1024]{1,0:T(8,128)(2,1)}, bf16[256,1024]{1,0:T(8,128)(2,1)S(1)}, u32[]{:S(2)}) copy-start(bf16[256,1024]{1,0:T(8,128)(2,1)S(1)} %get-tuple-element.200.rest_0_.o_ref) | copy-start | bytes 1572868
  68.0 9.0 %collective-permute-start.18 = (bf16[96,768]{1,0:T(8,128)(2,1)S(1)}, bf16[96,768]{1,0:T(8,128)(2,1)S(1)}, u32[]{:S(2)}, u32[]{:S(2)}) collective-permute-start(bf16[96,768]{1,0:T(8,128)(2,1)S(1)} %copy-done.24), channel_id=1, source_target_pairs={{0,3},{1,0},{2,1},{3,2},{4,7},{5,4},{6,5},{7,6},{8,11},{9,8},{10,9... | collective-permute-start | bytes 442376 | tf_op jit(solution)/shard_map/ppermute | solution.py:46
  78.3 18.6 %collective-permute-start.19 = (bf16[480,768]{1,0:T(8,128)(2,1)S(1)}, bf16[480,768]{1,0:T(8,128)(2,1)S(1)}, u32[]{:S(2)}, u32[]{:S(2)}) collective-permute-start(bf16[480,768]{1,0:T(8,128)(2,1)S(1)} %line_up.4.rest_3_.rest_11_), channel_id=1, source_target_pairs={{0,4},{4,0},{8,12},{12,8},{16,20},{20,16},{24,28},{28,24},{1,5},{5... | collective-permute-start | bytes 2211848 | tf_op jit(solution)/shard_map/ppermute | solution.py:42
  78.4 19.4 %collective-permute-start.20 = (bf16[480,768]{1,0:T(8,128)(2,1)S(1)}, bf16[480,768]{1,0:T(8,128)(2,1)S(1)}, u32[]{:S(2)}, u32[]{:S(2)}) collective-permute-start(bf16[480,768]{1,0:T(8,128)(2,1)S(1)} %collective-permute-done.13.rest_5_.rest_13_), channel_id=1, source_target_pairs={{0,4},{4,0},{8,12},{12,8},{16,20},{20,16},{24,28},{28,24},{1,5},{5... | collective-permute-start | bytes 2211848 | tf_op jit(solution)/shard_map/ppermute | solution.py:42
  78.9 20.3 %collective-permute-start.21 = (bf16[480,768]{1,0:T(8,128)(2,1)S(1)}, bf16[480,768]{1,0:T(8,128)(2,1)S(1)}, u32[]{:S(2)}, u32[]{:S(2)}) collective-permute-start(bf16[480,768]{1,0:T(8,128)(2,1)S(1)} %collective-permute-done.14.rest_7_.rest_15_), channel_id=1, source_target_pairs={{0,4},{4,0},{8,12},{12,8},{16,20},{20,16},{24,28},{28,24},{1,5},{5... | collective-permute-start | bytes 2211848 | tf_op jit(solution)/shard_map/ppermute | solution.py:42
  79.0 20.3 %collective-permute-start.22 = (bf16[480,768]{1,0:T(8,128)(2,1)S(1)}, bf16[480,768]{1,0:T(8,128)(2,1)S(1)}, u32[]{:S(2)}, u32[]{:S(2)}) collective-permute-start(bf16[480,768]{1,0:T(8,128)(2,1)S(1)} %collective-permute-done.15.rest_9_.rest_17_), channel_id=1, source_target_pairs={{0,4},{4,0},{8,12},{12,8},{16,20},{20,16},{24,28},{28,24},{1,5},{5... | collective-permute-start | bytes 2211848 | tf_op jit(solution)/shard_map/ppermute | solution.py:42
  89.5 40.0 %copy-start.4 = (bf16[384,768]{1,0:T(8,128)(2,1)}, bf16[384,768]{1,0:T(8,128)(2,1)S(1)}, u32[]{:S(2)}) copy-start(bf16[384,768]{1,0:T(8,128)(2,1)S(1)} %line_up.5.rest_3_) | copy-start | bytes 1769476
  89.5 35.3 %collective-permute-start.23 = (bf16[384,768]{1,0:T(8,128)(2,1)S(1)}, bf16[384,768]{1,0:T(8,128)(2,1)S(1)}, u32[]{:S(2)}, u32[]{:S(2)}) collective-permute-start(bf16[384,768]{1,0:T(8,128)(2,1)S(1)} %line_up.5.rest_3_), channel_id=1, source_target_pairs={{0,8},{4,12},{8,0},{12,4},{16,24},{20,28},{24,16},{28,20},{1,9},{5... | collective-permute-start | bytes 1769480 | tf_op jit(solution)/shard_map/ppermute | solution.py:42
  96.9 27.8 %copy-start.51 = (bf16[256,1024]{1,0:T(8,128)(2,1)}, bf16[256,1024]{1,0:T(8,128)(2,1)S(1)}, u32[]{:S(2)}) copy-start(bf16[256,1024]{1,0:T(8,128)(2,1)S(1)} %get-tuple-element.211.rest_2_.o_ref) | copy-start | bytes 1572868
  96.9 27.8 %copy-start.32 = (bf16[480,768]{1,0:T(8,128)(2,1)}, bf16[480,768]{1,0:T(8,128)(2,1)S(1)}, u32[]{:S(2)}) copy-start(bf16[480,768]{1,0:T(8,128)(2,1)S(1)} %collective-permute-done.19.rest_4_.rest_12_) | copy-start | bytes 2211844
  96.9 27.9 %collective-permute-start.24 = (bf16[384,768]{1,0:T(8,128)(2,1)S(1)}, bf16[384,768]{1,0:T(8,128)(2,1)S(1)}, u32[]{:S(2)}, u32[]{:S(2)}) collective-permute-start(bf16[384,768]{1,0:T(8,128)(2,1)S(1)} %line_up.5.rest_3_), channel_id=1, source_target_pairs={{0,16},{4,20},{8,24},{12,28},{16,0},{20,4},{24,8},{28,12},{1,17},{... | collective-permute-start | bytes 1769480 | tf_op jit(solution)/shard_map/ppermute | solution.py:42
  97.8 26.9 %copy-start.33 = (bf16[480,768]{1,0:T(8,128)(2,1)}, bf16[480,768]{1,0:T(8,128)(2,1)S(1)}, u32[]{:S(2)}) copy-start(bf16[480,768]{1,0:T(8,128)(2,1)S(1)} %collective-permute-done.20.rest_6_.rest_14_) | copy-start | bytes 2211844
  97.8 27.0 %collective-permute-start.25 = (bf16[384,768]{1,0:T(8,128)(2,1)S(1)}, bf16[384,768]{1,0:T(8,128)(2,1)S(1)}, u32[]{:S(2)}, u32[]{:S(2)}) collective-permute-start(bf16[384,768]{1,0:T(8,128)(2,1)S(1)} %line_up.5.rest_3_), channel_id=1, source_target_pairs={{0,24},{4,28},{8,16},{12,20},{16,8},{20,12},{24,0},{28,4},{1,25},{... | collective-permute-start | bytes 1769480 | tf_op jit(solution)/shard_map/ppermute | solution.py:42
  124.9 4.6 %collective-permute-start.26 = (bf16[4,384,768]{2,1,0:T(8,128)(2,1)S(1)}, bf16[4,384,768]{2,1,0:T(8,128)(2,1)S(1)}, u32[]{:S(2)}, u32[]{:S(2)}) collective-permute-start(bf16[4,384,768]{2,1,0:T(8,128)(2,1)S(1)} %get-tuple-element.220), channel_id=1, source_target_pairs={{0,4},{4,0},{8,12},{12,8},{16,20},{20,16},{24,28},{28,24},{1,5},{5... | collective-permute-start | bytes 7077896 | tf_op jit(solution)/shard_map/ppermute | solution.py:42
  129.5 3.0 %collective-permute-start.27 = (bf16[384,768]{1,0:T(8,128)(2,1)S(1)}, bf16[384,768]{1,0:T(8,128)(2,1)S(1)}, u32[]{:S(2)}, u32[]{:S(2)}) collective-permute-start(bf16[384,768]{1,0:T(8,128)(2,1)S(1)} %line_up.5.rest_3_), channel_id=1, source_target_pairs={{0,4},{4,0},{8,12},{12,8},{16,20},{20,16},{24,28},{28,24},{1,5},{5... | collective-permute-start | bytes 1769480 | tf_op jit(solution)/shard_map/ppermute | solution.py:42
  129.6 3.7 %collective-permute-start.28 = (bf16[384,768]{1,0:T(8,128)(2,1)S(1)}, bf16[384,768]{1,0:T(8,128)(2,1)S(1)}, u32[]{:S(2)}, u32[]{:S(2)}) collective-permute-start(bf16[384,768]{1,0:T(8,128)(2,1)S(1)} %collective-permute-done.23.rest_5_), channel_id=1, source_target_pairs={{0,4},{4,0},{8,12},{12,8},{16,20},{20,16},{24,28},{28,24},{1,5},{5... | collective-permute-start | bytes 1769480 | tf_op jit(solution)/shard_map/ppermute | solution.py:42
  130.0 4.7 %collective-permute-start.29 = (bf16[384,768]{1,0:T(8,128)(2,1)S(1)}, bf16[384,768]{1,0:T(8,128)(2,1)S(1)}, u32[]{:S(2)}, u32[]{:S(2)}) collective-permute-start(bf16[384,768]{1,0:T(8,128)(2,1)S(1)} %collective-permute-done.24.rest_7_), channel_id=1, source_target_pairs={{0,4},{4,0},{8,12},{12,8},{16,20},{20,16},{24,28},{28,24},{1,5},{5... | collective-permute-start | bytes 1769480 | tf_op jit(solution)/shard_map/ppermute | solution.py:42
  130.1 4.6 %collective-permute-start.30 = (bf16[384,768]{1,0:T(8,128)(2,1)S(1)}, bf16[384,768]{1,0:T(8,128)(2,1)S(1)}, u32[]{:S(2)}, u32[]{:S(2)}) collective-permute-start(bf16[384,768]{1,0:T(8,128)(2,1)S(1)} %collective-permute-done.25.rest_9_), channel_id=1, source_target_pairs={{0,4},{4,0},{8,12},{12,8},{16,20},{20,16},{24,28},{28,24},{1,5},{5... | collective-permute-start | bytes 1769480 | tf_op jit(solution)/shard_map/ppermute | solution.py:42
  131.2 34.2 %collective-permute-start.31 = (bf16[384,768]{1,0:T(8,128)(2,1)S(1)}, bf16[384,768]{1,0:T(8,128)(2,1)S(1)}, u32[]{:S(2)}, u32[]{:S(2)}) collective-permute-start(bf16[384,768]{1,0:T(8,128)(2,1)S(1)} %get-tuple-element.238), channel_id=1, source_target_pairs={{0,8},{4,12},{8,0},{12,4},{16,24},{20,28},{24,16},{28,20},{1,9},{5... | collective-permute-start | bytes 1769480 | tf_op jit(solution)/shard_map/ppermute | solution.py:42
  132.5 32.9 %collective-permute-start.32 = (bf16[384,768]{1,0:T(8,128)(2,1)S(1)}, bf16[384,768]{1,0:T(8,128)(2,1)S(1)}, u32[]{:S(2)}, u32[]{:S(2)}) collective-permute-start(bf16[384,768]{1,0:T(8,128)(2,1)S(1)} %get-tuple-element.239), channel_id=1, source_target_pairs={{0,16},{4,20},{8,24},{12,28},{16,0},{20,4},{24,8},{28,12},{1,17},{... | collective-permute-start | bytes 1769480 | tf_op jit(solution)/shard_map/ppermute | solution.py:42
  133.4 32.0 %collective-permute-start.33 = (bf16[384,768]{1,0:T(8,128)(2,1)S(1)}, bf16[384,768]{1,0:T(8,128)(2,1)S(1)}, u32[]{:S(2)}, u32[]{:S(2)}) collective-permute-start(bf16[384,768]{1,0:T(8,128)(2,1)S(1)} %get-tuple-element.240), channel_id=1, source_target_pairs={{0,24},{4,28},{8,16},{12,20},{16,8},{20,12},{24,0},{28,4},{1,25},{... | collective-permute-start | bytes 1769480 | tf_op jit(solution)/shard_map/ppermute | solution.py:42
  165.4 5.7 %collective-permute-start.34 = (bf16[4,480,768]{2,1,0:T(8,128)(2,1)}, bf16[4,480,768]{2,1,0:T(8,128)(2,1)S(1)}, u32[]{:S(2)}, u32[]{:S(2)}) collective-permute-start(bf16[4,480,768]{2,1,0:T(8,128)(2,1)} %get-tuple-element.244), channel_id=1, source_target_pairs={{0,4},{4,0},{8,12},{12,8},{16,20},{20,16},{24,28},{28,24},{1,5},{5... | collective-permute-start | bytes 8847368 | tf_op jit(solution)/shard_map/ppermute | solution.py:42
  173.7 20.0 %collective-permute-start.38 = (bf16[96,768]{1,0:T(8,128)(2,1)S(1)}, bf16[96,768]{1,0:T(8,128)(2,1)S(1)}, u32[]{:S(2)}, u32[]{:S(2)}) collective-permute-start(bf16[96,768]{1,0:T(8,128)(2,1)S(1)} %get-tuple-element.268), channel_id=1, source_target_pairs={{0,1},{1,2},{2,3},{3,0},{4,5},{5,6},{6,7},{7,4},{8,9},{9,10},{10,1... | collective-permute-start | bytes 442376 | tf_op jit(solution)/shard_map/ppermute | solution.py:46
  176.9 18.3 %collective-permute-start.39 = (bf16[96,768]{1,0:T(8,128)(2,1)S(1)}, bf16[96,768]{1,0:T(8,128)(2,1)S(1)}, u32[]{:S(2)}, u32[]{:S(2)}) collective-permute-start(bf16[96,768]{1,0:T(8,128)(2,1)S(1)} %get-tuple-element.269), channel_id=1, source_target_pairs={{0,2},{1,3},{2,0},{3,1},{4,6},{5,7},{6,4},{7,5},{8,10},{9,11},{10,... | collective-permute-start | bytes 442376 | tf_op jit(solution)/shard_map/ppermute | solution.py:46
  177.4 18.5 %collective-permute-start.40 = (bf16[96,768]{1,0:T(8,128)(2,1)S(1)}, bf16[96,768]{1,0:T(8,128)(2,1)S(1)}, u32[]{:S(2)}, u32[]{:S(2)}) collective-permute-start(bf16[96,768]{1,0:T(8,128)(2,1)S(1)} %get-tuple-element.270), channel_id=1, source_target_pairs={{0,3},{1,0},{2,1},{3,2},{4,7},{5,4},{6,5},{7,6},{8,11},{9,8},{10,9... | collective-permute-start | bytes 442376 | tf_op jit(solution)/shard_map/ppermute | solution.py:46
  179.7 39.7 %collective-permute-start.35 = (bf16[480,768]{1,0:T(8,128)(2,1)S(1)}, bf16[480,768]{1,0:T(8,128)(2,1)S(1)}, u32[]{:S(2)}, u32[]{:S(2)}) collective-permute-start(bf16[480,768]{1,0:T(8,128)(2,1)S(1)} %get-tuple-element.259), channel_id=1, source_target_pairs={{0,8},{4,12},{8,0},{12,4},{16,24},{20,28},{24,16},{28,20},{1,9},{5... | collective-permute-start | bytes 2211848 | tf_op jit(solution)/shard_map/ppermute | solution.py:42
  181.0 38.5 %collective-permute-start.36 = (bf16[480,768]{1,0:T(8,128)(2,1)S(1)}, bf16[480,768]{1,0:T(8,128)(2,1)S(1)}, u32[]{:S(2)}, u32[]{:S(2)}) collective-permute-start(bf16[480,768]{1,0:T(8,128)(2,1)S(1)} %get-tuple-element.260), channel_id=1, source_target_pairs={{0,16},{4,20},{8,24},{12,28},{16,0},{20,4},{24,8},{28,12},{1,17},{... | collective-permute-start | bytes 2211848 | tf_op jit(solution)/shard_map/ppermute | solution.py:42
  193.7 25.8 %copy-start.5 = (bf16[256,1024]{1,0:T(8,128)(2,1)}, bf16[256,1024]{1,0:T(8,128)(2,1)S(1)}, u32[]{:S(2)}) copy-start(bf16[256,1024]{1,0:T(8,128)(2,1)S(1)} %get-tuple-element.298.rest_0_) | copy-start | bytes 1572868
  193.7 25.8 %copy-start.6 = (bf16[256,1024]{1,0:T(8,128)(2,1)}, bf16[256,1024]{1,0:T(8,128)(2,1)S(1)}, u32[]{:S(2)}) copy-start(bf16[256,1024]{1,0:T(8,128)(2,1)S(1)} %get-tuple-element.301.rest_3_) | copy-start | bytes 1572868
  193.7 25.8 %copy-start.7 = (bf16[256,1024]{1,0:T(8,128)(2,1)}, bf16[256,1024]{1,0:T(8,128)(2,1)S(1)}, u32[]{:S(2)}) copy-start(bf16[256,1024]{1,0:T(8,128)(2,1)S(1)} %get-tuple-element.304.rest_6_) | copy-start | bytes 1572868
  194.5 25.0 %collective-permute-start.37 = (bf16[480,768]{1,0:T(8,128)(2,1)S(1)}, bf16[480,768]{1,0:T(8,128)(2,1)S(1)}, u32[]{:S(2)}, u32[]{:S(2)}) collective-permute-start(bf16[480,768]{1,0:T(8,128)(2,1)S(1)} %get-tuple-element.261), channel_id=1, source_target_pairs={{0,24},{4,28},{8,16},{12,20},{16,8},{20,12},{24,0},{28,4},{1,25},{... | collective-permute-start | bytes 2211848 | tf_op jit(solution)/shard_map/ppermute | solution.py:42
  228.5 3.9 %collective-permute-start.41 = (bf16[4,96,2432]{2,1,0:T(8,128)(2,1)S(1)}, bf16[4,96,2432]{2,1,0:T(8,128)(2,1)S(1)}, u32[]{:S(2)}, u32[]{:S(2)}) collective-permute-start(bf16[4,96,2432]{2,1,0:T(8,128)(2,1)S(1)} %get-tuple-element.297), channel_id=1, source_target_pairs={{0,4},{4,0},{8,12},{12,8},{16,20},{20,16},{24,28},{28,24},{1,5},{5... | collective-permute-start | bytes 5603336 | tf_op jit(solution)/shard_map/ppermute | solution.py:42
  229.1 8.9 %collective-permute-start.45 = (bf16[120,768]{1,0:T(8,128)(2,1)S(1)}, bf16[120,768]{1,0:T(8,128)(2,1)S(1)}, u32[]{:S(2)}, u32[]{:S(2)}) collective-permute-start(bf16[120,768]{1,0:T(8,128)(2,1)S(1)} %get-tuple-element.320), channel_id=1, source_target_pairs={{0,1},{1,2},{2,3},{3,0},{4,5},{5,6},{6,7},{7,4},{8,9},{9,10},{10,1... | collective-permute-start | bytes 552968 | tf_op jit(solution)/shard_map/ppermute | solution.py:46
  233.7 19.0 %collective-permute-start.42 = (bf16[96,2432]{1,0:T(8,128)(2,1)}, bf16[96,2432]{1,0:T(8,128)(2,1)}, u32[]{:S(2)}, u32[]{:S(2)}) collective-permute-start(bf16[96,2432]{1,0:T(8,128)(2,1)} %get-tuple-element.308), channel_id=1, source_target_pairs={{0,8},{4,12},{8,0},{12,4},{16,24},{20,28},{24,16},{28,20},{1,9},{5... | collective-permute-start | bytes 1400840 | tf_op jit(solution)/shard_map/ppermute | solution.py:42
  234.9 21.9 %collective-permute-start.43 = (bf16[96,2432]{1,0:T(8,128)(2,1)}, bf16[96,2432]{1,0:T(8,128)(2,1)}, u32[]{:S(2)}, u32[]{:S(2)}) collective-permute-start(bf16[96,2432]{1,0:T(8,128)(2,1)} %get-tuple-element.309), channel_id=1, source_target_pairs={{0,16},{4,20},{8,24},{12,28},{16,0},{20,4},{24,8},{28,12},{1,17},{... | collective-permute-start | bytes 1400840 | tf_op jit(solution)/shard_map/ppermute | solution.py:42
  236.5 21.2 %collective-permute-start.44 = (bf16[96,2432]{1,0:T(8,128)(2,1)}, bf16[96,2432]{1,0:T(8,128)(2,1)}, u32[]{:S(2)}, u32[]{:S(2)}) collective-permute-start(bf16[96,2432]{1,0:T(8,128)(2,1)} %get-tuple-element.310), channel_id=1, source_target_pairs={{0,24},{4,28},{8,16},{12,20},{16,8},{20,12},{24,0},{28,4},{1,25},{... | collective-permute-start | bytes 1400840 | tf_op jit(solution)/shard_map/ppermute | solution.py:42
  237.2 15.5 %collective-permute-start.46 = (bf16[120,768]{1,0:T(8,128)(2,1)S(1)}, bf16[120,768]{1,0:T(8,128)(2,1)S(1)}, u32[]{:S(2)}, u32[]{:S(2)}) collective-permute-start(bf16[120,768]{1,0:T(8,128)(2,1)S(1)} %get-tuple-element.321), channel_id=1, source_target_pairs={{0,2},{1,3},{2,0},{3,1},{4,6},{5,7},{6,4},{7,5},{8,10},{9,11},{10,... | collective-permute-start | bytes 552968 | tf_op jit(solution)/shard_map/ppermute | solution.py:46
  238.0 14.7 %collective-permute-start.47 = (bf16[120,768]{1,0:T(8,128)(2,1)S(1)}, bf16[120,768]{1,0:T(8,128)(2,1)S(1)}, u32[]{:S(2)}, u32[]{:S(2)}) collective-permute-start(bf16[120,768]{1,0:T(8,128)(2,1)S(1)} %get-tuple-element.322), channel_id=1, source_target_pairs={{0,3},{1,0},{2,1},{3,2},{4,7},{5,4},{6,5},{7,6},{8,11},{9,8},{10,9... | collective-permute-start | bytes 552968 | tf_op jit(solution)/shard_map/ppermute | solution.py:46
  260.0 10.3 %collective-permute-start.48 = (bf16[24,2432]{1,0:T(8,128)(2,1)}, bf16[24,2432]{1,0:T(8,128)(2,1)S(1)}, u32[]{:S(2)}, u32[]{:S(2)}) collective-permute-start(bf16[24,2432]{1,0:T(8,128)(2,1)} %get-tuple-element.357), channel_id=1, source_target_pairs={{0,1},{1,2},{2,3},{3,0},{4,5},{5,6},{6,7},{7,4},{8,9},{9,10},{10,1... | collective-permute-start | bytes 350216 | tf_op jit(solution)/shard_map/ppermute | solution.py:46
  260.0 11.6 %collective-permute-start.49 = (bf16[24,2432]{1,0:T(8,128)(2,1)S(1)}, bf16[24,2432]{1,0:T(8,128)(2,1)S(1)}, u32[]{:S(2)}, u32[]{:S(2)}) collective-permute-start(bf16[24,2432]{1,0:T(8,128)(2,1)S(1)} %get-tuple-element.359), channel_id=1, source_target_pairs={{0,2},{1,3},{2,0},{3,1},{4,6},{5,7},{6,4},{7,5},{8,10},{9,11},{10,... | collective-permute-start | bytes 350216 | tf_op jit(solution)/shard_map/ppermute | solution.py:46
  262.2 9.4 %collective-permute-start.50 = (bf16[24,2432]{1,0:T(8,128)(2,1)S(1)}, bf16[24,2432]{1,0:T(8,128)(2,1)}, u32[]{:S(2)}, u32[]{:S(2)}) collective-permute-start(bf16[24,2432]{1,0:T(8,128)(2,1)S(1)} %get-tuple-element.358), channel_id=1, source_target_pairs={{0,3},{1,0},{2,1},{3,2},{4,7},{5,4},{6,5},{7,6},{8,11},{9,8},{10,9... | collective-permute-start | bytes 350216 | tf_op jit(solution)/shard_map/ppermute | solution.py:46
  (52 other events, 510.2 us)

commit v2 on v1

--- a/solution.py
+++ b/solution.py
@@ -858,19 +858,19 @@
     m1, s2, k2, grad_t = tie((m1, s2, k2, grad_t))
     got = flip(s2, 1, nd)
     p1 = pieces(nf, cuts, m1)
-    got, k2, p1, grad_t = tie((got, k2, p1, grad_t))
+    p1, grad_t = tie((p1, grad_t))
+    p1 = [shift(p, k, nf) if k else p for k, p in enumerate(p1)]
+    grads = [attend_back(0, project_t, attended[0], grad_t, sums[0], segment_ids)]
+    got, k2, grads, grad_t, p1 = tie((got, k2, grads, grad_t, p1))
     t2 = [add(k2[m], got[m]) for m in range(nd // 2)]
     t2, grad_t = tie((t2, grad_t))
     m2 = meet_plane(t2, nd)
-    p1 = [shift(p, k, nf) if k else p for k, p in enumerate(p1)]
-    grads = [attend_back(0, project_t, attended[0], grad_t, sums[0], segment_ids)]
-    grads, grad_t, p1 = tie((grads, grad_t, p1))
     for g in range(1, GROUPS):
         grads.append(attend_back(g, project_t, attended[g], grad_t, sums[g], segment_ids))
     grads = [grads[g][j] for j in range(3) for g in range(GROUPS)]
-    m2, grads = tie((m2, grads))
     send, keep = weight_grad(me, nd, normed_t, vecs, gvec, (gbe1, gbe2), turns, grads, w)
-    p2 = pieces(nf, cuts + more, after(m2, send))
+    send, m2 = tie((send, m2))
+    p2 = pieces(nf, cuts + more, m2)
     p2 = [shift(p, k, nf) if k else p for k, p in enumerate(p2)]
     totals = sum_cores(send, keep, nd)
     grads, totals = tie((grads, totals))

time: 276 us -> 270 us (0.978)
  waiting for transfers between devices: 35.5 us -> 31.3 us
    ppermute x33, waiting for transfers between devices: 21.9 us -> 17.4 us  [flip(): return lax.ppermute(value, 'dp', [(i, i ^ bit) for i in range(count)])]
    unnamed x130 -> x126, local copies, waits for them, and re-layouts: 11.3 us -> 11.7 us
  transfers between devices with their start and end apart: 51 -> 51, of which waited for: 13 -> 12; matrix products, arithmetic and copies ran while one was open for 1% -> 1% of each run, Pallas kernels for 54% -> 58%
where the time goes in v2:
time: 270 us; the launch traced here: 269 us
  Pallas kernels  160 us (59%)
  starting transfers between devices  56.2 us (21%)
  waiting for transfers between devices  31.3 us (12%)
  local copies, waits for them, and re-layouts  14.6 us (5%)
  other arithmetic  5.23 us (2%)
    pallas_call x2, Pallas kernels, ffn_call(): pl.pallas_call(functools.partial(kernel, nd), grid=(ff // D,), in_specs=s...  55 us
    pallas_call x3, Pallas kernels, attend_back(): pl.pallas_call(attend_back_kernel, grid=(1,), in_specs=[head_rows(group +...  33.6 us
    ppermute x18, starting transfers between devices, shift(): lax.ppermute(value, 'fsdp', [(i, (i + step) % count) for i in range(count)])  31.2 us
    ppermute x33, starting transfers between devices, flip(): return lax.ppermute(value, 'dp', [(i, i ^ bit) for i in range(count)])  25 us
    pallas_call x3, Pallas kernels, attend(): pl.pallas_call(attend_kernel, grid=(1,), in_specs=[head_rows(group + j *...  18.2 us
    ppermute x33, waiting for transfers between devices, flip(): return lax.ppermute(value, 'dp', [(i, i ^ bit) for i in range(count)])  17.4 us
    ppermute x18, waiting for transfers between devices, shift(): lax.ppermute(value, 'fsdp', [(i, (i + step) % count) for i in range(count)])  13.9 us
    pallas_call x1, Pallas kernels, project_back(): pl.pallas_call(functools.partial(project_back_kernel, nd), grid=(1,), in_...  13.1 us
  transfers between devices with their start and end apart: 51, of which 12 were waited for; matrix products, arithmetic and copies ran while one was open for 1% of the time, Pallas kernels for 58%

profile of v2, /device:TPU:0, one launch (start us, length us, event | category | flops | bytes accessed | tf_op | source)
XLA Modules:
  0.0 269.1 jit_solution(6957681314636531603)
XLA Ops:
  0.7 3.1 %pack.1 = (bf16[24,2432]{1,0:T(8,128)(2,1)}, bf16[120,768]{1,0:T(8,128)(2,1)}, bf16[96,768]{1,0:T(8,128)(2,1)}) custom-call(bf16[24,2304]{1,0:T(8,128)(2,1)} %proj_ref.1, bf16[24,3072]{1,0:T(8,128)(2,1)} %exp_ref.1, bf16[96,768]{1,0:T(8,128)(2,1)} %red_ref.1, bf16[24,768]{1,0:T(8,128)(2,1)} %comb_ref.1, bf16[2,768,384]{2,1,0:T(8,128)(2,1)} %constant.32.clone.pick_ref, ...), custom_call_target="tpu_custom_call" | custom-call | bytes 3145728 | tf_op jit(solution)/shard_map/pack/pallas_call | solution.py:150
  3.7 3.1 %collective-permute-start = (bf16[24,2432]{1,0:T(8,128)(2,1)}, bf16[24,2432]{1,0:T(8,128)(2,1)S(1)}, u32[]{:S(2)}, u32[]{:S(2)}) collective-permute-start(bf16[24,2432]{1,0:T(8,128)(2,1)} %get-tuple-element.170.refs_0_), channel_id=1, source_target_pairs={{0,1},{1,2},{2,3},{3,0},{4,5},{5,6},{6,7},{7,4},{8,9},{9,10},{10,1... | collective-permute-start | bytes 350216 | tf_op jit(solution)/shard_map/ppermute | solution.py:46
  6.8 2.6 collective-permute-start.1
  9.4 1.3 collective-permute-start.2
  10.7 1.4 copy-done.27
  12.2 2.4 prepare.1
  14.6 1.7 copy-done.43
  16.2 1.2 copy-done.45
  17.5 1.6 collective-permute-start.3
  19.1 1.5 collective-permute-start.4
  21.1 2.9 %collective-permute-start.6 = (bf16[120,768]{1,0:T(8,128)(2,1)S(1)}, bf16[120,768]{1,0:T(8,128)(2,1)S(1)}, u32[]{:S(2)}, u32[]{:S(2)}) collective-permute-start(bf16[120,768]{1,0:T(8,128)(2,1)S(1)} %copy-done.15), channel_id=1, source_target_pairs={{0,1},{1,2},{2,3},{3,0},{4,5},{5,6},{6,7},{7,4},{8,9},{9,10},{10,1... | collective-permute-start | bytes 552968 | tf_op jit(solution)/shard_map/ppermute | solution.py:46
  24.0 1.6 collective-permute-start.7
  25.6 5.1 %collective-permute-done.6.refs_1_ = bf16[120,768]{1,0:T(8,128)(2,1)S(1)} collective-permute-done((bf16[120,768]{1,0:T(8,128)(2,1)S(1)}, bf16[120,768]{1,0:T(8,128)(2,1)S(1)}, u32[]{:S(2)}, u32[]{:S(2)}) %collective-permute-start.6) | collective-permute-done | bytes 184352 | tf_op jit(solution)/shard_map/ppermute | solution.py:46
  31.5 5.0 %collective-permute-done.7.refs_2_ = bf16[120,768]{1,0:T(8,128)(2,1)S(1)} collective-permute-done((bf16[120,768]{1,0:T(8,128)(2,1)S(1)}, bf16[120,768]{1,0:T(8,128)(2,1)S(1)}, u32[]{:S(2)}, u32[]{:S(2)}) %collective-permute-start.7) | collective-permute-done | bytes 184352 | tf_op jit(solution)/shard_map/ppermute | solution.py:46
  36.4 1.8 collective-permute-done.8.refs_3_
  38.3 3.1 %collective-permute-done.4.rest_4_.rest_13_ = bf16[96,2432]{1,0:T(8,128)(2,1)} collective-permute-done((bf16[96,2432]{1,0:T(8,128)(2,1)S(1)}, bf16[96,2432]{1,0:T(8,128)(2,1)}, u32[]{:S(2)}, u32[]{:S(2)}) %collective-permute-start.4) | collective-permute-done | bytes 466976 | tf_op jit(solution)/shard_map/ppermute | solution.py:42
  42.4 1.2 collective-permute-start.13
  44.0 1.5 collective-permute-start.14
  45.5 1.2 collective-permute-start.15
  46.7 1.3 copy-done.37
  48.0 1.9 copy-done.44
  49.9 7.5 %project.1 = (bf16[2304,1024]{1,0:T(8,128)(2,1)S(1)}, bf16[768,1024]{1,0:T(8,128)(2,1)S(1)}, f32[16,768]{1,0:T(8,128)S(1)}, f32[1,3072]{1,0:T(1,128)S(1)}) custom-call(s32[1]{0:T(128)} %bitcast.me_ref, f32[768,1024]{1,0:T(8,128)S(1)} %copy-done.44, bf16[2,768,384]{2,1,0:T(8,128)(2,1)S(1)} %copy-done.37, bf16[96,2432]{1,0:T(8,128)(2,1)S(1)} %line_up.3.rest_0_.rest_9_, ...), custom_call_target="tpu_custom_call" | custom-call | flops 3623878656 | bytes 12582912 | tf_op jit(solution)/shard_map/project/pallas_call | solution.py:287
  57.4 3.5 %collective-permute-start.16 = (bf16[96,768]{1,0:T(8,128)(2,1)S(1)}, bf16[96,768]{1,0:T(8,128)(2,1)S(1)}, u32[]{:S(2)}, u32[]{:S(2)}) collective-permute-start(bf16[96,768]{1,0:T(8,128)(2,1)S(1)} %copy-done.24), channel_id=1, source_target_pairs={{0,1},{1,2},{2,3},{3,0},{4,5},{5,6},{6,7},{7,4},{8,9},{9,10},{10,1... | collective-permute-start | bytes 442376 | tf_op jit(solution)/shard_map/ppermute | solution.py:46
  60.9 1.0 collective-permute-start.17
  61.9 6.1 %attend.3 = (bf16[256,1024]{1,0:T(8,128)(2,1)S(1)}, f32[8,1,1024]{2,1,0:T(1,128)S(1)}) custom-call(bf16[2304,1024]{1,0:T(8,128)(2,1)S(1)} %get-tuple-element.198.q_ref.k_ref.v_ref, bf16[2304,1024]{1,0:T(8,128)(2,1)S(1)} %get-tuple-element.198.q_ref.k_ref.v_ref, bf16[2304,1024]{1,0:T(8,128)(2,1)S(1)} %get-tuple-element.198.q_ref.k_ref.v_ref, ...), custom_call_target="tpu_custom_call" | custom-call | flops 7000000000 | bytes 3145728 | tf_op jit(solution)/shard_map/attend/pallas_call | solution.py:374
  68.0 2.9 %collective-permute-start.18 = (bf16[96,768]{1,0:T(8,128)(2,1)S(1)}, bf16[96,768]{1,0:T(8,128)(2,1)S(1)}, u32[]{:S(2)}, u32[]{:S(2)}) collective-permute-start(bf16[96,768]{1,0:T(8,128)(2,1)S(1)} %copy-done.24), channel_id=1, source_target_pairs={{0,3},{1,0},{2,1},{3,2},{4,7},{5,4},{6,5},{7,6},{8,11},{9,8},{10,9... | collective-permute-start | bytes 442376 | tf_op jit(solution)/shard_map/ppermute | solution.py:46
  70.9 6.1 %attend.4 = (bf16[256,1024]{1,0:T(8,128)(2,1)S(1)}, f32[8,1,1024]{2,1,0:T(1,128)S(1)}) custom-call(bf16[2304,1024]{1,0:T(8,128)(2,1)S(1)} %get-tuple-element.198.q_ref.k_ref.v_ref, bf16[2304,1024]{1,0:T(8,128)(2,1)S(1)} %get-tuple-element.198.q_ref.k_ref.v_ref, bf16[2304,1024]{1,0:T(8,128)(2,1)S(1)} %get-tuple-element.198.q_ref.k_ref.v_ref, ...), custom_call_target="tpu_custom_call" | custom-call | flops 7000000000 | bytes 3145728 | tf_op jit(solution)/shard_map/attend/pallas_call | solution.py:374
  77.0 1.3 collective-permute-done.14.rest_7_.rest_15_
  79.4 10.1 %line_up.5.rest_3_ = bf16[384,768]{1,0:T(8,128)(2,1)S(1)} custom-call(s32[1]{0:T(128)} %bitcast.1.me_ref, bf16[96,768]{1,0:T(8,128)(2,1)S(1)} %copy-done.24, bf16[96,768]{1,0:T(8,128)(2,1)S(1)} %collective-permute-done.16.refs_1_, bf16[96,768]{1,0:T(8,128)(2,1)S(1)} %collective-permute-done.17.refs_2_, bf16[96,768]{1,0:T(8,128)(2,1)S(1)} %collective-permute-done.18.refs_3_), custom_call_target="tpu_custom_call" | custom-call | bytes 4194304 | tf_op jit(solution)/shard_map/line_up/pallas_call | solution.py:71
  89.5 1.3 collective-permute-start.23
  90.8 6.1 %attend.5 = (bf16[256,1024]{1,0:T(8,128)(2,1)S(1)}, f32[8,1,1024]{2,1,0:T(1,128)S(1)}) custom-call(bf16[2304,1024]{1,0:T(8,128)(2,1)S(1)} %get-tuple-element.198.q_ref.k_ref.v_ref, bf16[2304,1024]{1,0:T(8,128)(2,1)S(1)} %get-tuple-element.198.q_ref.k_ref.v_ref, bf16[2304,1024]{1,0:T(8,128)(2,1)S(1)} %get-tuple-element.198.q_ref.k_ref.v_ref, ...), custom_call_target="tpu_custom_call" | custom-call | flops 7000000000 | bytes 3145728 | tf_op jit(solution)/shard_map/attend/pallas_call | solution.py:374
  96.9 0.9 collective-permute-start.24
  97.8 1.4 collective-permute-start.25
  99.3 25.4 %ffn_first.1 = (f32[1024,768]{1,0:T(8,128)}, bf16[1024,768]{1,0:T(8,128)(2,1)S(1)}, f32[1024,768]{1,0:T(8,128)}, f32[1024,768]{1,0:T(8,128)}, bf16[4,384,768]{2,...) custom-call(s32[1]{0:T(128)} %bitcast.me_ref, bf16[1024,768]{1,0:T(8,128)(2,1)S(1)} %copy-done.2, ...), custom_call_target="tpu_custom_call" | custom-call | flops 14495514624 | bytes 20971520 | tf_op jit(solution)/shard_map/ffn_first/pallas_call | solution.py:666
  125.0 4.5 %collective-permute-done.26 = bf16[4,384,768]{2,1,0:T(8,128)(2,1)S(1)} collective-permute-done((bf16[4,384,768]{2,1,0:T(8,128)(2,1)S(1)}, bf16[4,384,768]{2,1,0:T(8,128)(2,1)S(1)}, u32[]{:S(2)}, u32[]{:S(2)}) %collective-permute-start.26) | collective-permute-done | bytes 2359328 | tf_op jit(solution)/shard_map/ppermute | solution.py:42
  131.2 1.3 collective-permute-start.31
  132.5 0.9 collective-permute-start.32
  133.4 1.4 collective-permute-start.33
  134.8 0.8 copy-done.61
  135.8 29.6 %ffn_last.1 = (bf16[1024,768]{1,0:T(8,128)(2,1)}, f32[1024,768]{1,0:T(8,128)}, bf16[768,1024]{1,0:T(8,128)(2,1)}, bf16[4,480,768]{2,1,0:T(8,128)(2,1)}, bf16[4,4...) custom-call(s32[1]{0:T(128)} %bitcast.me_ref, bf16[1024,768]{1,0:T(8,128)(2,1)} %cot_ref.4, ...), custom_call_target="tpu_custom_call" | custom-call | flops 14495514624 | bytes 20971520 | tf_op jit(solution)/shard_map/ffn_last/pallas_call | solution.py:666
  166.7 3.1 %collective-permute-start.35 = (bf16[96,768]{1,0:T(8,128)(2,1)S(1)}, bf16[96,768]{1,0:T(8,128)(2,1)S(1)}, u32[]{:S(2)}, u32[]{:S(2)}) collective-permute-start(bf16[96,768]{1,0:T(8,128)(2,1)S(1)} %get-tuple-element.249), channel_id=1, source_target_pairs={{0,1},{1,2},{2,3},{3,0},{4,5},{5,6},{6,7},{7,4},{8,9},{9,10},{10,1... | collective-permute-start | bytes 442376 | tf_op jit(solution)/shard_map/ppermute | solution.py:46
  170.2 2.6 collective-permute-start.37
  172.9 2.3 copy-done.42
  175.2 11.1 %attend_back.3 = (bf16[256,1024]{1,0:T(8,128)(2,1)S(1)}, bf16[256,1024]{1,0:T(8,128)(2,1)S(1)}, bf16[256,1024]{1,0:T(8,128)(2,1)S(1)}) custom-call(bf16[2304,1024]{1,0:T(8,128)(2,1)S(1)} %copy-done.42, bf16[2304,1024]{1,0:T(8,128)(2,1)S(1)} %copy-done.42, bf16[2304,1024]{1,0:T(8,128)(2,1)S(1)} %copy-done.42, bf16[256,1024]{1,0:T(8,128)(2,1)S(1)} %copy-done.50, ...), custom_call_target="tpu_custom_call" | custom-call | flops 14000000000 | bytes 5242880 | tf_op jit(solution)/shard_map/attend_back/pallas_call | solution.py:460
  187.2 1.2 collective-permute-start.38
  188.4 1.6 collective-permute-start.39
  190.7 11.3 %attend_back.5 = (bf16[256,1024]{1,0:T(8,128)(2,1)S(1)}, bf16[256,1024]{1,0:T(8,128)(2,1)S(1)}, bf16[256,1024]{1,0:T(8,128)(2,1)S(1)}) custom-call(bf16[2304,1024]{1,0:T(8,128)(2,1)S(1)} %copy-done.42, bf16[2304,1024]{1,0:T(8,128)(2,1)S(1)} %copy-done.42, bf16[2304,1024]{1,0:T(8,128)(2,1)S(1)} %copy-done.42, bf16[256,1024]{1,0:T(8,128)(2,1)S(1)} %copy-done.52, ...), custom_call_target="tpu_custom_call" | custom-call | flops 14000000000 | bytes 5242880 | tf_op jit(solution)/shard_map/attend_back/pallas_call | solution.py:460
  202.0 11.3 %attend_back.4 = (bf16[256,1024]{1,0:T(8,128)(2,1)S(1)}, bf16[256,1024]{1,0:T(8,128)(2,1)S(1)}, bf16[256,1024]{1,0:T(8,128)(2,1)S(1)}) custom-call(bf16[2304,1024]{1,0:T(8,128)(2,1)S(1)} %copy-done.42, bf16[2304,1024]{1,0:T(8,128)(2,1)S(1)} %copy-done.42, bf16[2304,1024]{1,0:T(8,128)(2,1)S(1)} %copy-done.42, bf16[256,1024]{1,0:T(8,128)(2,1)S(1)} %copy-done.48, ...), custom_call_target="tpu_custom_call" | custom-call | flops 14000000000 | bytes 5242880 | tf_op jit(solution)/shard_map/attend_back/pallas_call | solution.py:460
  213.4 8.8 %weight_grad.1 = (bf16[4,96,2432]{2,1,0:T(8,128)(2,1)S(1)}, bf16[4,96,2432]{2,1,0:T(8,128)(2,1)S(1)}) custom-call(s32[1]{0:T(128)} %bitcast.me_ref, bf16[768,1024]{1,0:T(8,128)(2,1)S(1)} %copy-done.40, f32[16,768]{1,0:T(8,128)S(1)} %get-tuple-element.185.vec_ref, f32[8,768]{1,0:T(8,128)S(1)} %get-tuple-element.268.gv_ref, ...), custom_call_target="tpu_custom_call" | custom-call | flops 3623878656 | bytes 10485760 | tf_op jit(solution)/shard_map/weight_grad/pallas_call | solution.py:753
  223.3 2.9 %collective-permute-done.41 = bf16[4,96,2432]{2,1,0:T(8,128)(2,1)S(1)} collective-permute-done((bf16[4,96,2432]{2,1,0:T(8,128)(2,1)S(1)}, bf16[4,96,2432]{2,1,0:T(8,128)(2,1)S(1)}, u32[]{:S(2)}, u32[]{:S(2)}) %collective-permute-start.41) | collective-permute-done | bytes 1867808 | tf_op jit(solution)/shard_map/ppermute | solution.py:42
  226.2 1.4 fusion.11
  227.6 1.2 collective-permute-start.42
  228.8 1.6 collective-permute-start.43
  231.3 0.8 collective-permute-done.45.refs_5_
  232.1 1.1 collective-permute-start.47
  233.3 13.1 %project_back.1 = f32[1024,768]{1,0:T(8,128)} custom-call(s32[1]{0:T(128)} %bitcast.me_ref, bf16[1024,768]{1,0:T(8,128)(2,1)} %x_ref.4, f32[1024,768]{1,0:T(8,128)} %get-tuple-element.224.gm_ref, f32[16,768]{1,0:T(8,128)} %copy-done.26, bf16[256,1024]{1,0:T(8,128)(2,1)} %copy-done.5, bf16[256,1024]{1,0:T(8,128)(2,1)} %copy-done.11, ...), custom_call_target="tpu_custom_call" | custom-call | flops 3623878656 | bytes 20971520 | tf_op jit(solution)/shard_map/project_back/pallas_call | solution.py:794
  246.5 4.2 %collective-permute-done.43 = bf16[96,2432]{1,0:T(8,128)(2,1)} collective-permute-done((bf16[96,2432]{1,0:T(8,128)(2,1)}, bf16[96,2432]{1,0:T(8,128)(2,1)}, u32[]{:S(2)}, u32[]{:S(2)}) %collective-permute-start.43) | collective-permute-done | bytes 466976 | tf_op jit(solution)/shard_map/ppermute | solution.py:42
  250.7 0.9 collective-permute-done.44
  251.6 1.6 add_convert_fusion.8
  253.9 2.2 collective-permute-start.49
  256.1 1.6 collective-permute-start.50
  257.8 6.5 %finish.1 = (f32[24,3072]{1,0:T(8,128)}, f32[96,768]{1,0:T(8,128)}, f32[24,768]{1,0:T(8,128)}) custom-call(bf16[2,768,384]{2,1,0:T(8,128)(2,1)S(1)} %copy-done, bf16[96,768]{1,0:T(8,128)(2,1)S(1)} %copy-done.17, bf16[96,768]{1,0:T(8,128)(2,1)S(1)} %copy-done.19, bf16[96,768]{1,0:T(8,128)(2,1)S(1)} %copy-done.21, bf16[96,768]{1,0:T(8,128)(2,1)S(1)} %copy-done.23, ...), custom_call_target="tpu_custom_call" | custom-call | bytes 3145728 | tf_op jit(solution)/shard_map/finish/pallas_call | solution.py:206
  264.2 1.2 collective-permute-done.49
  265.5 1.0 convert_add_fusion
  (194 shorter events, 14.1 us)
Async XLA Ops:
  3.7 13.7 %collective-permute-start = (bf16[24,2432]{1,0:T(8,128)(2,1)}, bf16[24,2432]{1,0:T(8,128)(2,1)S(1)}, u32[]{:S(2)}, u32[]{:S(2)}) collective-permute-start(bf16[24,2432]{1,0:T(8,128)(2,1)} %get-tuple-element.170.refs_0_), channel_id=1, source_target_pairs={{0,1},{1,2},{2,3},{3,0},{4,5},{5,6},{6,7},{7,4},{8,9},{9,10},{10,1... | collective-permute-start | bytes 350216 | tf_op jit(solution)/shard_map/ppermute | solution.py:46
  6.8 10.6 %collective-permute-start.1 = (bf16[24,2432]{1,0:T(8,128)(2,1)}, bf16[24,2432]{1,0:T(8,128)(2,1)S(1)}, u32[]{:S(2)}, u32[]{:S(2)}) collective-permute-start(bf16[24,2432]{1,0:T(8,128)(2,1)} %get-tuple-element.170.refs_0_), channel_id=1, source_target_pairs={{0,2},{1,3},{2,0},{3,1},{4,6},{5,7},{6,4},{7,5},{8,10},{9,11},{10,... | collective-permute-start | bytes 350216 | tf_op jit(solution)/shard_map/ppermute | solution.py:46
  9.4 8.0 %collective-permute-start.2 = (bf16[24,2432]{1,0:T(8,128)(2,1)}, bf16[24,2432]{1,0:T(8,128)(2,1)S(1)}, u32[]{:S(2)}, u32[]{:S(2)}) collective-permute-start(bf16[24,2432]{1,0:T(8,128)(2,1)} %get-tuple-element.170.refs_0_), channel_id=1, source_target_pairs={{0,3},{1,0},{2,1},{3,2},{4,7},{5,4},{6,5},{7,6},{8,11},{9,8},{10,9... | collective-permute-start | bytes 350216 | tf_op jit(solution)/shard_map/ppermute | solution.py:46
  17.5 195.8 %copy-start.1 = (bf16[96,2432]{1,0:T(8,128)(2,1)}, bf16[96,2432]{1,0:T(8,128)(2,1)S(1)}, u32[]{:S(2)}) copy-start(bf16[96,2432]{1,0:T(8,128)(2,1)S(1)} %line_up.3.rest_0_.rest_9_) | copy-start | bytes 1400836
  17.5 20.8 %collective-permute-start.3 = (bf16[96,2432]{1,0:T(8,128)(2,1)S(1)}, bf16[96,2432]{1,0:T(8,128)(2,1)S(1)}, u32[]{:S(2)}, u32[]{:S(2)}) collective-permute-start(bf16[96,2432]{1,0:T(8,128)(2,1)S(1)} %line_up.3.rest_0_.rest_9_), channel_id=1, source_target_pairs={{0,8},{4,12},{8,0},{12,4},{16,24},{20,28},{24,16},{28,20},{1,9},{5... | collective-permute-start | bytes 1400840 | tf_op jit(solution)/shard_map/ppermute | solution.py:42
  19.1 22.3 %collective-permute-start.4 = (bf16[96,2432]{1,0:T(8,128)(2,1)S(1)}, bf16[96,2432]{1,0:T(8,128)(2,1)}, u32[]{:S(2)}, u32[]{:S(2)}) collective-permute-start(bf16[96,2432]{1,0:T(8,128)(2,1)S(1)} %line_up.3.rest_0_.rest_9_), channel_id=1, source_target_pairs={{0,16},{4,20},{8,24},{12,28},{16,0},{20,4},{24,8},{28,12},{1,17},{... | collective-permute-start | bytes 1400840 | tf_op jit(solution)/shard_map/ppermute | solution.py:42
  20.6 20.8 %collective-permute-start.5 = (bf16[96,2432]{1,0:T(8,128)(2,1)S(1)}, bf16[96,2432]{1,0:T(8,128)(2,1)}, u32[]{:S(2)}, u32[]{:S(2)}) collective-permute-start(bf16[96,2432]{1,0:T(8,128)(2,1)S(1)} %line_up.3.rest_0_.rest_9_), channel_id=1, source_target_pairs={{0,24},{4,28},{8,16},{12,20},{16,8},{20,12},{24,0},{28,4},{1,25},{... | collective-permute-start | bytes 1400840 | tf_op jit(solution)/shard_map/ppermute | solution.py:42
  21.1 9.6 %collective-permute-start.6 = (bf16[120,768]{1,0:T(8,128)(2,1)S(1)}, bf16[120,768]{1,0:T(8,128)(2,1)S(1)}, u32[]{:S(2)}, u32[]{:S(2)}) collective-permute-start(bf16[120,768]{1,0:T(8,128)(2,1)S(1)} %copy-done.15), channel_id=1, source_target_pairs={{0,1},{1,2},{2,3},{3,0},{4,5},{5,6},{6,7},{7,4},{8,9},{9,10},{10,1... | collective-permute-start | bytes 552968 | tf_op jit(solution)/shard_map/ppermute | solution.py:46
  24.0 12.5 %collective-permute-start.7 = (bf16[120,768]{1,0:T(8,128)(2,1)S(1)}, bf16[120,768]{1,0:T(8,128)(2,1)S(1)}, u32[]{:S(2)}, u32[]{:S(2)}) collective-permute-start(bf16[120,768]{1,0:T(8,128)(2,1)S(1)} %copy-done.15), channel_id=1, source_target_pairs={{0,2},{1,3},{2,0},{3,1},{4,6},{5,7},{6,4},{7,5},{8,10},{9,11},{10,... | collective-permute-start | bytes 552968 | tf_op jit(solution)/shard_map/ppermute | solution.py:46
  30.7 7.5 %collective-permute-start.8 = (bf16[120,768]{1,0:T(8,128)(2,1)S(1)}, bf16[120,768]{1,0:T(8,128)(2,1)S(1)}, u32[]{:S(2)}, u32[]{:S(2)}) collective-permute-start(bf16[120,768]{1,0:T(8,128)(2,1)S(1)} %copy-done.15), channel_id=1, source_target_pairs={{0,3},{1,0},{2,1},{3,2},{4,7},{5,4},{6,5},{7,6},{8,11},{9,8},{10,9... | collective-permute-start | bytes 552968 | tf_op jit(solution)/shard_map/ppermute | solution.py:46
  38.3 61.0 %copy-start.3 = (bf16[480,768]{1,0:T(8,128)(2,1)}, bf16[480,768]{1,0:T(8,128)(2,1)S(1)}, u32[]{:S(2)}) copy-start(bf16[480,768]{1,0:T(8,128)(2,1)S(1)} %line_up.4.rest_3_.rest_11_) | copy-start | bytes 2211844
  38.3 175.0 %copy-start.14 = (bf16[96,2432]{1,0:T(8,128)(2,1)}, bf16[96,2432]{1,0:T(8,128)(2,1)S(1)}, u32[]{:S(2)}) copy-start(bf16[96,2432]{1,0:T(8,128)(2,1)S(1)} %collective-permute-done.3.rest_2_.rest_11_) | copy-start | bytes 1400836
  41.4 2.6 collective-permute-start.10
  41.4 4.1 %collective-permute-start.11 = (bf16[96,2432]{1,0:T(8,128)(2,1)}, bf16[96,2432]{1,0:T(8,128)(2,1)}, u32[]{:S(2)}, u32[]{:S(2)}) collective-permute-start(bf16[96,2432]{1,0:T(8,128)(2,1)} %collective-permute-done.4.rest_4_.rest_13_), channel_id=1, source_target_pairs={{0,4},{4,0},{8,12},{12,8},{16,20},{20,16},{24,28},{28,24},{1,5},{5... | collective-permute-start | bytes 1400840 | tf_op jit(solution)/shard_map/ppermute | solution.py:42
  41.9 4.8 %collective-permute-start.12 = (bf16[96,2432]{1,0:T(8,128)(2,1)}, bf16[96,2432]{1,0:T(8,128)(2,1)}, u32[]{:S(2)}, u32[]{:S(2)}) collective-permute-start(bf16[96,2432]{1,0:T(8,128)(2,1)} %collective-permute-done.5.rest_6_.rest_15_), channel_id=1, source_target_pairs={{0,4},{4,0},{8,12},{12,8},{16,20},{20,16},{24,28},{28,24},{1,5},{5... | collective-permute-start | bytes 1400840 | tf_op jit(solution)/shard_map/ppermute | solution.py:42
  41.9 4.8 %collective-permute-start.9 = (bf16[96,2432]{1,0:T(8,128)(2,1)S(1)}, bf16[96,2432]{1,0:T(8,128)(2,1)}, u32[]{:S(2)}, u32[]{:S(2)}) collective-permute-start(bf16[96,2432]{1,0:T(8,128)(2,1)S(1)} %line_up.3.rest_0_.rest_9_), channel_id=1, source_target_pairs={{0,4},{4,0},{8,12},{12,8},{16,20},{20,16},{24,28},{28,24},{1,5},{5... | collective-permute-start | bytes 1400840 | tf_op jit(solution)/shard_map/ppermute | solution.py:42
  42.4 34.6 %collective-permute-start.13 = (bf16[480,768]{1,0:T(8,128)(2,1)S(1)}, bf16[480,768]{1,0:T(8,128)(2,1)S(1)}, u32[]{:S(2)}, u32[]{:S(2)}) collective-permute-start(bf16[480,768]{1,0:T(8,128)(2,1)S(1)} %line_up.4.rest_3_.rest_11_), channel_id=1, source_target_pairs={{0,8},{4,12},{8,0},{12,4},{16,24},{20,28},{24,16},{28,20},{1,9},{5... | collective-permute-start | bytes 2211848 | tf_op jit(solution)/shard_map/ppermute | solution.py:42
  44.0 34.3 %collective-permute-start.14 = (bf16[480,768]{1,0:T(8,128)(2,1)S(1)}, bf16[480,768]{1,0:T(8,128)(2,1)S(1)}, u32[]{:S(2)}, u32[]{:S(2)}) collective-permute-start(bf16[480,768]{1,0:T(8,128)(2,1)S(1)} %line_up.4.rest_3_.rest_11_), channel_id=1, source_target_pairs={{0,16},{4,20},{8,24},{12,28},{16,0},{20,4},{24,8},{28,12},{1,17},{... | collective-permute-start | bytes 2211848 | tf_op jit(solution)/shard_map/ppermute | solution.py:42
  45.5 32.8 %collective-permute-start.15 = (bf16[480,768]{1,0:T(8,128)(2,1)S(1)}, bf16[480,768]{1,0:T(8,128)(2,1)S(1)}, u32[]{:S(2)}, u32[]{:S(2)}) collective-permute-start(bf16[480,768]{1,0:T(8,128)(2,1)S(1)} %line_up.4.rest_3_.rest_11_), channel_id=1, source_target_pairs={{0,24},{4,28},{8,16},{12,20},{16,8},{20,12},{24,0},{28,4},{1,25},{... | collective-permute-start | bytes 2211848 | tf_op jit(solution)/shard_map/ppermute | solution.py:42
  57.4 33.4 %copy-start.41 = (bf16[2304,1024]{1,0:T(8,128)(2,1)}, bf16[2304,1024]{1,0:T(8,128)(2,1)S(1)}, u32[]{:S(2)}) copy-start(bf16[2304,1024]{1,0:T(8,128)(2,1)S(1)} %get-tuple-element.198.q_ref.k_ref.v_ref) | copy-start | bytes 14155780
  57.4 155.9 %copy-start.26 = (f32[16,768]{1,0:T(8,128)}, f32[16,768]{1,0:T(8,128)S(1)}, u32[]{:S(2)}) copy-start(f32[16,768]{1,0:T(8,128)S(1)} %get-tuple-element.185.vec_ref) | copy-start | bytes 147460
  57.4 10.6 %collective-permute-start.16 = (bf16[96,768]{1,0:T(8,128)(2,1)S(1)}, bf16[96,768]{1,0:T(8,128)(2,1)S(1)}, u32[]{:S(2)}, u32[]{:S(2)}) collective-permute-start(bf16[96,768]{1,0:T(8,128)(2,1)S(1)} %copy-done.24), channel_id=1, source_target_pairs={{0,1},{1,2},{2,3},{3,0},{4,5},{5,6},{6,7},{7,4},{8,9},{9,10},{10,1... | collective-permute-start | bytes 442376 | tf_op jit(solution)/shard_map/ppermute | solution.py:46
  60.9 16.0 %collective-permute-start.17 = (bf16[96,768]{1,0:T(8,128)(2,1)S(1)}, bf16[96,768]{1,0:T(8,128)(2,1)S(1)}, u32[]{:S(2)}, u32[]{:S(2)}) collective-permute-start(bf16[96,768]{1,0:T(8,128)(2,1)S(1)} %copy-done.24), channel_id=1, source_target_pairs={{0,2},{1,3},{2,0},{3,1},{4,6},{5,7},{6,4},{7,5},{8,10},{9,11},{10,... | collective-permute-start | bytes 442376 | tf_op jit(solution)/shard_map/ppermute | solution.py:46
  68.0 31.3 %copy-start.49 = (bf16[256,1024]{1,0:T(8,128)(2,1)}, bf16[256,1024]{1,0:T(8,128)(2,1)S(1)}, u32[]{:S(2)}) copy-start(bf16[256,1024]{1,0:T(8,128)(2,1)S(1)} %get-tuple-element.188.rest_0_.o_ref) | copy-start | bytes 1572868
  68.0 9.0 %collective-permute-start.18 = (bf16[96,768]{1,0:T(8,128)(2,1)S(1)}, bf16[96,768]{1,0:T(8,128)(2,1)S(1)}, u32[]{:S(2)}, u32[]{:S(2)}) collective-permute-start(bf16[96,768]{1,0:T(8,128)(2,1)S(1)} %copy-done.24), channel_id=1, source_target_pairs={{0,3},{1,0},{2,1},{3,2},{4,7},{5,4},{6,5},{7,6},{8,11},{9,8},{10,9... | collective-permute-start | bytes 442376 | tf_op jit(solution)/shard_map/ppermute | solution.py:46
  78.3 18.6 %collective-permute-start.19 = (bf16[480,768]{1,0:T(8,128)(2,1)S(1)}, bf16[480,768]{1,0:T(8,128)(2,1)S(1)}, u32[]{:S(2)}, u32[]{:S(2)}) collective-permute-start(bf16[480,768]{1,0:T(8,128)(2,1)S(1)} %line_up.4.rest_3_.rest_11_), channel_id=1, source_target_pairs={{0,4},{4,0},{8,12},{12,8},{16,20},{20,16},{24,28},{28,24},{1,5},{5... | collective-permute-start | bytes 2211848 | tf_op jit(solution)/shard_map/ppermute | solution.py:42
  78.4 19.4 %collective-permute-start.20 = (bf16[480,768]{1,0:T(8,128)(2,1)S(1)}, bf16[480,768]{1,0:T(8,128)(2,1)S(1)}, u32[]{:S(2)}, u32[]{:S(2)}) collective-permute-start(bf16[480,768]{1,0:T(8,128)(2,1)S(1)} %collective-permute-done.13.rest_5_.rest_13_), channel_id=1, source_target_pairs={{0,4},{4,0},{8,12},{12,8},{16,20},{20,16},{24,28},{28,24},{1,5},{5... | collective-permute-start | bytes 2211848 | tf_op jit(solution)/shard_map/ppermute | solution.py:42
  78.9 20.3 %collective-permute-start.21 = (bf16[480,768]{1,0:T(8,128)(2,1)S(1)}, bf16[480,768]{1,0:T(8,128)(2,1)S(1)}, u32[]{:S(2)}, u32[]{:S(2)}) collective-permute-start(bf16[480,768]{1,0:T(8,128)(2,1)S(1)} %collective-permute-done.14.rest_7_.rest_15_), channel_id=1, source_target_pairs={{0,4},{4,0},{8,12},{12,8},{16,20},{20,16},{24,28},{28,24},{1,5},{5... | collective-permute-start | bytes 2211848 | tf_op jit(solution)/shard_map/ppermute | solution.py:42
  79.0 20.3 %collective-permute-start.22 = (bf16[480,768]{1,0:T(8,128)(2,1)S(1)}, bf16[480,768]{1,0:T(8,128)(2,1)S(1)}, u32[]{:S(2)}, u32[]{:S(2)}) collective-permute-start(bf16[480,768]{1,0:T(8,128)(2,1)S(1)} %collective-permute-done.15.rest_9_.rest_17_), channel_id=1, source_target_pairs={{0,4},{4,0},{8,12},{12,8},{16,20},{20,16},{24,28},{28,24},{1,5},{5... | collective-permute-start | bytes 2211848 | tf_op jit(solution)/shard_map/ppermute | solution.py:42
  89.5 40.0 %copy-start.4 = (bf16[384,768]{1,0:T(8,128)(2,1)}, bf16[384,768]{1,0:T(8,128)(2,1)S(1)}, u32[]{:S(2)}) copy-start(bf16[384,768]{1,0:T(8,128)(2,1)S(1)} %line_up.5.rest_3_) | copy-start | bytes 1769476
  89.5 35.3 %collective-permute-start.23 = (bf16[384,768]{1,0:T(8,128)(2,1)S(1)}, bf16[384,768]{1,0:T(8,128)(2,1)S(1)}, u32[]{:S(2)}, u32[]{:S(2)}) collective-permute-start(bf16[384,768]{1,0:T(8,128)(2,1)S(1)} %line_up.5.rest_3_), channel_id=1, source_target_pairs={{0,8},{4,12},{8,0},{12,4},{16,24},{20,28},{24,16},{28,20},{1,9},{5... | collective-permute-start | bytes 1769480 | tf_op jit(solution)/shard_map/ppermute | solution.py:42
  96.9 27.9 %copy-start.51 = (bf16[256,1024]{1,0:T(8,128)(2,1)}, bf16[256,1024]{1,0:T(8,128)(2,1)S(1)}, u32[]{:S(2)}) copy-start(bf16[256,1024]{1,0:T(8,128)(2,1)S(1)} %get-tuple-element.199.rest_2_.o_ref) | copy-start | bytes 1572868
  96.9 27.9 %copy-start.32 = (bf16[480,768]{1,0:T(8,128)(2,1)}, bf16[480,768]{1,0:T(8,128)(2,1)S(1)}, u32[]{:S(2)}) copy-start(bf16[480,768]{1,0:T(8,128)(2,1)S(1)} %collective-permute-done.19.rest_4_.rest_12_) | copy-start | bytes 2211844
  96.9 27.9 %collective-permute-start.24 = (bf16[384,768]{1,0:T(8,128)(2,1)S(1)}, bf16[384,768]{1,0:T(8,128)(2,1)S(1)}, u32[]{:S(2)}, u32[]{:S(2)}) collective-permute-start(bf16[384,768]{1,0:T(8,128)(2,1)S(1)} %line_up.5.rest_3_), channel_id=1, source_target_pairs={{0,16},{4,20},{8,24},{12,28},{16,0},{20,4},{24,8},{28,12},{1,17},{... | collective-permute-start | bytes 1769480 | tf_op jit(solution)/shard_map/ppermute | solution.py:42
  97.8 27.0 %copy-start.33 = (bf16[480,768]{1,0:T(8,128)(2,1)}, bf16[480,768]{1,0:T(8,128)(2,1)S(1)}, u32[]{:S(2)}) copy-start(bf16[480,768]{1,0:T(8,128)(2,1)S(1)} %collective-permute-done.20.rest_6_.rest_14_) | copy-start | bytes 2211844
  97.8 27.0 %collective-permute-start.25 = (bf16[384,768]{1,0:T(8,128)(2,1)S(1)}, bf16[384,768]{1,0:T(8,128)(2,1)S(1)}, u32[]{:S(2)}, u32[]{:S(2)}) collective-permute-start(bf16[384,768]{1,0:T(8,128)(2,1)S(1)} %line_up.5.rest_3_), channel_id=1, source_target_pairs={{0,24},{4,28},{8,16},{12,20},{16,8},{20,12},{24,0},{28,4},{1,25},{... | collective-permute-start | bytes 1769480 | tf_op jit(solution)/shard_map/ppermute | solution.py:42
  124.9 4.6 %collective-permute-start.26 = (bf16[4,384,768]{2,1,0:T(8,128)(2,1)S(1)}, bf16[4,384,768]{2,1,0:T(8,128)(2,1)S(1)}, u32[]{:S(2)}, u32[]{:S(2)}) collective-permute-start(bf16[4,384,768]{2,1,0:T(8,128)(2,1)S(1)} %get-tuple-element.208), channel_id=1, source_target_pairs={{0,4},{4,0},{8,12},{12,8},{16,20},{20,16},{24,28},{28,24},{1,5},{5... | collective-permute-start | bytes 7077896 | tf_op jit(solution)/shard_map/ppermute | solution.py:42
  129.5 3.0 %collective-permute-start.27 = (bf16[384,768]{1,0:T(8,128)(2,1)S(1)}, bf16[384,768]{1,0:T(8,128)(2,1)S(1)}, u32[]{:S(2)}, u32[]{:S(2)}) collective-permute-start(bf16[384,768]{1,0:T(8,128)(2,1)S(1)} %line_up.5.rest_3_), channel_id=1, source_target_pairs={{0,4},{4,0},{8,12},{12,8},{16,20},{20,16},{24,28},{28,24},{1,5},{5... | collective-permute-start | bytes 1769480 | tf_op jit(solution)/shard_map/ppermute | solution.py:42
  129.7 3.7 %collective-permute-start.28 = (bf16[384,768]{1,0:T(8,128)(2,1)S(1)}, bf16[384,768]{1,0:T(8,128)(2,1)S(1)}, u32[]{:S(2)}, u32[]{:S(2)}) collective-permute-start(bf16[384,768]{1,0:T(8,128)(2,1)S(1)} %collective-permute-done.23.rest_5_), channel_id=1, source_target_pairs={{0,4},{4,0},{8,12},{12,8},{16,20},{20,16},{24,28},{28,24},{1,5},{5... | collective-permute-start | bytes 1769480 | tf_op jit(solution)/shard_map/ppermute | solution.py:42
  130.0 4.7 %collective-permute-start.29 = (bf16[384,768]{1,0:T(8,128)(2,1)S(1)}, bf16[384,768]{1,0:T(8,128)(2,1)S(1)}, u32[]{:S(2)}, u32[]{:S(2)}) collective-permute-start(bf16[384,768]{1,0:T(8,128)(2,1)S(1)} %collective-permute-done.24.rest_7_), channel_id=1, source_target_pairs={{0,4},{4,0},{8,12},{12,8},{16,20},{20,16},{24,28},{28,24},{1,5},{5... | collective-permute-start | bytes 1769480 | tf_op jit(solution)/shard_map/ppermute | solution.py:42
  130.2 4.6 %collective-permute-start.30 = (bf16[384,768]{1,0:T(8,128)(2,1)S(1)}, bf16[384,768]{1,0:T(8,128)(2,1)S(1)}, u32[]{:S(2)}, u32[]{:S(2)}) collective-permute-start(bf16[384,768]{1,0:T(8,128)(2,1)S(1)} %collective-permute-done.25.rest_9_), channel_id=1, source_target_pairs={{0,4},{4,0},{8,12},{12,8},{16,20},{20,16},{24,28},{28,24},{1,5},{5... | collective-permute-start | bytes 1769480 | tf_op jit(solution)/shard_map/ppermute | solution.py:42
  131.2 34.2 %collective-permute-start.31 = (bf16[384,768]{1,0:T(8,128)(2,1)S(1)}, bf16[384,768]{1,0:T(8,128)(2,1)S(1)}, u32[]{:S(2)}, u32[]{:S(2)}) collective-permute-start(bf16[384,768]{1,0:T(8,128)(2,1)S(1)} %get-tuple-element.226), channel_id=1, source_target_pairs={{0,8},{4,12},{8,0},{12,4},{16,24},{20,28},{24,16},{28,20},{1,9},{5... | collective-permute-start | bytes 1769480 | tf_op jit(solution)/shard_map/ppermute | solution.py:42
  132.5 32.9 %collective-permute-start.32 = (bf16[384,768]{1,0:T(8,128)(2,1)S(1)}, bf16[384,768]{1,0:T(8,128)(2,1)S(1)}, u32[]{:S(2)}, u32[]{:S(2)}) collective-permute-start(bf16[384,768]{1,0:T(8,128)(2,1)S(1)} %get-tuple-element.227), channel_id=1, source_target_pairs={{0,16},{4,20},{8,24},{12,28},{16,0},{20,4},{24,8},{28,12},{1,17},{... | collective-permute-start | bytes 1769480 | tf_op jit(solution)/shard_map/ppermute | solution.py:42
  133.4 32.1 %collective-permute-start.33 = (bf16[384,768]{1,0:T(8,128)(2,1)S(1)}, bf16[384,768]{1,0:T(8,128)(2,1)S(1)}, u32[]{:S(2)}, u32[]{:S(2)}) collective-permute-start(bf16[384,768]{1,0:T(8,128)(2,1)S(1)} %get-tuple-element.228), channel_id=1, source_target_pairs={{0,24},{4,28},{8,16},{12,20},{16,8},{20,12},{24,0},{28,4},{1,25},{... | collective-permute-start | bytes 1769480 | tf_op jit(solution)/shard_map/ppermute | solution.py:42
  165.5 20.9 %collective-permute-start.34 = (bf16[4,480,768]{2,1,0:T(8,128)(2,1)}, bf16[4,480,768]{2,1,0:T(8,128)(2,1)S(1)}, u32[]{:S(2)}, u32[]{:S(2)}) collective-permute-start(bf16[4,480,768]{2,1,0:T(8,128)(2,1)} %get-tuple-element.232), channel_id=1, source_target_pairs={{0,4},{4,0},{8,12},{12,8},{16,20},{20,16},{24,28},{28,24},{1,5},{5... | collective-permute-start | bytes 8847368 | tf_op jit(solution)/shard_map/ppermute | solution.py:42
  166.7 19.6 %collective-permute-start.35 = (bf16[96,768]{1,0:T(8,128)(2,1)S(1)}, bf16[96,768]{1,0:T(8,128)(2,1)S(1)}, u32[]{:S(2)}, u32[]{:S(2)}) collective-permute-start(bf16[96,768]{1,0:T(8,128)(2,1)S(1)} %get-tuple-element.249), channel_id=1, source_target_pairs={{0,1},{1,2},{2,3},{3,0},{4,5},{5,6},{6,7},{7,4},{8,9},{9,10},{10,1... | collective-permute-start | bytes 442376 | tf_op jit(solution)/shard_map/ppermute | solution.py:46
  169.7 16.6 %collective-permute-start.36 = (bf16[96,768]{1,0:T(8,128)(2,1)S(1)}, bf16[96,768]{1,0:T(8,128)(2,1)S(1)}, u32[]{:S(2)}, u32[]{:S(2)}) collective-permute-start(bf16[96,768]{1,0:T(8,128)(2,1)S(1)} %get-tuple-element.250), channel_id=1, source_target_pairs={{0,2},{1,3},{2,0},{3,1},{4,6},{5,7},{6,4},{7,5},{8,10},{9,11},{10,... | collective-permute-start | bytes 442376 | tf_op jit(solution)/shard_map/ppermute | solution.py:46
  170.2 16.1 %collective-permute-start.37 = (bf16[96,768]{1,0:T(8,128)(2,1)S(1)}, bf16[96,768]{1,0:T(8,128)(2,1)S(1)}, u32[]{:S(2)}, u32[]{:S(2)}) collective-permute-start(bf16[96,768]{1,0:T(8,128)(2,1)S(1)} %get-tuple-element.251), channel_id=1, source_target_pairs={{0,3},{1,0},{2,1},{3,2},{4,7},{5,4},{6,5},{7,6},{8,11},{9,8},{10,9... | collective-permute-start | bytes 442376 | tf_op jit(solution)/shard_map/ppermute | solution.py:46
  186.3 27.1 %copy-start.5 = (bf16[256,1024]{1,0:T(8,128)(2,1)}, bf16[256,1024]{1,0:T(8,128)(2,1)S(1)}, u32[]{:S(2)}) copy-start(bf16[256,1024]{1,0:T(8,128)(2,1)S(1)} %get-tuple-element.278.rest_0_) | copy-start | bytes 1572868
  186.3 27.1 %copy-start.6 = (bf16[256,1024]{1,0:T(8,128)(2,1)}, bf16[256,1024]{1,0:T(8,128)(2,1)S(1)}, u32[]{:S(2)}) copy-start(bf16[256,1024]{1,0:T(8,128)(2,1)S(1)} %get-tuple-element.281.rest_3_) | copy-start | bytes 1572868
  186.3 27.1 %copy-start.7 = (bf16[256,1024]{1,0:T(8,128)(2,1)}, bf16[256,1024]{1,0:T(8,128)(2,1)S(1)}, u32[]{:S(2)}) copy-start(bf16[256,1024]{1,0:T(8,128)(2,1)S(1)} %get-tuple-element.284.rest_6_) | copy-start | bytes 1572868
  187.2 35.1 %collective-permute-start.38 = (bf16[480,768]{1,0:T(8,128)(2,1)S(1)}, bf16[480,768]{1,0:T(8,128)(2,1)S(1)}, u32[]{:S(2)}, u32[]{:S(2)}) collective-permute-start(bf16[480,768]{1,0:T(8,128)(2,1)S(1)} %get-tuple-element.274), channel_id=1, source_target_pairs={{0,8},{4,12},{8,0},{12,4},{16,24},{20,28},{24,16},{28,20},{1,9},{5... | collective-permute-start | bytes 2211848 | tf_op jit(solution)/shard_map/ppermute | solution.py:42
  188.4 33.9 %collective-permute-start.39 = (bf16[480,768]{1,0:T(8,128)(2,1)S(1)}, bf16[480,768]{1,0:T(8,128)(2,1)S(1)}, u32[]{:S(2)}, u32[]{:S(2)}) collective-permute-start(bf16[480,768]{1,0:T(8,128)(2,1)S(1)} %get-tuple-element.275), channel_id=1, source_target_pairs={{0,16},{4,20},{8,24},{12,28},{16,0},{20,4},{24,8},{28,12},{1,17},{... | collective-permute-start | bytes 2211848 | tf_op jit(solution)/shard_map/ppermute | solution.py:42
  190.0 32.4 %collective-permute-start.40 = (bf16[480,768]{1,0:T(8,128)(2,1)S(1)}, bf16[480,768]{1,0:T(8,128)(2,1)S(1)}, u32[]{:S(2)}, u32[]{:S(2)}) collective-permute-start(bf16[480,768]{1,0:T(8,128)(2,1)S(1)} %get-tuple-element.276), channel_id=1, source_target_pairs={{0,24},{4,28},{8,16},{12,20},{16,8},{20,12},{24,0},{28,4},{1,25},{... | collective-permute-start | bytes 2211848 | tf_op jit(solution)/shard_map/ppermute | solution.py:42
  222.3 3.9 %collective-permute-start.41 = (bf16[4,96,2432]{2,1,0:T(8,128)(2,1)S(1)}, bf16[4,96,2432]{2,1,0:T(8,128)(2,1)S(1)}, u32[]{:S(2)}, u32[]{:S(2)}) collective-permute-start(bf16[4,96,2432]{2,1,0:T(8,128)(2,1)S(1)} %get-tuple-element.277), channel_id=1, source_target_pairs={{0,4},{4,0},{8,12},{12,8},{16,20},{20,16},{24,28},{28,24},{1,5},{5... | collective-permute-start | bytes 5603336 | tf_op jit(solution)/shard_map/ppermute | solution.py:42
  223.0 9.1 %collective-permute-start.45 = (bf16[120,768]{1,0:T(8,128)(2,1)S(1)}, bf16[120,768]{1,0:T(8,128)(2,1)S(1)}, u32[]{:S(2)}, u32[]{:S(2)}) collective-permute-start(bf16[120,768]{1,0:T(8,128)(2,1)S(1)} %get-tuple-element.296), channel_id=1, source_target_pairs={{0,1},{1,2},{2,3},{3,0},{4,5},{5,6},{6,7},{7,4},{8,9},{9,10},{10,1... | collective-permute-start | bytes 552968 | tf_op jit(solution)/shard_map/ppermute | solution.py:46
  227.6 18.9 %collective-permute-start.42 = (bf16[96,2432]{1,0:T(8,128)(2,1)}, bf16[96,2432]{1,0:T(8,128)(2,1)}, u32[]{:S(2)}, u32[]{:S(2)}) collective-permute-start(bf16[96,2432]{1,0:T(8,128)(2,1)} %get-tuple-element.288), channel_id=1, source_target_pairs={{0,8},{4,12},{8,0},{12,4},{16,24},{20,28},{24,16},{28,20},{1,9},{5... | collective-permute-start | bytes 1400840 | tf_op jit(solution)/shard_map/ppermute | solution.py:42
  228.8 21.9 %collective-permute-start.43 = (bf16[96,2432]{1,0:T(8,128)(2,1)}, bf16[96,2432]{1,0:T(8,128)(2,1)}, u32[]{:S(2)}, u32[]{:S(2)}) collective-permute-start(bf16[96,2432]{1,0:T(8,128)(2,1)} %get-tuple-element.289), channel_id=1, source_target_pairs={{0,16},{4,20},{8,24},{12,28},{16,0},{20,4},{24,8},{28,12},{1,17},{... | collective-permute-start | bytes 1400840 | tf_op jit(solution)/shard_map/ppermute | solution.py:42
  230.4 21.2 %collective-permute-start.44 = (bf16[96,2432]{1,0:T(8,128)(2,1)}, bf16[96,2432]{1,0:T(8,128)(2,1)}, u32[]{:S(2)}, u32[]{:S(2)}) collective-permute-start(bf16[96,2432]{1,0:T(8,128)(2,1)} %get-tuple-element.290), channel_id=1, source_target_pairs={{0,24},{4,28},{8,16},{12,20},{16,8},{20,12},{24,0},{28,4},{1,25},{... | collective-permute-start | bytes 1400840 | tf_op jit(solution)/shard_map/ppermute | solution.py:42
  231.1 15.3 %collective-permute-start.46 = (bf16[120,768]{1,0:T(8,128)(2,1)S(1)}, bf16[120,768]{1,0:T(8,128)(2,1)S(1)}, u32[]{:S(2)}, u32[]{:S(2)}) collective-permute-start(bf16[120,768]{1,0:T(8,128)(2,1)S(1)} %get-tuple-element.297), channel_id=1, source_target_pairs={{0,2},{1,3},{2,0},{3,1},{4,6},{5,7},{6,4},{7,5},{8,10},{9,11},{10,... | collective-permute-start | bytes 552968 | tf_op jit(solution)/shard_map/ppermute | solution.py:46
  232.1 14.3 %collective-permute-start.47 = (bf16[120,768]{1,0:T(8,128)(2,1)S(1)}, bf16[120,768]{1,0:T(8,128)(2,1)S(1)}, u32[]{:S(2)}, u32[]{:S(2)}) collective-permute-start(bf16[120,768]{1,0:T(8,128)(2,1)S(1)} %get-tuple-element.298), channel_id=1, source_target_pairs={{0,3},{1,0},{2,1},{3,2},{4,7},{5,4},{6,5},{7,6},{8,11},{9,8},{10,9... | collective-permute-start | bytes 552968 | tf_op jit(solution)/shard_map/ppermute | solution.py:46
  253.9 10.3 %collective-permute-start.48 = (bf16[24,2432]{1,0:T(8,128)(2,1)}, bf16[24,2432]{1,0:T(8,128)(2,1)S(1)}, u32[]{:S(2)}, u32[]{:S(2)}) collective-permute-start(bf16[24,2432]{1,0:T(8,128)(2,1)} %get-tuple-element.333), channel_id=1, source_target_pairs={{0,1},{1,2},{2,3},{3,0},{4,5},{5,6},{6,7},{7,4},{8,9},{9,10},{10,1... | collective-permute-start | bytes 350216 | tf_op jit(solution)/shard_map/ppermute | solution.py:46
  253.9 11.6 %collective-permute-start.49 = (bf16[24,2432]{1,0:T(8,128)(2,1)S(1)}, bf16[24,2432]{1,0:T(8,128)(2,1)S(1)}, u32[]{:S(2)}, u32[]{:S(2)}) collective-permute-start(bf16[24,2432]{1,0:T(8,128)(2,1)S(1)} %get-tuple-element.335), channel_id=1, source_target_pairs={{0,2},{1,3},{2,0},{3,1},{4,6},{5,7},{6,4},{7,5},{8,10},{9,11},{10,... | collective-permute-start | bytes 350216 | tf_op jit(solution)/shard_map/ppermute | solution.py:46
  256.1 9.4 %collective-permute-start.50 = (bf16[24,2432]{1,0:T(8,128)(2,1)S(1)}, bf16[24,2432]{1,0:T(8,128)(2,1)}, u32[]{:S(2)}, u32[]{:S(2)}) collective-permute-start(bf16[24,2432]{1,0:T(8,128)(2,1)S(1)} %get-tuple-element.334), channel_id=1, source_target_pairs={{0,3},{1,0},{2,1},{3,2},{4,7},{5,4},{6,5},{7,6},{8,11},{9,8},{10,9... | collective-permute-start | bytes 350216 | tf_op jit(solution)/shard_map/ppermute | solution.py:46
  (50 other events, 466.3 us)

commit v3 on v2

--- a/solution.py
+++ b/solution.py
@@ -159,52 +159,60 @@
     )(*arrays)
 
 
-def pieces_kernel(nf, moves, me_ref, *refs):
+def pieces_kernel(nf, groups, me_ref, *refs):
     terms, outs = refs[:-nf], refs[-nf:]
     me = me_ref[0]
-    for row, rows, at in moves:
-        for j in range(nf):
-            here = slice(row + j * rows, row + (j + 1) * rows)
-            value = sum(t[here, :].astype(f32) for t in terms).astype(bf16)
-            for k in range(nf):
-                @pl.when(lax.rem(me + k, nf) == j)
-                def _():
-                    outs[k][at : at + rows, :] = value
-
-
-def pieces(nf, moves, terms):
-    rows = sum(m[1] for m in moves)
-    return pl.pallas_call(
-        functools.partial(pieces_kernel, nf, moves),
+    at = 0
+    for first, last, moves in groups:
+        for row, rows in moves:
+            for j in range(nf):
+                here = slice(row + j * rows, row + (j + 1) * rows)
+                value = sum(t[here, :].astype(f32) for t in terms[first:last]).astype(bf16)
+                for k in range(nf):
+                    @pl.when(lax.rem(me + k, nf) == j)
+                    def _():
+                        outs[k][at : at + rows, :] = value
+            at += rows
+
+
+def pieces(nf, groups):
+    terms, spans, rows = [], [], 0
+    for moves, arrays in groups:
+        spans.append((len(terms), len(terms) + len(arrays), moves))
+        terms += arrays
+        rows += sum(m[1] for m in moves)
+    return pl.pallas_call(
+        functools.partial(pieces_kernel, nf, spans),
         in_specs=[SMEM] + [whole(x.shape) for x in terms],
         out_specs=[whole((rows, D))] * nf,
         out_shape=[jax.ShapeDtypeStruct((rows, D), bf16)] * nf,
         grid=(1,),
-        compiler_params=room(12),
-        cost_estimate=pl.CostEstimate(flops=0, bytes_accessed=6 << 20, transcendentals=0),
+        compiler_params=room(16),
+        cost_estimate=pl.CostEstimate(flops=0, bytes_accessed=10 << 20, transcendentals=0),
         name="pieces",
     )(lax.axis_index("fsdp").astype(jnp.int32).reshape(1), *terms)
 
 
-def finish_kernel(r, q, nf, pick_ref, *refs):
-    halves, (ge_ref, gr_ref, gc_ref) = (refs[:nf], refs[nf : 2 * nf]), refs[2 * nf :]
+def finish_kernel(r, q, pick_ref, *refs):
+    parts, (ge_ref, gr_ref, gc_ref) = refs[:-3], refs[-3:]
     for c in range(4):
         total = jnp.zeros((r, D), f32)
         for h in range(2):
-            at, col = (c // 2) * r, (c % 2) * (D // 2)
-            for p in halves[h]:
+            at, col = h * (2 * r + q) + (c // 2) * r, (c % 2) * (D // 2)
+            for p in parts:
                 total += dot(p[at : at + r, col : col + D // 2], pick_ref[h], NT)
         ge_ref[:, c * D : (c + 1) * D] = total
     for h in range(2):
-        gr_ref[h * q : (h + 1) * q, :] = sum(p[2 * r : 2 * r + q, :].astype(f32) for p in halves[h])
-    gc_ref[...] = sum(p[2 * r + q :, :].astype(f32) for p in halves[1])
-
-
-def finish(r, q, picks, first, second):
+        at = h * (2 * r + q) + 2 * r
+        gr_ref[h * q : (h + 1) * q, :] = sum(p[at : at + q, :].astype(f32) for p in parts)
+    gc_ref[...] = sum(p[2 * (2 * r + q) :, :].astype(f32) for p in parts)
+
+
+def finish(r, q, picks, parts):
     shapes = [(r, 4 * D), (2 * q, D), (r, D)]
-    arrays = (picks, *first, *second)
-    return pl.pallas_call(
-        functools.partial(finish_kernel, r, q, len(first)),
+    arrays = (picks, *parts)
+    return pl.pallas_call(
+        functools.partial(finish_kernel, r, q),
         grid=(1,),
         in_specs=[whole(x.shape) for x in arrays],
         out_specs=[whole(x) for x in shapes],
@@ -271,10 +279,11 @@
     vec = columns.T
     vec_ref[...] = vec[:16]
     low = vec[:16].astype(bf16)
-    for i in range(4):
-        c, row = i % 2, 6 + 2 * (i // 2)
+    for c in range(2):
         parts = [dot(low[:, c * (D // 2) : (c + 1) * (D // 2)], turn_ref[k], NT) for k in range(2)]
-        bias_ref[:, i * D : (i + 1) * D] = parts[0][row : row + 1] + parts[1][row + 1 : row + 2]
+        for h in range(2):
+            row, at = 6 + 2 * h, (2 * h + c) * D
+            bias_ref[:, at : at + D] = parts[0][row : row + 1] + parts[1][row + 1 : row + 2]
     nt_ref[...] = (ht_ref[...] * columns[:, 0:1] + columns[:, 1:2]).astype(bf16)
 
     for c in range(0, 3 * D, BLOCK):
@@ -853,15 +862,12 @@
         me, attended, cotangent, cotangent_t, vecs, bias, f2, f1, state, nd
     )
 
-    cuts = [(0, r, 0), (nf * r, r, r), (2 * nf * r, q, 2 * r)]
-    more = [(nf * (2 * r + q), r, 2 * r + q)]
+    cuts = [(0, r), (nf * r, r), (2 * nf * r, q)]
+    more = [(nf * (2 * r + q), r)]
     m1, s2, k2, grad_t = tie((m1, s2, k2, grad_t))
     got = flip(s2, 1, nd)
-    p1 = pieces(nf, cuts, m1)
-    p1, grad_t = tie((p1, grad_t))
-    p1 = [shift(p, k, nf) if k else p for k, p in enumerate(p1)]
     grads = [attend_back(0, project_t, attended[0], grad_t, sums[0], segment_ids)]
-    got, k2, grads, grad_t, p1 = tie((got, k2, grads, grad_t, p1))
+    got, k2, grads, grad_t = tie((got, k2, grads, grad_t))
     t2 = [add(k2[m], got[m]) for m in range(nd // 2)]
     t2, grad_t = tie((t2, grad_t))
     m2 = meet_plane(t2, nd)
@@ -870,7 +876,7 @@
     grads = [grads[g][j] for j in range(3) for g in range(GROUPS)]
     send, keep = weight_grad(me, nd, normed_t, vecs, gvec, (gbe1, gbe2), turns, grads, w)
     send, m2 = tie((send, m2))
-    p2 = pieces(nf, cuts + more, m2)
+    p2 = pieces(nf, [(cuts, m1), (cuts + more, m2)])
     p2 = [shift(p, k, nf) if k else p for k, p in enumerate(p2)]
     totals = sum_cores(send, keep, nd)
     grads, totals = tie((grads, totals))
@@ -878,7 +884,7 @@
     grad_tokens = project_back(me, tokens, grad_middle, vecs, grads, w)
     grad_tokens, met, p2 = tie((grad_tokens, met, p2))
     gw = sum(v.astype(f32) for v in met).astype(bf16)
-    grad_expander, grad_reducer, grad_combiner = finish(r, q, picks, p1, p2)
+    grad_expander, grad_reducer, grad_combiner = finish(r, q, picks, p2)
     last = scatter_z(gw, [r], nf)
     grad_projector, small = last[:, : 3 * D], last[:, 3 * D :]
     return (

time: 270 us -> 270 us (level)
  waiting for transfers between devices: 31.3 us -> 26.2 us
  starting transfers between devices: 56.2 us -> 59.2 us
    ppermute x33, waiting for transfers between devices: 17.4 us -> 10.8 us  [flip(): return lax.ppermute(value, 'dp', [(i, i ^ bit) for i in range(count)])]
    ppermute x18 -> x15, starting transfers between devices: 31.2 us -> 34.1 us  [shift(): lax.ppermute(value, 'fsdp', [(i, (i + step) % count) for i in range(count)])]
    ppermute x18 -> x15, waiting for transfers between devices: 13.9 us -> 15.5 us  [shift(): lax.ppermute(value, 'fsdp', [(i, (i + step) % count) for i in range(count)])]
    unnamed x126 -> x124, local copies, waits for them, and re-layouts: 11.7 us -> 13 us
    pallas_call x3 -> x2, Pallas kernels: 7.54 us -> 7.76 us  [the longest x1 6.49 us: finish(): pl.pallas_call(functools.partial(finish_kernel, r, q), grid=(1,), in_spec...]
  transfers between devices with their start and end apart: 51 -> 48, of which waited for: 12 -> 14; matrix products, arithmetic and copies ran while one was open for 1% -> 1% of each run, Pallas kernels for 58% -> 58%
where the time goes in v3:
time: 270 us; the launch traced here: 268 us
  Pallas kernels  160 us (59%)
  starting transfers between devices  59.2 us (22%)
  waiting for transfers between devices  26.2 us (10%)
  local copies, waits for them, and re-layouts  15.9 us (6%)
  other arithmetic  5.45 us (2%)
    pallas_call x2, Pallas kernels, ffn_call(): pl.pallas_call(functools.partial(kernel, nd), grid=(ff // D,), in_specs=s...  55.1 us
    ppermute x15, starting transfers between devices, shift(): lax.ppermute(value, 'fsdp', [(i, (i + step) % count) for i in range(count)])  34.1 us
    pallas_call x3, Pallas kernels, attend_back(): pl.pallas_call(attend_back_kernel, grid=(1,), in_specs=[head_rows(group +...  33.5 us
    ppermute x33, starting transfers between devices, flip(): return lax.ppermute(value, 'dp', [(i, i ^ bit) for i in range(count)])  25.1 us
    pallas_call x3, Pallas kernels, attend(): pl.pallas_call(attend_kernel, grid=(1,), in_specs=[head_rows(group + j *...  18.3 us
    ppermute x15, waiting for transfers between devices, shift(): lax.ppermute(value, 'fsdp', [(i, (i + step) % count) for i in range(count)])  15.5 us
    pallas_call x1, Pallas kernels, project_back(): pl.pallas_call(functools.partial(project_back_kernel, nd), grid=(1,), in_...  13.2 us
    unnamed x124, local copies, waits for them, and re-layouts  13 us
  transfers between devices with their start and end apart: 48, of which 14 were waited for; matrix products, arithmetic and copies ran while one was open for 1% of the time, Pallas kernels for 58%

profile of v3, /device:TPU:0, one launch (start us, length us, event | category | flops | bytes accessed | tf_op | source)
XLA Modules:
  0.0 268.4 jit_solution(546748714384163226)
XLA Ops:
  0.7 3.1 %pack.1 = (bf16[24,2432]{1,0:T(8,128)(2,1)}, bf16[120,768]{1,0:T(8,128)(2,1)}, bf16[96,768]{1,0:T(8,128)(2,1)}) custom-call(bf16[24,2304]{1,0:T(8,128)(2,1)} %proj_ref.1, bf16[24,3072]{1,0:T(8,128)(2,1)} %exp_ref.1, bf16[96,768]{1,0:T(8,128)(2,1)} %red_ref.1, bf16[24,768]{1,0:T(8,128)(2,1)} %comb_ref.1, bf16[2,768,384]{2,1,0:T(8,128)(2,1)} %constant.32.clone.pick_ref, ...), custom_call_target="tpu_custom_call" | custom-call | bytes 3145728 | tf_op jit(solution)/shard_map/pack/pallas_call | solution.py:150
  3.7 3.1 %collective-permute-start = (bf16[24,2432]{1,0:T(8,128)(2,1)}, bf16[24,2432]{1,0:T(8,128)(2,1)S(1)}, u32[]{:S(2)}, u32[]{:S(2)}) collective-permute-start(bf16[24,2432]{1,0:T(8,128)(2,1)} %get-tuple-element.157.refs_0_), channel_id=1, source_target_pairs={{0,1},{1,2},{2,3},{3,0},{4,5},{5,6},{6,7},{7,4},{8,9},{9,10},{10,1... | collective-permute-start | bytes 350216 | tf_op jit(solution)/shard_map/ppermute | solution.py:46
  6.8 2.6 collective-permute-start.1
  9.4 1.3 collective-permute-start.2
  10.7 1.4 copy-done.19
  12.2 2.4 prepare.1
  14.6 1.7 copy-done.35
  16.2 1.1 copy-done.37
  17.5 1.6 collective-permute-start.3
  19.1 1.5 collective-permute-start.4
  21.1 2.9 %collective-permute-start.6 = (bf16[120,768]{1,0:T(8,128)(2,1)S(1)}, bf16[120,768]{1,0:T(8,128)(2,1)S(1)}, u32[]{:S(2)}, u32[]{:S(2)}) collective-permute-start(bf16[120,768]{1,0:T(8,128)(2,1)S(1)} %copy-done.15), channel_id=1, source_target_pairs={{0,1},{1,2},{2,3},{3,0},{4,5},{5,6},{6,7},{7,4},{8,9},{9,10},{10,1... | collective-permute-start | bytes 552968 | tf_op jit(solution)/shard_map/ppermute | solution.py:46
  24.0 1.6 collective-permute-start.7
  25.6 5.1 %collective-permute-done.6.refs_1_ = bf16[120,768]{1,0:T(8,128)(2,1)S(1)} collective-permute-done((bf16[120,768]{1,0:T(8,128)(2,1)S(1)}, bf16[120,768]{1,0:T(8,128)(2,1)S(1)}, u32[]{:S(2)}, u32[]{:S(2)}) %collective-permute-start.6) | collective-permute-done | bytes 184352 | tf_op jit(solution)/shard_map/ppermute | solution.py:46
  31.5 5.0 %collective-permute-done.7.refs_2_ = bf16[120,768]{1,0:T(8,128)(2,1)S(1)} collective-permute-done((bf16[120,768]{1,0:T(8,128)(2,1)S(1)}, bf16[120,768]{1,0:T(8,128)(2,1)S(1)}, u32[]{:S(2)}, u32[]{:S(2)}) %collective-permute-start.7) | collective-permute-done | bytes 184352 | tf_op jit(solution)/shard_map/ppermute | solution.py:46
  36.4 1.8 collective-permute-done.8.refs_3_
  38.3 3.1 %collective-permute-done.4.rest_4_.rest_13_ = bf16[96,2432]{1,0:T(8,128)(2,1)} collective-permute-done((bf16[96,2432]{1,0:T(8,128)(2,1)S(1)}, bf16[96,2432]{1,0:T(8,128)(2,1)}, u32[]{:S(2)}, u32[]{:S(2)}) %collective-permute-start.4) | collective-permute-done | bytes 466976 | tf_op jit(solution)/shard_map/ppermute | solution.py:42
  42.4 1.2 collective-permute-start.13
  44.0 1.5 collective-permute-start.14
  45.5 1.2 collective-permute-start.15
  46.7 1.3 copy-done.29
  48.0 1.9 copy-done.36
  49.9 6.9 %project.1 = (bf16[2304,1024]{1,0:T(8,128)(2,1)S(1)}, bf16[768,1024]{1,0:T(8,128)(2,1)S(1)}, f32[16,768]{1,0:T(8,128)S(1)}, f32[1,3072]{1,0:T(1,128)S(1)}) custom-call(s32[1]{0:T(128)} %bitcast.me_ref, f32[768,1024]{1,0:T(8,128)S(1)} %copy-done.36, bf16[2,768,384]{2,1,0:T(8,128)(2,1)S(1)} %copy-done.29, bf16[96,2432]{1,0:T(8,128)(2,1)S(1)} %line_up.3.rest_0_.rest_9_, ...), custom_call_target="tpu_custom_call" | custom-call | flops 3623878656 | bytes 12582912 | tf_op jit(solution)/shard_map/project/pallas_call | solution.py:296
  56.8 3.5 %collective-permute-start.16 = (bf16[96,768]{1,0:T(8,128)(2,1)S(1)}, bf16[96,768]{1,0:T(8,128)(2,1)S(1)}, u32[]{:S(2)}, u32[]{:S(2)}) collective-permute-start(bf16[96,768]{1,0:T(8,128)(2,1)S(1)} %copy-done.16), channel_id=1, source_target_pairs={{0,1},{1,2},{2,3},{3,0},{4,5},{5,6},{6,7},{7,4},{8,9},{9,10},{10,1... | collective-permute-start | bytes 442376 | tf_op jit(solution)/shard_map/ppermute | solution.py:46
  60.3 1.0 collective-permute-start.17
  61.3 6.1 %attend.3 = (bf16[256,1024]{1,0:T(8,128)(2,1)S(1)}, f32[8,1,1024]{2,1,0:T(1,128)S(1)}) custom-call(bf16[2304,1024]{1,0:T(8,128)(2,1)S(1)} %get-tuple-element.185.q_ref.k_ref.v_ref, bf16[2304,1024]{1,0:T(8,128)(2,1)S(1)} %get-tuple-element.185.q_ref.k_ref.v_ref, bf16[2304,1024]{1,0:T(8,128)(2,1)S(1)} %get-tuple-element.185.q_ref.k_ref.v_ref, ...), custom_call_target="tpu_custom_call" | custom-call | flops 7000000000 | bytes 3145728 | tf_op jit(solution)/shard_map/attend/pallas_call | solution.py:383
  68.0 2.8 %collective-permute-start.18 = (bf16[96,768]{1,0:T(8,128)(2,1)S(1)}, bf16[96,768]{1,0:T(8,128)(2,1)S(1)}, u32[]{:S(2)}, u32[]{:S(2)}) collective-permute-start(bf16[96,768]{1,0:T(8,128)(2,1)S(1)} %copy-done.16), channel_id=1, source_target_pairs={{0,3},{1,0},{2,1},{3,2},{4,7},{5,4},{6,5},{7,6},{8,11},{9,8},{10,9... | collective-permute-start | bytes 442376 | tf_op jit(solution)/shard_map/ppermute | solution.py:46
  70.9 6.1 %attend.4 = (bf16[256,1024]{1,0:T(8,128)(2,1)S(1)}, f32[8,1,1024]{2,1,0:T(1,128)S(1)}) custom-call(bf16[2304,1024]{1,0:T(8,128)(2,1)S(1)} %get-tuple-element.185.q_ref.k_ref.v_ref, bf16[2304,1024]{1,0:T(8,128)(2,1)S(1)} %get-tuple-element.185.q_ref.k_ref.v_ref, bf16[2304,1024]{1,0:T(8,128)(2,1)S(1)} %get-tuple-element.185.q_ref.k_ref.v_ref, ...), custom_call_target="tpu_custom_call" | custom-call | flops 7000000000 | bytes 3145728 | tf_op jit(solution)/shard_map/attend/pallas_call | solution.py:383
  77.0 1.3 collective-permute-done.14.rest_7_.rest_15_
  79.4 10.1 %line_up.5.rest_3_ = bf16[384,768]{1,0:T(8,128)(2,1)S(1)} custom-call(s32[1]{0:T(128)} %bitcast.1.me_ref, bf16[96,768]{1,0:T(8,128)(2,1)S(1)} %copy-done.16, bf16[96,768]{1,0:T(8,128)(2,1)S(1)} %collective-permute-done.16.refs_1_, bf16[96,768]{1,0:T(8,128)(2,1)S(1)} %collective-permute-done.17.refs_2_, bf16[96,768]{1,0:T(8,128)(2,1)S(1)} %collective-permute-done.18.refs_3_), custom_call_target="tpu_custom_call" | custom-call | bytes 4194304 | tf_op jit(solution)/shard_map/line_up/pallas_call | solution.py:71
  89.5 1.3 collective-permute-start.23
  90.8 6.1 %attend.5 = (bf16[256,1024]{1,0:T(8,128)(2,1)S(1)}, f32[8,1,1024]{2,1,0:T(1,128)S(1)}) custom-call(bf16[2304,1024]{1,0:T(8,128)(2,1)S(1)} %get-tuple-element.185.q_ref.k_ref.v_ref, bf16[2304,1024]{1,0:T(8,128)(2,1)S(1)} %get-tuple-element.185.q_ref.k_ref.v_ref, bf16[2304,1024]{1,0:T(8,128)(2,1)S(1)} %get-tuple-element.185.q_ref.k_ref.v_ref, ...), custom_call_target="tpu_custom_call" | custom-call | flops 7000000000 | bytes 3145728 | tf_op jit(solution)/shard_map/attend/pallas_call | solution.py:383
  97.0 0.9 collective-permute-start.24
  97.9 1.4 collective-permute-start.25
  99.4 25.4 %ffn_first.1 = (f32[1024,768]{1,0:T(8,128)}, bf16[1024,768]{1,0:T(8,128)(2,1)S(1)}, f32[1024,768]{1,0:T(8,128)}, f32[1024,768]{1,0:T(8,128)}, bf16[4,384,768]{2,...) custom-call(s32[1]{0:T(128)} %bitcast.me_ref, bf16[1024,768]{1,0:T(8,128)(2,1)S(1)} %copy-done.2, ...), custom_call_target="tpu_custom_call" | custom-call | flops 14495514624 | bytes 20971520 | tf_op jit(solution)/shard_map/ffn_first/pallas_call | solution.py:675
  125.1 4.5 %collective-permute-done.26 = bf16[4,384,768]{2,1,0:T(8,128)(2,1)S(1)} collective-permute-done((bf16[4,384,768]{2,1,0:T(8,128)(2,1)S(1)}, bf16[4,384,768]{2,1,0:T(8,128)(2,1)S(1)}, u32[]{:S(2)}, u32[]{:S(2)}) %collective-permute-start.26) | collective-permute-done | bytes 2359328 | tf_op jit(solution)/shard_map/ppermute | solution.py:42
  131.3 1.3 collective-permute-start.31
  132.6 0.9 collective-permute-start.32
  133.4 1.5 collective-permute-start.33
  136.0 29.7 %ffn_last.1 = (bf16[1024,768]{1,0:T(8,128)(2,1)}, f32[1024,768]{1,0:T(8,128)}, bf16[768,1024]{1,0:T(8,128)(2,1)}, bf16[4,480,768]{2,1,0:T(8,128)(2,1)}, bf16[4,4...) custom-call(s32[1]{0:T(128)} %bitcast.me_ref, bf16[1024,768]{1,0:T(8,128)(2,1)} %cot_ref.4, ...), custom_call_target="tpu_custom_call" | custom-call | flops 14495514624 | bytes 20971520 | tf_op jit(solution)/shard_map/ffn_last/pallas_call | solution.py:675
  165.9 2.3 copy-done.34
  168.2 1.4 copy-done.47
  169.6 11.0 %attend_back.3 = (bf16[256,1024]{1,0:T(8,128)(2,1)S(1)}, bf16[256,1024]{1,0:T(8,128)(2,1)S(1)}, bf16[256,1024]{1,0:T(8,128)(2,1)S(1)}) custom-call(bf16[2304,1024]{1,0:T(8,128)(2,1)S(1)} %copy-done.34, bf16[2304,1024]{1,0:T(8,128)(2,1)S(1)} %copy-done.34, bf16[2304,1024]{1,0:T(8,128)(2,1)S(1)} %copy-done.34, bf16[256,1024]{1,0:T(8,128)(2,1)S(1)} %copy-done.43, ...), custom_call_target="tpu_custom_call" | custom-call | flops 14000000000 | bytes 5242880 | tf_op jit(solution)/shard_map/attend_back/pallas_call | solution.py:469
  181.4 1.5 collective-permute-start.35
  183.5 1.5 collective-permute-start.37
  185.0 11.2 %attend_back.5 = (bf16[256,1024]{1,0:T(8,128)(2,1)S(1)}, bf16[256,1024]{1,0:T(8,128)(2,1)S(1)}, bf16[256,1024]{1,0:T(8,128)(2,1)S(1)}) custom-call(bf16[2304,1024]{1,0:T(8,128)(2,1)S(1)} %copy-done.34, bf16[2304,1024]{1,0:T(8,128)(2,1)S(1)} %copy-done.34, bf16[2304,1024]{1,0:T(8,128)(2,1)S(1)} %copy-done.34, bf16[256,1024]{1,0:T(8,128)(2,1)S(1)} %copy-done.45, ...), custom_call_target="tpu_custom_call" | custom-call | flops 14000000000 | bytes 5242880 | tf_op jit(solution)/shard_map/attend_back/pallas_call | solution.py:469
  196.3 11.3 %attend_back.4 = (bf16[256,1024]{1,0:T(8,128)(2,1)S(1)}, bf16[256,1024]{1,0:T(8,128)(2,1)S(1)}, bf16[256,1024]{1,0:T(8,128)(2,1)S(1)}) custom-call(bf16[2304,1024]{1,0:T(8,128)(2,1)S(1)} %copy-done.34, bf16[2304,1024]{1,0:T(8,128)(2,1)S(1)} %copy-done.34, bf16[2304,1024]{1,0:T(8,128)(2,1)S(1)} %copy-done.34, bf16[256,1024]{1,0:T(8,128)(2,1)S(1)} %copy-done.41, ...), custom_call_target="tpu_custom_call" | custom-call | flops 14000000000 | bytes 5242880 | tf_op jit(solution)/shard_map/attend_back/pallas_call | solution.py:469
  207.7 9.1 %weight_grad.1 = (bf16[4,96,2432]{2,1,0:T(8,128)(2,1)S(1)}, bf16[4,96,2432]{2,1,0:T(8,128)(2,1)S(1)}) custom-call(s32[1]{0:T(128)} %bitcast.me_ref, bf16[768,1024]{1,0:T(8,128)(2,1)S(1)} %copy-done.32, f32[16,768]{1,0:T(8,128)S(1)} %get-tuple-element.172.vec_ref, f32[8,768]{1,0:T(8,128)S(1)} %get-tuple-element.242.gv_ref, ...), custom_call_target="tpu_custom_call" | custom-call | flops 3623878656 | bytes 10485760 | tf_op jit(solution)/shard_map/weight_grad/pallas_call | solution.py:762
  217.4 1.3 pieces.1
  218.7 3.1 %collective-permute-start.42 = (bf16[216,768]{1,0:T(8,128)(2,1)S(1)}, bf16[216,768]{1,0:T(8,128)(2,1)S(1)}, u32[]{:S(2)}, u32[]{:S(2)}) collective-permute-start(bf16[216,768]{1,0:T(8,128)(2,1)S(1)} %get-tuple-element.274), channel_id=1, source_target_pairs={{0,1},{1,2},{2,3},{3,0},{4,5},{5,6},{6,7},{7,4},{8,9},{9,10},{10,1... | collective-permute-start | bytes 995336 | tf_op jit(solution)/shard_map/ppermute | solution.py:46
  221.8 1.6 fusion.11
  223.4 1.0 collective-permute-start.39
  224.4 0.9 collective-permute-start.40
  225.3 1.5 collective-permute-start.41
  226.9 2.6 collective-permute-start.43
  229.4 1.4 collective-permute-done.42.refs_1_
  230.8 1.1 collective-permute-start.44
  231.9 13.2 %project_back.1 = f32[1024,768]{1,0:T(8,128)} custom-call(s32[1]{0:T(128)} %bitcast.me_ref, bf16[1024,768]{1,0:T(8,128)(2,1)} %x_ref.4, f32[1024,768]{1,0:T(8,128)} %get-tuple-element.211.gm_ref, f32[16,768]{1,0:T(8,128)} %copy-done.18, bf16[256,1024]{1,0:T(8,128)(2,1)} %copy-done.5, bf16[256,1024]{1,0:T(8,128)(2,1)} %copy-done.11, ...), custom_call_target="tpu_custom_call" | custom-call | flops 3623878656 | bytes 20971520 | tf_op jit(solution)/shard_map/project_back/pallas_call | solution.py:803
  246.3 0.9 collective-permute-done.40
  247.3 1.5 add_convert_fusion.8
  249.5 5.4 %collective-permute-start.45 = (bf16[24,2432]{1,0:T(8,128)(2,1)}, bf16[24,2432]{1,0:T(8,128)(2,1)S(1)}, u32[]{:S(2)}, u32[]{:S(2)}) collective-permute-start(bf16[24,2432]{1,0:T(8,128)(2,1)} %get-tuple-element.307), channel_id=1, source_target_pairs={{0,1},{1,2},{2,3},{3,0},{4,5},{5,6},{6,7},{7,4},{8,9},{9,10},{10,1... | collective-permute-start | bytes 350216 | tf_op jit(solution)/shard_map/ppermute | solution.py:46
  254.9 2.2 collective-permute-start.46
  257.3 6.5 %finish.1 = (f32[24,3072]{1,0:T(8,128)}, f32[96,768]{1,0:T(8,128)}, f32[24,768]{1,0:T(8,128)}) custom-call(bf16[2,768,384]{2,1,0:T(8,128)(2,1)S(1)} %copy-done, bf16[216,768]{1,0:T(8,128)(2,1)S(1)} %get-tuple-element.282.refs_0_, bf16[216,768]{1,0:T(8,128)(2,1)S(1)} %collective-permute-done.42.refs_1_, bf16[216,768]{1,0:T(8,128)(2,1)S(1)} %collective-permute-done.43.refs_2_, ...), custom_call_target="tpu_custom_call" | custom-call | bytes 3145728 | tf_op jit(solution)/shard_map/finish/pallas_call | solution.py:214
  263.8 0.8 collective-permute-done.46
  264.8 1.0 convert_add_fusion
  (185 shorter events, 13.9 us)
Async XLA Ops:
  3.7 13.7 %collective-permute-start = (bf16[24,2432]{1,0:T(8,128)(2,1)}, bf16[24,2432]{1,0:T(8,128)(2,1)S(1)}, u32[]{:S(2)}, u32[]{:S(2)}) collective-permute-start(bf16[24,2432]{1,0:T(8,128)(2,1)} %get-tuple-element.157.refs_0_), channel_id=1, source_target_pairs={{0,1},{1,2},{2,3},{3,0},{4,5},{5,6},{6,7},{7,4},{8,9},{9,10},{10,1... | collective-permute-start | bytes 350216 | tf_op jit(solution)/shard_map/ppermute | solution.py:46
  6.8 10.6 %collective-permute-start.1 = (bf16[24,2432]{1,0:T(8,128)(2,1)}, bf16[24,2432]{1,0:T(8,128)(2,1)S(1)}, u32[]{:S(2)}, u32[]{:S(2)}) collective-permute-start(bf16[24,2432]{1,0:T(8,128)(2,1)} %get-tuple-element.157.refs_0_), channel_id=1, source_target_pairs={{0,2},{1,3},{2,0},{3,1},{4,6},{5,7},{6,4},{7,5},{8,10},{9,11},{10,... | collective-permute-start | bytes 350216 | tf_op jit(solution)/shard_map/ppermute | solution.py:46
  9.4 8.0 %collective-permute-start.2 = (bf16[24,2432]{1,0:T(8,128)(2,1)}, bf16[24,2432]{1,0:T(8,128)(2,1)S(1)}, u32[]{:S(2)}, u32[]{:S(2)}) collective-permute-start(bf16[24,2432]{1,0:T(8,128)(2,1)} %get-tuple-element.157.refs_0_), channel_id=1, source_target_pairs={{0,3},{1,0},{2,1},{3,2},{4,7},{5,4},{6,5},{7,6},{8,11},{9,8},{10,9... | collective-permute-start | bytes 350216 | tf_op jit(solution)/shard_map/ppermute | solution.py:46
  17.5 190.1 %copy-start.1 = (bf16[96,2432]{1,0:T(8,128)(2,1)}, bf16[96,2432]{1,0:T(8,128)(2,1)S(1)}, u32[]{:S(2)}) copy-start(bf16[96,2432]{1,0:T(8,128)(2,1)S(1)} %line_up.3.rest_0_.rest_9_) | copy-start | bytes 1400836
  17.5 20.8 %collective-permute-start.3 = (bf16[96,2432]{1,0:T(8,128)(2,1)S(1)}, bf16[96,2432]{1,0:T(8,128)(2,1)S(1)}, u32[]{:S(2)}, u32[]{:S(2)}) collective-permute-start(bf16[96,2432]{1,0:T(8,128)(2,1)S(1)} %line_up.3.rest_0_.rest_9_), channel_id=1, source_target_pairs={{0,8},{4,12},{8,0},{12,4},{16,24},{20,28},{24,16},{28,20},{1,9},{5... | collective-permute-start | bytes 1400840 | tf_op jit(solution)/shard_map/ppermute | solution.py:42
  19.1 22.3 %collective-permute-start.4 = (bf16[96,2432]{1,0:T(8,128)(2,1)S(1)}, bf16[96,2432]{1,0:T(8,128)(2,1)}, u32[]{:S(2)}, u32[]{:S(2)}) collective-permute-start(bf16[96,2432]{1,0:T(8,128)(2,1)S(1)} %line_up.3.rest_0_.rest_9_), channel_id=1, source_target_pairs={{0,16},{4,20},{8,24},{12,28},{16,0},{20,4},{24,8},{28,12},{1,17},{... | collective-permute-start | bytes 1400840 | tf_op jit(solution)/shard_map/ppermute | solution.py:42
  20.6 20.8 %collective-permute-start.5 = (bf16[96,2432]{1,0:T(8,128)(2,1)S(1)}, bf16[96,2432]{1,0:T(8,128)(2,1)}, u32[]{:S(2)}, u32[]{:S(2)}) collective-permute-start(bf16[96,2432]{1,0:T(8,128)(2,1)S(1)} %line_up.3.rest_0_.rest_9_), channel_id=1, source_target_pairs={{0,24},{4,28},{8,16},{12,20},{16,8},{20,12},{24,0},{28,4},{1,25},{... | collective-permute-start | bytes 1400840 | tf_op jit(solution)/shard_map/ppermute | solution.py:42
  21.1 9.6 %collective-permute-start.6 = (bf16[120,768]{1,0:T(8,128)(2,1)S(1)}, bf16[120,768]{1,0:T(8,128)(2,1)S(1)}, u32[]{:S(2)}, u32[]{:S(2)}) collective-permute-start(bf16[120,768]{1,0:T(8,128)(2,1)S(1)} %copy-done.15), channel_id=1, source_target_pairs={{0,1},{1,2},{2,3},{3,0},{4,5},{5,6},{6,7},{7,4},{8,9},{9,10},{10,1... | collective-permute-start | bytes 552968 | tf_op jit(solution)/shard_map/ppermute | solution.py:46
  24.0 12.5 %collective-permute-start.7 = (bf16[120,768]{1,0:T(8,128)(2,1)S(1)}, bf16[120,768]{1,0:T(8,128)(2,1)S(1)}, u32[]{:S(2)}, u32[]{:S(2)}) collective-permute-start(bf16[120,768]{1,0:T(8,128)(2,1)S(1)} %copy-done.15), channel_id=1, source_target_pairs={{0,2},{1,3},{2,0},{3,1},{4,6},{5,7},{6,4},{7,5},{8,10},{9,11},{10,... | collective-permute-start | bytes 552968 | tf_op jit(solution)/shard_map/ppermute | solution.py:46
  30.7 7.5 %collective-permute-start.8 = (bf16[120,768]{1,0:T(8,128)(2,1)S(1)}, bf16[120,768]{1,0:T(8,128)(2,1)S(1)}, u32[]{:S(2)}, u32[]{:S(2)}) collective-permute-start(bf16[120,768]{1,0:T(8,128)(2,1)S(1)} %copy-done.15), channel_id=1, source_target_pairs={{0,3},{1,0},{2,1},{3,2},{4,7},{5,4},{6,5},{7,6},{8,11},{9,8},{10,9... | collective-permute-start | bytes 552968 | tf_op jit(solution)/shard_map/ppermute | solution.py:46
  38.3 61.0 %copy-start.3 = (bf16[480,768]{1,0:T(8,128)(2,1)}, bf16[480,768]{1,0:T(8,128)(2,1)S(1)}, u32[]{:S(2)}) copy-start(bf16[480,768]{1,0:T(8,128)(2,1)S(1)} %line_up.4.rest_3_.rest_11_) | copy-start | bytes 2211844
  38.3 169.3 %copy-start.14 = (bf16[96,2432]{1,0:T(8,128)(2,1)}, bf16[96,2432]{1,0:T(8,128)(2,1)S(1)}, u32[]{:S(2)}) copy-start(bf16[96,2432]{1,0:T(8,128)(2,1)S(1)} %collective-permute-done.3.rest_2_.rest_11_) | copy-start | bytes 1400836
  41.4 2.6 collective-permute-start.10
  41.4 4.1 %collective-permute-start.11 = (bf16[96,2432]{1,0:T(8,128)(2,1)}, bf16[96,2432]{1,0:T(8,128)(2,1)}, u32[]{:S(2)}, u32[]{:S(2)}) collective-permute-start(bf16[96,2432]{1,0:T(8,128)(2,1)} %collective-permute-done.4.rest_4_.rest_13_), channel_id=1, source_target_pairs={{0,4},{4,0},{8,12},{12,8},{16,20},{20,16},{24,28},{28,24},{1,5},{5... | collective-permute-start | bytes 1400840 | tf_op jit(solution)/shard_map/ppermute | solution.py:42
  41.9 4.8 %collective-permute-start.12 = (bf16[96,2432]{1,0:T(8,128)(2,1)}, bf16[96,2432]{1,0:T(8,128)(2,1)}, u32[]{:S(2)}, u32[]{:S(2)}) collective-permute-start(bf16[96,2432]{1,0:T(8,128)(2,1)} %collective-permute-done.5.rest_6_.rest_15_), channel_id=1, source_target_pairs={{0,4},{4,0},{8,12},{12,8},{16,20},{20,16},{24,28},{28,24},{1,5},{5... | collective-permute-start | bytes 1400840 | tf_op jit(solution)/shard_map/ppermute | solution.py:42
  41.9 4.8 %collective-permute-start.9 = (bf16[96,2432]{1,0:T(8,128)(2,1)S(1)}, bf16[96,2432]{1,0:T(8,128)(2,1)}, u32[]{:S(2)}, u32[]{:S(2)}) collective-permute-start(bf16[96,2432]{1,0:T(8,128)(2,1)S(1)} %line_up.3.rest_0_.rest_9_), channel_id=1, source_target_pairs={{0,4},{4,0},{8,12},{12,8},{16,20},{20,16},{24,28},{28,24},{1,5},{5... | collective-permute-start | bytes 1400840 | tf_op jit(solution)/shard_map/ppermute | solution.py:42
  42.4 34.6 %collective-permute-start.13 = (bf16[480,768]{1,0:T(8,128)(2,1)S(1)}, bf16[480,768]{1,0:T(8,128)(2,1)S(1)}, u32[]{:S(2)}, u32[]{:S(2)}) collective-permute-start(bf16[480,768]{1,0:T(8,128)(2,1)S(1)} %line_up.4.rest_3_.rest_11_), channel_id=1, source_target_pairs={{0,8},{4,12},{8,0},{12,4},{16,24},{20,28},{24,16},{28,20},{1,9},{5... | collective-permute-start | bytes 2211848 | tf_op jit(solution)/shard_map/ppermute | solution.py:42
  44.0 34.3 %collective-permute-start.14 = (bf16[480,768]{1,0:T(8,128)(2,1)S(1)}, bf16[480,768]{1,0:T(8,128)(2,1)S(1)}, u32[]{:S(2)}, u32[]{:S(2)}) collective-permute-start(bf16[480,768]{1,0:T(8,128)(2,1)S(1)} %line_up.4.rest_3_.rest_11_), channel_id=1, source_target_pairs={{0,16},{4,20},{8,24},{12,28},{16,0},{20,4},{24,8},{28,12},{1,17},{... | collective-permute-start | bytes 2211848 | tf_op jit(solution)/shard_map/ppermute | solution.py:42
  45.5 32.8 %collective-permute-start.15 = (bf16[480,768]{1,0:T(8,128)(2,1)S(1)}, bf16[480,768]{1,0:T(8,128)(2,1)S(1)}, u32[]{:S(2)}, u32[]{:S(2)}) collective-permute-start(bf16[480,768]{1,0:T(8,128)(2,1)S(1)} %line_up.4.rest_3_.rest_11_), channel_id=1, source_target_pairs={{0,24},{4,28},{8,16},{12,20},{16,8},{20,12},{24,0},{28,4},{1,25},{... | collective-permute-start | bytes 2211848 | tf_op jit(solution)/shard_map/ppermute | solution.py:42
  56.8 34.1 %copy-start.33 = (bf16[2304,1024]{1,0:T(8,128)(2,1)}, bf16[2304,1024]{1,0:T(8,128)(2,1)S(1)}, u32[]{:S(2)}) copy-start(bf16[2304,1024]{1,0:T(8,128)(2,1)S(1)} %get-tuple-element.185.q_ref.k_ref.v_ref) | copy-start | bytes 14155780
  56.8 150.9 %copy-start.18 = (f32[16,768]{1,0:T(8,128)}, f32[16,768]{1,0:T(8,128)S(1)}, u32[]{:S(2)}) copy-start(f32[16,768]{1,0:T(8,128)S(1)} %get-tuple-element.172.vec_ref) | copy-start | bytes 147460
  56.8 11.2 %collective-permute-start.16 = (bf16[96,768]{1,0:T(8,128)(2,1)S(1)}, bf16[96,768]{1,0:T(8,128)(2,1)S(1)}, u32[]{:S(2)}, u32[]{:S(2)}) collective-permute-start(bf16[96,768]{1,0:T(8,128)(2,1)S(1)} %copy-done.16), channel_id=1, source_target_pairs={{0,1},{1,2},{2,3},{3,0},{4,5},{5,6},{6,7},{7,4},{8,9},{9,10},{10,1... | collective-permute-start | bytes 442376 | tf_op jit(solution)/shard_map/ppermute | solution.py:46
  60.3 16.7 %collective-permute-start.17 = (bf16[96,768]{1,0:T(8,128)(2,1)S(1)}, bf16[96,768]{1,0:T(8,128)(2,1)S(1)}, u32[]{:S(2)}, u32[]{:S(2)}) collective-permute-start(bf16[96,768]{1,0:T(8,128)(2,1)S(1)} %copy-done.16), channel_id=1, source_target_pairs={{0,2},{1,3},{2,0},{3,1},{4,6},{5,7},{6,4},{7,5},{8,10},{9,11},{10,... | collective-permute-start | bytes 442376 | tf_op jit(solution)/shard_map/ppermute | solution.py:46
  68.0 31.3 %copy-start.42 = (bf16[256,1024]{1,0:T(8,128)(2,1)}, bf16[256,1024]{1,0:T(8,128)(2,1)S(1)}, u32[]{:S(2)}) copy-start(bf16[256,1024]{1,0:T(8,128)(2,1)S(1)} %get-tuple-element.175.rest_0_.o_ref) | copy-start | bytes 1572868
  68.0 9.0 %collective-permute-start.18 = (bf16[96,768]{1,0:T(8,128)(2,1)S(1)}, bf16[96,768]{1,0:T(8,128)(2,1)S(1)}, u32[]{:S(2)}, u32[]{:S(2)}) collective-permute-start(bf16[96,768]{1,0:T(8,128)(2,1)S(1)} %copy-done.16), channel_id=1, source_target_pairs={{0,3},{1,0},{2,1},{3,2},{4,7},{5,4},{6,5},{7,6},{8,11},{9,8},{10,9... | collective-permute-start | bytes 442376 | tf_op jit(solution)/shard_map/ppermute | solution.py:46
  78.3 18.6 %collective-permute-start.19 = (bf16[480,768]{1,0:T(8,128)(2,1)S(1)}, bf16[480,768]{1,0:T(8,128)(2,1)S(1)}, u32[]{:S(2)}, u32[]{:S(2)}) collective-permute-start(bf16[480,768]{1,0:T(8,128)(2,1)S(1)} %line_up.4.rest_3_.rest_11_), channel_id=1, source_target_pairs={{0,4},{4,0},{8,12},{12,8},{16,20},{20,16},{24,28},{28,24},{1,5},{5... | collective-permute-start | bytes 2211848 | tf_op jit(solution)/shard_map/ppermute | solution.py:42
  78.4 19.5 %collective-permute-start.20 = (bf16[480,768]{1,0:T(8,128)(2,1)S(1)}, bf16[480,768]{1,0:T(8,128)(2,1)S(1)}, u32[]{:S(2)}, u32[]{:S(2)}) collective-permute-start(bf16[480,768]{1,0:T(8,128)(2,1)S(1)} %collective-permute-done.13.rest_5_.rest_13_), channel_id=1, source_target_pairs={{0,4},{4,0},{8,12},{12,8},{16,20},{20,16},{24,28},{28,24},{1,5},{5... | collective-permute-start | bytes 2211848 | tf_op jit(solution)/shard_map/ppermute | solution.py:42
  78.9 20.4 %collective-permute-start.21 = (bf16[480,768]{1,0:T(8,128)(2,1)S(1)}, bf16[480,768]{1,0:T(8,128)(2,1)S(1)}, u32[]{:S(2)}, u32[]{:S(2)}) collective-permute-start(bf16[480,768]{1,0:T(8,128)(2,1)S(1)} %collective-permute-done.14.rest_7_.rest_15_), channel_id=1, source_target_pairs={{0,4},{4,0},{8,12},{12,8},{16,20},{20,16},{24,28},{28,24},{1,5},{5... | collective-permute-start | bytes 2211848 | tf_op jit(solution)/shard_map/ppermute | solution.py:42
  79.0 20.3 %collective-permute-start.22 = (bf16[480,768]{1,0:T(8,128)(2,1)S(1)}, bf16[480,768]{1,0:T(8,128)(2,1)S(1)}, u32[]{:S(2)}, u32[]{:S(2)}) collective-permute-start(bf16[480,768]{1,0:T(8,128)(2,1)S(1)} %collective-permute-done.15.rest_9_.rest_17_), channel_id=1, source_target_pairs={{0,4},{4,0},{8,12},{12,8},{16,20},{20,16},{24,28},{28,24},{1,5},{5... | collective-permute-start | bytes 2211848 | tf_op jit(solution)/shard_map/ppermute | solution.py:42
  89.5 40.1 %copy-start.4 = (bf16[384,768]{1,0:T(8,128)(2,1)}, bf16[384,768]{1,0:T(8,128)(2,1)S(1)}, u32[]{:S(2)}) copy-start(bf16[384,768]{1,0:T(8,128)(2,1)S(1)} %line_up.5.rest_3_) | copy-start | bytes 1769476
  89.5 35.4 %collective-permute-start.23 = (bf16[384,768]{1,0:T(8,128)(2,1)S(1)}, bf16[384,768]{1,0:T(8,128)(2,1)S(1)}, u32[]{:S(2)}, u32[]{:S(2)}) collective-permute-start(bf16[384,768]{1,0:T(8,128)(2,1)S(1)} %line_up.5.rest_3_), channel_id=1, source_target_pairs={{0,8},{4,12},{8,0},{12,4},{16,24},{20,28},{24,16},{28,20},{1,9},{5... | collective-permute-start | bytes 1769480 | tf_op jit(solution)/shard_map/ppermute | solution.py:42
  97.0 27.9 %copy-start.44 = (bf16[256,1024]{1,0:T(8,128)(2,1)}, bf16[256,1024]{1,0:T(8,128)(2,1)S(1)}, u32[]{:S(2)}) copy-start(bf16[256,1024]{1,0:T(8,128)(2,1)S(1)} %get-tuple-element.186.rest_2_.o_ref) | copy-start | bytes 1572868
  97.0 27.9 %copy-start.53 = (f32[8,1,1024]{2,1,0:T(1,128)}, f32[8,1,1024]{2,1,0:T(1,128)S(1)}, u32[]{:S(2)}) copy-start(f32[8,1,1024]{2,1,0:T(1,128)S(1)} %get-tuple-element.233.lse_ref) | copy-start | bytes 98308
  97.0 27.9 %copy-start.24 = (bf16[480,768]{1,0:T(8,128)(2,1)}, bf16[480,768]{1,0:T(8,128)(2,1)S(1)}, u32[]{:S(2)}) copy-start(bf16[480,768]{1,0:T(8,128)(2,1)S(1)} %collective-permute-done.19.rest_4_.rest_12_) | copy-start | bytes 2211844
  97.0 27.9 %collective-permute-start.24 = (bf16[384,768]{1,0:T(8,128)(2,1)S(1)}, bf16[384,768]{1,0:T(8,128)(2,1)S(1)}, u32[]{:S(2)}, u32[]{:S(2)}) collective-permute-start(bf16[384,768]{1,0:T(8,128)(2,1)S(1)} %line_up.5.rest_3_), channel_id=1, source_target_pairs={{0,16},{4,20},{8,24},{12,28},{16,0},{20,4},{24,8},{28,12},{1,17},{... | collective-permute-start | bytes 1769480 | tf_op jit(solution)/shard_map/ppermute | solution.py:42
  97.9 27.0 %copy-start.25 = (bf16[480,768]{1,0:T(8,128)(2,1)}, bf16[480,768]{1,0:T(8,128)(2,1)S(1)}, u32[]{:S(2)}) copy-start(bf16[480,768]{1,0:T(8,128)(2,1)S(1)} %collective-permute-done.20.rest_6_.rest_14_) | copy-start | bytes 2211844
  97.9 27.0 %collective-permute-start.25 = (bf16[384,768]{1,0:T(8,128)(2,1)S(1)}, bf16[384,768]{1,0:T(8,128)(2,1)S(1)}, u32[]{:S(2)}, u32[]{:S(2)}) collective-permute-start(bf16[384,768]{1,0:T(8,128)(2,1)S(1)} %line_up.5.rest_3_), channel_id=1, source_target_pairs={{0,24},{4,28},{8,16},{12,20},{16,8},{20,12},{24,0},{28,4},{1,25},{... | collective-permute-start | bytes 1769480 | tf_op jit(solution)/shard_map/ppermute | solution.py:42
  99.3 25.5 %copy-start.27 = (bf16[480,768]{1,0:T(8,128)(2,1)}, bf16[480,768]{1,0:T(8,128)(2,1)S(1)}, u32[]{:S(2)}) copy-start(bf16[480,768]{1,0:T(8,128)(2,1)S(1)} %collective-permute-done.22.rest_10_.rest_18_) | copy-start | bytes 2211844
  125.0 4.6 %collective-permute-start.26 = (bf16[4,384,768]{2,1,0:T(8,128)(2,1)S(1)}, bf16[4,384,768]{2,1,0:T(8,128)(2,1)S(1)}, u32[]{:S(2)}, u32[]{:S(2)}) collective-permute-start(bf16[4,384,768]{2,1,0:T(8,128)(2,1)S(1)} %get-tuple-element.195), channel_id=1, source_target_pairs={{0,4},{4,0},{8,12},{12,8},{16,20},{20,16},{24,28},{28,24},{1,5},{5... | collective-permute-start | bytes 7077896 | tf_op jit(solution)/shard_map/ppermute | solution.py:42
  129.6 3.0 %collective-permute-start.27 = (bf16[384,768]{1,0:T(8,128)(2,1)S(1)}, bf16[384,768]{1,0:T(8,128)(2,1)}, u32[]{:S(2)}, u32[]{:S(2)}) collective-permute-start(bf16[384,768]{1,0:T(8,128)(2,1)S(1)} %line_up.5.rest_3_), channel_id=1, source_target_pairs={{0,4},{4,0},{8,12},{12,8},{16,20},{20,16},{24,28},{28,24},{1,5},{5... | collective-permute-start | bytes 1769480 | tf_op jit(solution)/shard_map/ppermute | solution.py:42
  129.7 3.7 %collective-permute-start.28 = (bf16[384,768]{1,0:T(8,128)(2,1)S(1)}, bf16[384,768]{1,0:T(8,128)(2,1)}, u32[]{:S(2)}, u32[]{:S(2)}) collective-permute-start(bf16[384,768]{1,0:T(8,128)(2,1)S(1)} %collective-permute-done.23.rest_5_), channel_id=1, source_target_pairs={{0,4},{4,0},{8,12},{12,8},{16,20},{20,16},{24,28},{28,24},{1,5},{5... | collective-permute-start | bytes 1769480 | tf_op jit(solution)/shard_map/ppermute | solution.py:42
  130.1 4.8 %collective-permute-start.29 = (bf16[384,768]{1,0:T(8,128)(2,1)S(1)}, bf16[384,768]{1,0:T(8,128)(2,1)S(1)}, u32[]{:S(2)}, u32[]{:S(2)}) collective-permute-start(bf16[384,768]{1,0:T(8,128)(2,1)S(1)} %collective-permute-done.24.rest_7_), channel_id=1, source_target_pairs={{0,4},{4,0},{8,12},{12,8},{16,20},{20,16},{24,28},{28,24},{1,5},{5... | collective-permute-start | bytes 1769480 | tf_op jit(solution)/shard_map/ppermute | solution.py:42
  130.2 4.7 %collective-permute-start.30 = (bf16[384,768]{1,0:T(8,128)(2,1)S(1)}, bf16[384,768]{1,0:T(8,128)(2,1)S(1)}, u32[]{:S(2)}, u32[]{:S(2)}) collective-permute-start(bf16[384,768]{1,0:T(8,128)(2,1)S(1)} %collective-permute-done.25.rest_9_), channel_id=1, source_target_pairs={{0,4},{4,0},{8,12},{12,8},{16,20},{20,16},{24,28},{28,24},{1,5},{5... | collective-permute-start | bytes 1769480 | tf_op jit(solution)/shard_map/ppermute | solution.py:42
  131.3 34.5 %collective-permute-start.31 = (bf16[384,768]{1,0:T(8,128)(2,1)S(1)}, bf16[384,768]{1,0:T(8,128)(2,1)S(1)}, u32[]{:S(2)}, u32[]{:S(2)}) collective-permute-start(bf16[384,768]{1,0:T(8,128)(2,1)S(1)} %get-tuple-element.213), channel_id=1, source_target_pairs={{0,8},{4,12},{8,0},{12,4},{16,24},{20,28},{24,16},{28,20},{1,9},{5... | collective-permute-start | bytes 1769480 | tf_op jit(solution)/shard_map/ppermute | solution.py:42
  132.6 33.2 %collective-permute-start.32 = (bf16[384,768]{1,0:T(8,128)(2,1)S(1)}, bf16[384,768]{1,0:T(8,128)(2,1)S(1)}, u32[]{:S(2)}, u32[]{:S(2)}) collective-permute-start(bf16[384,768]{1,0:T(8,128)(2,1)S(1)} %get-tuple-element.214), channel_id=1, source_target_pairs={{0,16},{4,20},{8,24},{12,28},{16,0},{20,4},{24,8},{28,12},{1,17},{... | collective-permute-start | bytes 1769480 | tf_op jit(solution)/shard_map/ppermute | solution.py:42
  133.4 32.3 %collective-permute-start.33 = (bf16[384,768]{1,0:T(8,128)(2,1)S(1)}, bf16[384,768]{1,0:T(8,128)(2,1)S(1)}, u32[]{:S(2)}, u32[]{:S(2)}) collective-permute-start(bf16[384,768]{1,0:T(8,128)(2,1)S(1)} %get-tuple-element.215), channel_id=1, source_target_pairs={{0,24},{4,28},{8,16},{12,20},{16,8},{20,12},{24,0},{28,4},{1,25},{... | collective-permute-start | bytes 1769480 | tf_op jit(solution)/shard_map/ppermute | solution.py:42
  136.0 29.9 %copy-start.52 = (f32[8,1,1024]{2,1,0:T(1,128)S(1)}, f32[8,1,1024]{2,1,0:T(1,128)}, u32[]{:S(2)}) copy-start(f32[8,1,1024]{2,1,0:T(1,128)} %copy-done.51) | copy-start | bytes 98308
  165.8 14.9 %collective-permute-start.34 = (bf16[4,480,768]{2,1,0:T(8,128)(2,1)}, bf16[4,480,768]{2,1,0:T(8,128)(2,1)S(1)}, u32[]{:S(2)}, u32[]{:S(2)}) collective-permute-start(bf16[4,480,768]{2,1,0:T(8,128)(2,1)} %get-tuple-element.219), channel_id=1, source_target_pairs={{0,4},{4,0},{8,12},{12,8},{16,20},{20,16},{24,28},{28,24},{1,5},{5... | collective-permute-start | bytes 8847368 | tf_op jit(solution)/shard_map/ppermute | solution.py:42
  180.6 27.0 %copy-start.5 = (bf16[256,1024]{1,0:T(8,128)(2,1)}, bf16[256,1024]{1,0:T(8,128)(2,1)S(1)}, u32[]{:S(2)}) copy-start(bf16[256,1024]{1,0:T(8,128)(2,1)S(1)} %get-tuple-element.252.rest_0_) | copy-start | bytes 1572868
  180.6 27.0 %copy-start.6 = (bf16[256,1024]{1,0:T(8,128)(2,1)}, bf16[256,1024]{1,0:T(8,128)(2,1)S(1)}, u32[]{:S(2)}) copy-start(bf16[256,1024]{1,0:T(8,128)(2,1)S(1)} %get-tuple-element.255.rest_3_) | copy-start | bytes 1572868
  180.6 27.0 %copy-start.7 = (bf16[256,1024]{1,0:T(8,128)(2,1)}, bf16[256,1024]{1,0:T(8,128)(2,1)S(1)}, u32[]{:S(2)}) copy-start(bf16[256,1024]{1,0:T(8,128)(2,1)S(1)} %get-tuple-element.258.rest_6_) | copy-start | bytes 1572868
  181.4 35.4 %collective-permute-start.35 = (bf16[480,768]{1,0:T(8,128)(2,1)S(1)}, bf16[480,768]{1,0:T(8,128)(2,1)S(1)}, u32[]{:S(2)}, u32[]{:S(2)}) collective-permute-start(bf16[480,768]{1,0:T(8,128)(2,1)S(1)} %get-tuple-element.248), channel_id=1, source_target_pairs={{0,8},{4,12},{8,0},{12,4},{16,24},{20,28},{24,16},{28,20},{1,9},{5... | collective-permute-start | bytes 2211848 | tf_op jit(solution)/shard_map/ppermute | solution.py:42
  183.0 34.4 %collective-permute-start.36 = (bf16[480,768]{1,0:T(8,128)(2,1)S(1)}, bf16[480,768]{1,0:T(8,128)(2,1)S(1)}, u32[]{:S(2)}, u32[]{:S(2)}) collective-permute-start(bf16[480,768]{1,0:T(8,128)(2,1)S(1)} %get-tuple-element.249), channel_id=1, source_target_pairs={{0,16},{4,20},{8,24},{12,28},{16,0},{20,4},{24,8},{28,12},{1,17},{... | collective-permute-start | bytes 2211848 | tf_op jit(solution)/shard_map/ppermute | solution.py:42
  183.5 33.9 %collective-permute-start.37 = (bf16[480,768]{1,0:T(8,128)(2,1)S(1)}, bf16[480,768]{1,0:T(8,128)(2,1)S(1)}, u32[]{:S(2)}, u32[]{:S(2)}) collective-permute-start(bf16[480,768]{1,0:T(8,128)(2,1)S(1)} %get-tuple-element.250), channel_id=1, source_target_pairs={{0,24},{4,28},{8,16},{12,20},{16,8},{20,12},{24,0},{28,4},{1,25},{... | collective-permute-start | bytes 2211848 | tf_op jit(solution)/shard_map/ppermute | solution.py:42
  217.4 4.4 %collective-permute-start.38 = (bf16[4,96,2432]{2,1,0:T(8,128)(2,1)S(1)}, bf16[4,96,2432]{2,1,0:T(8,128)(2,1)S(1)}, u32[]{:S(2)}, u32[]{:S(2)}) collective-permute-start(bf16[4,96,2432]{2,1,0:T(8,128)(2,1)S(1)} %get-tuple-element.251), channel_id=1, source_target_pairs={{0,4},{4,0},{8,12},{12,8},{16,20},{20,16},{24,28},{28,24},{1,5},{5... | collective-permute-start | bytes 5603336 | tf_op jit(solution)/shard_map/ppermute | solution.py:42
  218.7 12.2 %collective-permute-start.42 = (bf16[216,768]{1,0:T(8,128)(2,1)S(1)}, bf16[216,768]{1,0:T(8,128)(2,1)S(1)}, u32[]{:S(2)}, u32[]{:S(2)}) collective-permute-start(bf16[216,768]{1,0:T(8,128)(2,1)S(1)} %get-tuple-element.274), channel_id=1, source_target_pairs={{0,1},{1,2},{2,3},{3,0},{4,5},{5,6},{6,7},{7,4},{8,9},{9,10},{10,1... | collective-permute-start | bytes 995336 | tf_op jit(solution)/shard_map/ppermute | solution.py:46
  223.4 23.0 %collective-permute-start.39 = (bf16[96,2432]{1,0:T(8,128)(2,1)}, bf16[96,2432]{1,0:T(8,128)(2,1)}, u32[]{:S(2)}, u32[]{:S(2)}) collective-permute-start(bf16[96,2432]{1,0:T(8,128)(2,1)} %get-tuple-element.262), channel_id=1, source_target_pairs={{0,8},{4,12},{8,0},{12,4},{16,24},{20,28},{24,16},{28,20},{1,9},{5... | collective-permute-start | bytes 1400840 | tf_op jit(solution)/shard_map/ppermute | solution.py:42
  224.4 22.8 %collective-permute-start.40 = (bf16[96,2432]{1,0:T(8,128)(2,1)}, bf16[96,2432]{1,0:T(8,128)(2,1)}, u32[]{:S(2)}, u32[]{:S(2)}) collective-permute-start(bf16[96,2432]{1,0:T(8,128)(2,1)} %get-tuple-element.263), channel_id=1, source_target_pairs={{0,16},{4,20},{8,24},{12,28},{16,0},{20,4},{24,8},{28,12},{1,17},{... | collective-permute-start | bytes 1400840 | tf_op jit(solution)/shard_map/ppermute | solution.py:42
  225.3 21.9 %collective-permute-start.41 = (bf16[96,2432]{1,0:T(8,128)(2,1)}, bf16[96,2432]{1,0:T(8,128)(2,1)}, u32[]{:S(2)}, u32[]{:S(2)}) collective-permute-start(bf16[96,2432]{1,0:T(8,128)(2,1)} %get-tuple-element.264), channel_id=1, source_target_pairs={{0,24},{4,28},{8,16},{12,20},{16,8},{20,12},{24,0},{28,4},{1,25},{... | collective-permute-start | bytes 1400840 | tf_op jit(solution)/shard_map/ppermute | solution.py:42
  226.9 18.8 %collective-permute-start.43 = (bf16[216,768]{1,0:T(8,128)(2,1)S(1)}, bf16[216,768]{1,0:T(8,128)(2,1)S(1)}, u32[]{:S(2)}, u32[]{:S(2)}) collective-permute-start(bf16[216,768]{1,0:T(8,128)(2,1)S(1)} %get-tuple-element.275), channel_id=1, source_target_pairs={{0,2},{1,3},{2,0},{3,1},{4,6},{5,7},{6,4},{7,5},{8,10},{9,11},{10,... | collective-permute-start | bytes 995336 | tf_op jit(solution)/shard_map/ppermute | solution.py:46
  230.8 15.5 %collective-permute-start.44 = (bf16[216,768]{1,0:T(8,128)(2,1)S(1)}, bf16[216,768]{1,0:T(8,128)(2,1)S(1)}, u32[]{:S(2)}, u32[]{:S(2)}) collective-permute-start(bf16[216,768]{1,0:T(8,128)(2,1)S(1)} %get-tuple-element.276), channel_id=1, source_target_pairs={{0,3},{1,0},{2,1},{3,2},{4,7},{5,4},{6,5},{7,6},{8,11},{9,8},{10,9... | collective-permute-start | bytes 995336 | tf_op jit(solution)/shard_map/ppermute | solution.py:46
  249.5 14.3 %collective-permute-start.45 = (bf16[24,2432]{1,0:T(8,128)(2,1)}, bf16[24,2432]{1,0:T(8,128)(2,1)S(1)}, u32[]{:S(2)}, u32[]{:S(2)}) collective-permute-start(bf16[24,2432]{1,0:T(8,128)(2,1)} %get-tuple-element.307), channel_id=1, source_target_pairs={{0,1},{1,2},{2,3},{3,0},{4,5},{5,6},{6,7},{7,4},{8,9},{9,10},{10,1... | collective-permute-start | bytes 350216 | tf_op jit(solution)/shard_map/ppermute | solution.py:46
  254.9 9.7 %collective-permute-start.46 = (bf16[24,2432]{1,0:T(8,128)(2,1)S(1)}, bf16[24,2432]{1,0:T(8,128)(2,1)S(1)}, u32[]{:S(2)}, u32[]{:S(2)}) collective-permute-start(bf16[24,2432]{1,0:T(8,128)(2,1)S(1)} %get-tuple-element.309), channel_id=1, source_target_pairs={{0,2},{1,3},{2,0},{3,1},{4,6},{5,7},{6,4},{7,5},{8,10},{9,11},{10,... | collective-permute-start | bytes 350216 | tf_op jit(solution)/shard_map/ppermute | solution.py:46
  257.1 7.7 %collective-permute-start.47 = (bf16[24,2432]{1,0:T(8,128)(2,1)S(1)}, bf16[24,2432]{1,0:T(8,128)(2,1)}, u32[]{:S(2)}, u32[]{:S(2)}) collective-permute-start(bf16[24,2432]{1,0:T(8,128)(2,1)S(1)} %get-tuple-element.308), channel_id=1, source_target_pairs={{0,3},{1,0},{2,1},{3,2},{4,7},{5,4},{6,5},{7,6},{8,11},{9,8},{10,9... | collective-permute-start | bytes 350216 | tf_op jit(solution)/shard_map/ppermute | solution.py:46
  (46 other events, 448.8 us)
